TPU v7x, 32 devices: a whole 2x2x4 slice. The times are simulated.
32 devices in a mesh: slab: 4 (over y, x), chan: 8 (over z, core).
Axes of the slice: x: 2, y: 2, z: 4, core: 2. Of those that a mesh axis runs over, the one named last changes fastest.
Arguments:
- volume: bfloat16 [8, 16, 64, 256], P('slab', 'chan'), may hold values from -6 to 6
- weights: bfloat16 [6912, 256], P(None, 'slab'), may hold values from -0.078125 to 0.078125
Outputs:
- conv_out: bfloat16 [8, 16, 64, 256], P('slab', 'chan')
All inputs are finite; a program needn't handle non-finite values.
Results may differ from a plain program's by a relative error of at most 0.001.
Values may be sent and summed in bfloat16 or wider, within the bound.
No kernel may reach another device: no remote copies, remote signals or barrier semaphores. Data moves between devices by JAX's collectives and lax.ppermute only.
A program may use at most 64 MiB of HBM per device.

v0:
```python
import jax
import jax.numpy as jnp
from jax import lax
from jax.sharding import PartitionSpec as P


def extended_2(block, sides, width):
    for axis, dim in sides:
        count = lax.axis_size(axis)
        forward = [(i, i + 1) for i in range(count - 1)]
        backward = [(target, source) for source, target in forward]
        low = lax.ppermute(
            lax.slice_in_dim(block, block.shape[dim] - width, None, axis=dim), axis, forward
        )
        high = lax.ppermute(lax.slice_in_dim(block, 0, width, axis=dim), axis, backward)
        block = jnp.concatenate([low, block, high], axis=dim)
    return block


def local(volume, weights):
    depth_cells, row_cells, col_cells, channels = volume.shape
    voxels = depth_cells * row_cells * col_cells
    extended = extended_2(volume, (("slab", 0), ("chan", 1)), 1)
    padded = jnp.pad(extended, ((0, 0), (0, 0), (1, 1), (0, 0)))
    gathered = lax.all_gather(weights, "slab", axis=1, tiled=True)
    out_width = gathered.shape[1]
    summed = jnp.zeros((voxels, out_width), jnp.float32)
    for depth_off in range(3):
        pieces = []
        for row_off in range(3):
            for col_off in range(3):
                shifted = padded[
                    depth_off : depth_off + depth_cells,
                    row_off : row_off + row_cells,
                    col_off : col_off + col_cells,
                    :,
                ]
                pieces.append(shifted.reshape(voxels, channels))
        columns = jnp.concatenate(pieces, axis=1)
        kernel_rows = gathered[9 * depth_off * channels : (9 * depth_off + 9) * channels, :]
        summed = summed + jnp.dot(columns, kernel_rows, preferred_element_type=jnp.float32)
    return summed.astype(jnp.bfloat16).reshape(depth_cells, row_cells, col_cells, channels)


def solution(mesh):
    placed = (P("slab", "chan", None, None), P(None, "slab"))
    return jax.shard_map(
        local, mesh=mesh, in_specs=placed, out_specs=P("slab", "chan", None, None), check_vma=False
    )
```

profile of v0, /device:TPU:0, one launch (start us, length us, event | category | flops | bytes accessed | tf_op | source)
XLA Modules:
  0.0 72.4 jit_solution(17654274896068505251)
XLA Ops:
  6.5 0.0 copy-start
  6.5 0.0 all-gather.2.cloned.1.call-start
  6.5 0.7 all-gather.2.cloned.1.call-update
  7.3 0.9 %fusion.27 = (bf16[1,2,64,256]{3,2,1,0:T(8,128)(2,1)S(1)}, bf16[1,2,64,256]{3,2,1,0:T(8,128)(2,1)S(1)}) fusion(bf16[2,2,64,256]{3,2,1,0:T(8,128)(2,1)} %param.2), kind=kLoop, calls=%fused_computation.65 | loop fusion | bytes 262144 | tf_op jit(solution)/shard_map/slice | solution.py:15
  8.1 4.8 %collective-permute-start = (bf16[1,2,64,256]{3,2,1,0:T(8,128)(2,1)S(1)}, bf16[1,2,64,256]{3,2,1,0:T(8,128)(2,1)S(1)}, u32[]{:S(2)}, u32[]{:S(2)}) collective-permute-start(bf16[1,2,64,256]{3,2,1,0:T(8,128)(2,1)S(1)} %get-tuple-element.38), channel_id=1, source_target_pairs={{0,8},{8,16},{16,24},{1,9},{9,17},{17,25},{2,10},{10,18},{18,26},{... | collective-permute-start | bytes 196616 | tf_op jit(solution)/shard_map/ppermute | solution.py:12
  13.0 1.3 %collective-permute-start.1 = (bf16[1,2,64,256]{3,2,1,0:T(8,128)(2,1)S(1)}, bf16[1,2,64,256]{3,2,1,0:T(8,128)(2,1)S(1)}, u32[]{:S(2)}, u32[]{:S(2)}) collective-permute-start(bf16[1,2,64,256]{3,2,1,0:T(8,128)(2,1)S(1)} %get-tuple-element.37), channel_id=1, source_target_pairs={{8,0},{16,8},{24,16},{9,1},{17,9},{25,17},{10,2},{18,10},{26,18},{... | collective-permute-start | bytes 196616 | tf_op jit(solution)/shard_map/ppermute | solution.py:15
  14.3 0.6 collective-permute-done
  14.9 4.3 %collective-permute-done.1 = bf16[1,2,64,256]{3,2,1,0:T(8,128)(2,1)S(1)} collective-permute-done((bf16[1,2,64,256]{3,2,1,0:T(8,128)(2,1)S(1)}, bf16[1,2,64,256]{3,2,1,0:T(8,128)(2,1)S(1)}, u32[]{:S(2)}, u32[]{:S(2)}) %collective-permute-start.1) | collective-permute-done | bytes 65568 | tf_op jit(solution)/shard_map/ppermute | solution.py:15
  19.2 0.0 copy-done
  19.2 1.3 %collective-permute-start.3 = (bf16[4,1,64,256]{3,2,1,0:T(8,128)(2,1)S(1)}, bf16[4,1,64,256]{3,2,1,0:T(8,128)(2,1)S(1)}, u32[]{:S(2)}, u32[]{:S(2)}) collective-permute-start(bf16[4,1,64,256]{3,2,1,0:T(8,128)(2,1)S(1)} %get-tuple-element.33), channel_id=1, source_target_pairs={{1,0},{2,1},{3,2},{4,3},{5,4},{6,5},{7,6},{9,8},{10,9},{11,10},{12... | collective-permute-start | bytes 393224 | tf_op jit(solution)/shard_map/ppermute | solution.py:15
  20.5 3.0 %collective-permute-start.2 = (bf16[4,1,64,256]{3,2,1,0:T(8,128)(2,1)S(1)}, bf16[4,1,64,256]{3,2,1,0:T(8,128)(2,1)S(1)}, u32[]{:S(2)}, u32[]{:S(2)}) collective-permute-start(bf16[4,1,64,256]{3,2,1,0:T(8,128)(2,1)S(1)} %get-tuple-element.32), channel_id=1, source_target_pairs={{0,1},{1,2},{2,3},{3,4},{4,5},{5,6},{6,7},{8,9},{9,10},{10,11},{11... | collective-permute-start | bytes 393224 | tf_op jit(solution)/shard_map/ppermute | solution.py:12
  23.6 0.0 collective-permute-done.3
  23.6 1.0 %collective-permute-done.2 = bf16[4,1,64,256]{3,2,1,0:T(8,128)(2,1)S(1)} collective-permute-done((bf16[4,1,64,256]{3,2,1,0:T(8,128)(2,1)S(1)}, bf16[4,1,64,256]{3,2,1,0:T(8,128)(2,1)S(1)}, u32[]{:S(2)}, u32[]{:S(2)}) %collective-permute-start.2) | collective-permute-done | bytes 131104 | tf_op jit(solution)/shard_map/ppermute | solution.py:12
  24.5 0.2 fusion.20
  24.8 0.3 fusion.25
  25.1 0.1 fusion.22
  25.4 0.0 copy-start.1
  25.6 0.8 %copy-done.1 = bf16[256,2304]{1,0:T(8,128)(2,1)} copy-done((bf16[256,2304]{1,0:T(8,128)(2,1)}, bf16[256,2304]{1,0:T(8,128)(2,1)S(1)}, u32[]{:S(2)}) %copy-start.1) | copy-done | bytes 1179672
  26.5 32.7 %all-gather.2.cloned.1.call-done = bf16[6912,256]{0,1:T(8,128)(2,1)} async-done(((bf16[6912,64]{0,1:T(8,128)(2,1)}), bf16[6912,256]{0,1:T(8,128)(2,1)}) %all-gather.2.cloned.1.call-update) | async-done | bytes 3538960 | tf_op jit(solution)/shard_map/all_gather | solution.py:25
  59.2 2.1 %fusion = f32[256,256]{1,0:T(8,128)S(1)} fusion(bf16[256,2304]{1,0:T(8,128)(2,1)} %copy-done.1, bf16[6912,256]{0,1:T(8,128)(2,1)} %all-gather.2.cloned.1.call-done), kind=kOutput, calls=%fused_computation.2 | convolution fusion | flops 301989888 | bytes 2621440 | tf_op jit(solution)/shard_map/dot_general | solution.py:41
  61.3 1.8 %fusion.2 = f32[256,256]{1,0:T(8,128)S(1)} fusion(bf16[256,2304]{1,0:T(8,128)(2,1)S(1)} %constant_dynamic-update-slice_fusion.12, bf16[6912,256]{0,1:T(8,128)(2,1)} %all-gather.2.cloned.1.call-done), kind=kOutput, calls=%fused_computation.4 | convolution fusion | flops 301989888 | bytes 2621440 | tf_op jit(solution)/shard_map/dot_general | solution.py:41
  63.1 2.4 %fusion.13 = bf16[256,256]{1,0:T(8,128)(2,1)} fusion(f32[256,256]{1,0:T(8,128)S(1)} %fusion, f32[256,256]{1,0:T(8,128)S(1)} %fusion.2, bf16[256,2304]{1,0:T(8,128)(2,1)S(1)} %constant_dynamic-update-slice_fusion.3, bf16[6912,256]{0,1:T(8,128)(2,1)} %all-gather.2.cloned.1.call-done), kind=kOutput, calls=%fused_computation.11 | convolution fusion | flops 302186496 | bytes 3014656 | tf_op jit(solution)/shard_map/dot_general | solution.py:41
  (31 shorter events, 0.4 us)
Async XLA Ops:
  6.5 12.6 %copy-start = (bf16[2,2,64,256]{3,2,1,0:T(8,128)(2,1)S(1)}, bf16[2,2,64,256]{3,2,1,0:T(8,128)(2,1)}, u32[]{:S(2)}) copy-start(bf16[2,2,64,256]{3,2,1,0:T(8,128)(2,1)} %param.2) | copy-start | bytes 393220
  6.5 52.7 %all-gather.2.cloned.1.call-start = ((), (), s32[]{:S(2)}) async-start(), calls=%async_computation | async-start | bytes 4423680 | tf_op jit(solution)/shard_map/all_gather | solution.py:25
  8.1 6.7 %collective-permute-start = (bf16[1,2,64,256]{3,2,1,0:T(8,128)(2,1)S(1)}, bf16[1,2,64,256]{3,2,1,0:T(8,128)(2,1)S(1)}, u32[]{:S(2)}, u32[]{:S(2)}) collective-permute-start(bf16[1,2,64,256]{3,2,1,0:T(8,128)(2,1)S(1)} %get-tuple-element.38), channel_id=1, source_target_pairs={{0,8},{8,16},{16,24},{1,9},{9,17},{17,25},{2,10},{10,18},{18,26},{... | collective-permute-start | bytes 196616 | tf_op jit(solution)/shard_map/ppermute | solution.py:12
  13.0 6.2 %collective-permute-start.1 = (bf16[1,2,64,256]{3,2,1,0:T(8,128)(2,1)S(1)}, bf16[1,2,64,256]{3,2,1,0:T(8,128)(2,1)S(1)}, u32[]{:S(2)}, u32[]{:S(2)}) collective-permute-start(bf16[1,2,64,256]{3,2,1,0:T(8,128)(2,1)S(1)} %get-tuple-element.37), channel_id=1, source_target_pairs={{8,0},{16,8},{24,16},{9,1},{17,9},{25,17},{10,2},{18,10},{26,18},{... | collective-permute-start | bytes 196616 | tf_op jit(solution)/shard_map/ppermute | solution.py:15
  19.2 4.3 %collective-permute-start.3 = (bf16[4,1,64,256]{3,2,1,0:T(8,128)(2,1)S(1)}, bf16[4,1,64,256]{3,2,1,0:T(8,128)(2,1)S(1)}, u32[]{:S(2)}, u32[]{:S(2)}) collective-permute-start(bf16[4,1,64,256]{3,2,1,0:T(8,128)(2,1)S(1)} %get-tuple-element.33), channel_id=1, source_target_pairs={{1,0},{2,1},{3,2},{4,3},{5,4},{6,5},{7,6},{9,8},{10,9},{11,10},{12... | collective-permute-start | bytes 393224 | tf_op jit(solution)/shard_map/ppermute | solution.py:15
  20.5 4.0 %collective-permute-start.2 = (bf16[4,1,64,256]{3,2,1,0:T(8,128)(2,1)S(1)}, bf16[4,1,64,256]{3,2,1,0:T(8,128)(2,1)S(1)}, u32[]{:S(2)}, u32[]{:S(2)}) collective-permute-start(bf16[4,1,64,256]{3,2,1,0:T(8,128)(2,1)S(1)} %get-tuple-element.32), channel_id=1, source_target_pairs={{0,1},{1,2},{2,3},{3,4},{4,5},{5,6},{6,7},{8,9},{9,10},{10,11},{11... | collective-permute-start | bytes 393224 | tf_op jit(solution)/shard_map/ppermute | solution.py:12
  25.4 1.0 %copy-start.1 = (bf16[256,2304]{1,0:T(8,128)(2,1)}, bf16[256,2304]{1,0:T(8,128)(2,1)S(1)}, u32[]{:S(2)}) copy-start(bf16[256,2304]{1,0:T(8,128)(2,1)S(1)} %constant_dynamic-update-slice_fusion.21) | copy-start | bytes 3538948
Sparse Core Ops, SparseCore 0:
  9.2 49.9 all-gather.1
where the time goes:
time: 72.7 us; the launch traced here: 72.4 us
  waiting for transfers between devices  39.2 us (54%)
  between operations  13.7 us (19%)
  starting transfers between devices  10.5 us (14%)
  matrix products  6.33 us (9%)
  local copies, waits for them, and re-layouts  2.38 us (3%)
    all_gather x1, waiting for transfers between devices, local(): gathered = lax.all_gather(weights, 'slab', axis=1, tiled=True)  32.7 us
    ppermute x2, starting transfers between devices, extended_2(): lax.ppermute(lax.slice_in_dim(block, block.shape[dim] - width, None, axis...  7.88 us
    dot_general x3, matrix products, local(): jnp.dot(columns, kernel_rows, preferred_element_type=jnp.float32)  6.33 us
    ppermute x2, waiting for transfers between devices, extended_2(): lax.ppermute(lax.slice_in_dim(block, 0, width, axis=dim), axis, backward)  4.27 us
    ppermute x2, starting transfers between devices, extended_2(): lax.ppermute(lax.slice_in_dim(block, 0, width, axis=dim), axis, backward)  2.58 us
    ppermute x2, waiting for transfers between devices, extended_2(): lax.ppermute(lax.slice_in_dim(block, block.shape[dim] - width, None, axis...  1.54 us
  transfers between devices with their start and end apart: 5, of which 4 were waited for; matrix products, arithmetic and copies ran while one was open for 3% of the time, Pallas kernels for 0%

commit v1 on v0

v1 whole, which is shorter than its diff:
```python
import functools

import jax
import jax.numpy as jnp
from jax import lax
from jax.experimental import pallas as pl
from jax.experimental.pallas import tpu as pltpu
from jax.sharding import PartitionSpec as P

TAPS = 27
BOTH = ("slab", "chan")
VMEM_LIMIT = 24 * 1024 * 1024


def whole_vmem(count):
    return [pl.BlockSpec(memory_space=pltpu.VMEM)] * count


def columns_kernel(volume, low, high, row_low, row_high, columns):
    depth, rows, cols, channels = volume.shape
    position = lax.broadcasted_iota(jnp.int32, (cols, channels), 0)
    for d in range(depth + 2):
        for r in range(rows + 2):
            if r == 0:
                line = row_low[d, 0]
            elif r == rows + 1:
                line = row_high[d, 0]
            elif d == 0:
                line = low[0, r - 1]
            elif d == depth + 1:
                line = high[0, r - 1]
            else:
                line = volume[d - 1, r - 1]
            wide = line.astype(jnp.float32)
            before = jnp.where(position == 0, 0.0, pltpu.roll(wide, 1, 0))
            after = jnp.where(position == cols - 1, 0.0, pltpu.roll(wide, cols - 1, 0))
            shifted = (before.astype(line.dtype), line, after.astype(line.dtype))
            for a in range(3):
                for b in range(3):
                    if 0 <= d - a < depth and 0 <= r - b < rows:
                        start = ((d - a) * rows + (r - b)) * cols
                        for e in range(3):
                            tap = 9 * a + 3 * b + e
                            columns[start : start + cols, tap * channels : (tap + 1) * channels] = shifted[e]


def build_columns(volume, low, high, row_low, row_high):
    depth, rows, cols, channels = volume.shape
    return pl.pallas_call(
        columns_kernel,
        out_shape=jax.ShapeDtypeStruct((depth * rows * cols, TAPS * channels), volume.dtype),
        in_specs=whole_vmem(5),
        out_specs=pl.BlockSpec(memory_space=pltpu.VMEM),
        compiler_params=pltpu.CompilerParams(vmem_limit_bytes=VMEM_LIMIT),
        name="columns",
    )(volume, low, high, row_low, row_high)


def product(columns, kernel_rows):
    return lax.dot_general(
        columns, kernel_rows, (((1,), (1,)), ((), ())), preferred_element_type=jnp.float32
    )


def part_kernel(columns, *refs):
    *pieces, out = refs
    kernel_rows = jnp.concatenate([piece[...] for piece in pieces], axis=0)
    out[...] = product(columns[...], kernel_rows).astype(out.dtype)


def part(columns, *pieces):
    voxels, depth = columns.shape
    width = sum(piece.shape[0] for piece in pieces)
    return pl.pallas_call(
        part_kernel,
        out_shape=jax.ShapeDtypeStruct((voxels, width), columns.dtype),
        in_specs=whole_vmem(1 + len(pieces)),
        out_specs=pl.BlockSpec(memory_space=pltpu.VMEM),
        compiler_params=pltpu.CompilerParams(vmem_limit_bytes=VMEM_LIMIT),
        cost_estimate=pl.CostEstimate(
            flops=2 * voxels * depth * width, bytes_accessed=2 * depth * (voxels + width), transcendentals=0
        ),
        name="part",
    )(columns, *pieces)


def last_kernel(columns, first, second, here, there, out):
    slab = lax.axis_index("slab")
    core = lax.rem(lax.axis_index("chan"), 2)
    kernel_rows = jnp.concatenate([here[...], there[...]], axis=0)
    third = product(columns[...], kernel_rows)
    half = here.shape[0]
    first_sum = first[...].astype(jnp.float32)
    second_sum = second[...].astype(jnp.float32)
    own = first_sum[:, : 2 * half]
    r1, o1 = first_sum[:, 2 * half : 3 * half], first_sum[:, 3 * half :]
    r2, o2 = second_sum[:, :half], second_sum[:, half:]
    d, other_d = third[:, :half], third[:, half:]
    even = core == 0
    across_x = jnp.concatenate([jnp.where(even, r1, o1), jnp.where(even, r2, o2)], axis=1)
    across_y = jnp.concatenate([jnp.where(even, o2, r2), jnp.where(even, o1, r1)], axis=1)
    opposite = jnp.concatenate([jnp.where(even, d, other_d), jnp.where(even, other_d, d)], axis=1)
    blocks = [own, across_x, across_y, opposite]
    odd_x = lax.rem(slab, 2) == 1
    blocks = [jnp.where(odd_x, blocks[j ^ 1], blocks[j]) for j in range(4)]
    odd_y = slab >= 2
    blocks = [jnp.where(odd_y, blocks[j ^ 2], blocks[j]) for j in range(4)]
    out[...] = jnp.concatenate(blocks, axis=1).astype(out.dtype)


def last(columns, first, second, here, there):
    voxels, depth = columns.shape
    width = first.shape[1] + second.shape[1] + here.shape[0] + there.shape[0]
    return pl.pallas_call(
        last_kernel,
        out_shape=jax.ShapeDtypeStruct((voxels, width), columns.dtype),
        in_specs=whole_vmem(5),
        out_specs=pl.BlockSpec(memory_space=pltpu.VMEM),
        compiler_params=pltpu.CompilerParams(vmem_limit_bytes=VMEM_LIMIT),
        cost_estimate=pl.CostEstimate(
            flops=2 * voxels * depth * 2 * here.shape[0],
            bytes_accessed=2 * depth * (voxels + 2 * here.shape[0]),
            transcendentals=0,
        ),
        name="last",
    )(columns, first, second, here, there)


def halo(block, axis, dim):
    count = lax.axis_size(axis)
    forward = [(i, i + 1) for i in range(count - 1)]
    backward = [(target, source) for source, target in forward]
    extent = block.shape[dim]
    low = lax.ppermute(lax.slice_in_dim(block, extent - 1, extent, axis=dim), axis, forward)
    high = lax.ppermute(lax.slice_in_dim(block, 0, 1, axis=dim), axis, backward)
    return low, high


def four_slabs(columns_of, weights):
    chans = lax.axis_size("chan")

    def pairs(even_step, odd_step, core_step=0):
        return [
            (s * chans + c, (s ^ (odd_step if c % 2 else even_step)) * chans + (c ^ core_step))
            for s in range(4)
            for c in range(chans)
        ]

    kernel_rows = weights.T
    half = kernel_rows.shape[0] // 2
    core = lax.rem(lax.axis_index("chan"), 2)
    mine = lax.dynamic_slice_in_dim(kernel_rows, core * half, half, 0)
    rest = lax.dynamic_slice_in_dim(kernel_rows, (1 - core) * half, half, 0)
    r1 = lax.ppermute(mine, BOTH, pairs(1, 2))
    r2 = lax.ppermute(rest, BOTH, pairs(1, 2))
    columns = columns_of()
    d = lax.ppermute(r1, BOTH, pairs(2, 1))
    swap = pairs(0, 0, 1)
    o1 = lax.ppermute(r1, BOTH, swap)
    o2 = lax.ppermute(r2, BOTH, swap)
    other_d = lax.ppermute(d, BOTH, swap)
    first = part(columns, kernel_rows, r1, o1)
    second = part(columns, r2, o2)
    return last(columns, first, second, d, other_d)


def local(volume, weights):
    def columns_of():
        low, high = halo(volume, "slab", 0)
        tall = jnp.concatenate([low, volume, high], axis=0)
        row_low, row_high = halo(tall, "chan", 1)
        return build_columns(volume, low, high, row_low, row_high)

    if lax.axis_size("slab") == 4 and lax.axis_size("chan") % 2 == 0:
        out = four_slabs(columns_of, weights)
    else:
        gathered = lax.all_gather(weights.T, "slab", axis=0, tiled=True)
        out = part(columns_of(), gathered)
    return out.reshape(volume.shape)


def solution(mesh):
    placed = (P("slab", "chan", None, None), P(None, "slab"))
    return jax.shard_map(
        local, mesh=mesh, in_specs=placed, out_specs=P("slab", "chan", None, None), check_vma=False
    )
```

time: 72.7 us -> 38.4 us (0.53)
  the two profiles are of different devices: /device:TPU:0 before, /device:TPU:1 now
where the time goes in v1:
time: 38.4 us; the launch traced here: 38.1 us
  waiting for transfers between devices  16 us (42%)
  starting transfers between devices  13.9 us (36%)
  Pallas kernels  4.23 us (11%)
  local copies, waits for them, and re-layouts  3.94 us (10%)
    ppermute x2, starting transfers between devices, halo(): lax.ppermute(lax.slice_in_dim(block, extent - 1, extent, axis=dim), axis,...  6.22 us
    ppermute x1, waiting for transfers between devices, four_slabs(): r1 = lax.ppermute(mine, BOTH, pairs(1, 2))  5.91 us
    ppermute x2, waiting for transfers between devices, halo(): lax.ppermute(lax.slice_in_dim(block, extent - 1, extent, axis=dim), axis,...  5.69 us
    ppermute x2, waiting for transfers between devices, halo(): high = lax.ppermute(lax.slice_in_dim(block, 0, 1, axis=dim), axis, backward)  4.35 us
    ppermute x2, starting transfers between devices, halo(): high = lax.ppermute(lax.slice_in_dim(block, 0, 1, axis=dim), axis, backward)  3.34 us
    ppermute x1, starting transfers between devices, four_slabs(): r1 = lax.ppermute(mine, BOTH, pairs(1, 2))  2.13 us
    pallas_call x2, Pallas kernels, part(): pl.pallas_call(part_kernel, out_shape=jax.ShapeDtypeStruct((voxels, width...  2.12 us
    pallas_call x1, Pallas kernels, last(): pl.pallas_call(last_kernel, out_shape=jax.ShapeDtypeStruct((voxels, width...  1.86 us
  transfers between devices with their start and end apart: 10, of which 3 were waited for; matrix products, arithmetic and copies ran while one was open for 5% of the time, Pallas kernels for 6%

profile of v1, /device:TPU:1, one launch (start us, length us, event | category | flops | bytes accessed | tf_op | source)
XLA Modules:
  0.0 38.1 jit_solution(754814702402617866)
XLA Ops:
  0.0 1.2 %dynamic-slice_bitcast_fusion = (bf16[32,6912]{1,0:T(8,128)(2,1)S(1)}, bf16[32,6912]{1,0:T(8,128)(2,1)S(1)}) fusion(bf16[6912,64]{0,1:T(8,128)(2,1)} %param.3, s32[]{:T(128)S(6)} %select_n.7, s32[]{:T(128)S(6)} %select_n.6), kind=kLoop, calls=%fused_computation | loop fusion | bytes 1769480 | tf_op jit(solution)/shard_map/dynamic_slice | solution.py:153
  1.2 2.1 %collective-permute-start.4 = (bf16[32,6912]{1,0:T(8,128)(2,1)S(1)}, bf16[32,6912]{1,0:T(8,128)(2,1)S(1)}, u32[]{:S(2)}, u32[]{:S(2)}) collective-permute-start(bf16[32,6912]{1,0:T(8,128)(2,1)S(1)} %get-tuple-element.6), channel_id=1, source_target_pairs={{0,8},{1,17},{2,10},{3,19},{4,12},{5,21},{6,14},{7,23},{8,0},{9,25... | collective-permute-start | bytes 1327112 | tf_op jit(solution)/shard_map/ppermute | solution.py:154
  3.3 0.1 collective-permute-start.6
  3.4 5.9 %collective-permute-done.4.refs_1_ = bf16[32,6912]{1,0:T(8,128)(2,1)S(1)} collective-permute-done((bf16[32,6912]{1,0:T(8,128)(2,1)S(1)}, bf16[32,6912]{1,0:T(8,128)(2,1)S(1)}, u32[]{:S(2)}, u32[]{:S(2)}) %collective-permute-start.4) | collective-permute-done | bytes 442400 | tf_op jit(solution)/shard_map/ppermute | solution.py:154
  9.3 1.4 %collective-permute-start.8 = (bf16[32,6912]{1,0:T(8,128)(2,1)S(1)}, bf16[32,6912]{1,0:T(8,128)(2,1)S(1)}, u32[]{:S(2)}, u32[]{:S(2)}) collective-permute-start(bf16[32,6912]{1,0:T(8,128)(2,1)S(1)} %collective-permute-done.4.refs_1_), channel_id=1, source_target_pairs={{0,16},{1,9},{2,18},{3,11},{4,20},{5,13},{6,22},{7,15},{8,24},{9,1... | collective-permute-start | bytes 1327112 | tf_op jit(solution)/shard_map/ppermute | solution.py:157
  10.8 0.9 %fusion.1 = (bf16[1,2,64,256]{3,2,1,0:T(8,128)(2,1)S(1)}, bf16[1,2,64,256]{3,2,1,0:T(8,128)(2,1)S(1)}) fusion(bf16[2,2,64,256]{3,2,1,0:T(8,128)(2,1)} %volume.1), kind=kLoop, calls=%fused_computation.6 | loop fusion | bytes 262144 | tf_op jit(solution)/shard_map/slice | solution.py:135
  11.6 1.9 %collective-permute-start = (bf16[1,2,64,256]{3,2,1,0:T(8,128)(2,1)S(1)}, bf16[1,2,64,256]{3,2,1,0:T(8,128)(2,1)S(1)}, u32[]{:S(2)}, u32[]{:S(2)}) collective-permute-start(bf16[1,2,64,256]{3,2,1,0:T(8,128)(2,1)S(1)} %get-tuple-element.10), channel_id=1, source_target_pairs={{0,8},{8,16},{16,24},{1,9},{9,17},{17,25},{2,10},{10,18},{18,26},{... | collective-permute-start | bytes 196616 | tf_op jit(solution)/shard_map/ppermute | solution.py:134
  13.6 1.3 %collective-permute-start.1 = (bf16[1,2,64,256]{3,2,1,0:T(8,128)(2,1)S(1)}, bf16[1,2,64,256]{3,2,1,0:T(8,128)(2,1)S(1)}, u32[]{:S(2)}, u32[]{:S(2)}) collective-permute-start(bf16[1,2,64,256]{3,2,1,0:T(8,128)(2,1)S(1)} %get-tuple-element.9), channel_id=1, source_target_pairs={{8,0},{16,8},{24,16},{9,1},{17,9},{25,17},{10,2},{18,10},{26,18},{... | collective-permute-start | bytes 196616 | tf_op jit(solution)/shard_map/ppermute | solution.py:135
  14.9 5.7 %collective-permute-done.low = bf16[1,2,64,256]{3,2,1,0:T(8,128)(2,1)S(1)} collective-permute-done((bf16[1,2,64,256]{3,2,1,0:T(8,128)(2,1)S(1)}, bf16[1,2,64,256]{3,2,1,0:T(8,128)(2,1)S(1)}, u32[]{:S(2)}, u32[]{:S(2)}) %collective-permute-start) | collective-permute-done | bytes 65568 | tf_op jit(solution)/shard_map/ppermute | solution.py:134
  20.6 0.9 %constant_dynamic-update-slice_fusion.1 = bf16[4,2,64,256]{3,2,1,0:T(8,128)(2,1)S(1)} fusion(bf16[4,2,64,256]{3,2,1,0:T(8,128)(2,1)S(1)} %constant_dynamic-update-slice_fusion.2, bf16[2,2,64,256]{3,2,1,0:T(8,128)(2,1)} %volume.1), kind=kLoop, calls=%fused_computation.3 | loop fusion | bytes 262144
  21.5 0.1 collective-permute-start.5
  21.6 0.0 collective-permute-done.6.refs_0_
  21.6 0.5 %collective-permute-start.7 = (bf16[32,6912]{1,0:T(8,128)(2,1)S(1)}, bf16[32,6912]{1,0:T(8,128)(2,1)S(1)}, u32[]{:S(2)}, u32[]{:S(2)}) collective-permute-start(bf16[32,6912]{1,0:T(8,128)(2,1)S(1)} %collective-permute-done.6.refs_0_), channel_id=1, source_target_pairs={{0,1},{1,0},{2,3},{3,2},{4,5},{5,4},{6,7},{7,6},{8,9},{9,8},{10,11... | collective-permute-start | bytes 1327112 | tf_op jit(solution)/shard_map/ppermute | solution.py:160
  22.1 0.0 collective-permute-done.8.here
  22.1 0.1 collective-permute-start.9
  22.2 0.0 collective-permute-done.1.high
  22.2 4.3 %collective-permute-start.2 = (bf16[4,1,64,256]{3,2,1,0:T(8,128)(2,1)S(1)}, bf16[4,1,64,256]{3,2,1,0:T(8,128)(2,1)S(1)}, u32[]{:S(2)}, u32[]{:S(2)}) collective-permute-start(bf16[4,1,64,256]{3,2,1,0:T(8,128)(2,1)S(1)} %get-tuple-element.8), channel_id=1, source_target_pairs={{0,1},{1,2},{2,3},{3,4},{4,5},{5,6},{6,7},{8,9},{9,10},{10,11},{11... | collective-permute-start | bytes 393224 | tf_op jit(solution)/shard_map/ppermute | solution.py:134
  26.5 0.0 copy-start
  26.5 2.1 %collective-permute-start.3 = (bf16[4,1,64,256]{3,2,1,0:T(8,128)(2,1)S(1)}, bf16[4,1,64,256]{3,2,1,0:T(8,128)(2,1)S(1)}, u32[]{:S(2)}, u32[]{:S(2)}) collective-permute-start(bf16[4,1,64,256]{3,2,1,0:T(8,128)(2,1)S(1)} %get-tuple-element.7), channel_id=1, source_target_pairs={{1,0},{2,1},{3,2},{4,3},{5,4},{6,5},{7,6},{9,8},{10,9},{11,10},{12... | collective-permute-start | bytes 393224 | tf_op jit(solution)/shard_map/ppermute | solution.py:135
  28.6 0.0 collective-permute-done.2.row_low
  28.6 4.3 %collective-permute-done.3.row_high = bf16[4,1,64,256]{3,2,1,0:T(8,128)(2,1)S(1)} collective-permute-done((bf16[4,1,64,256]{3,2,1,0:T(8,128)(2,1)S(1)}, bf16[4,1,64,256]{3,2,1,0:T(8,128)(2,1)S(1)}, u32[]{:S(2)}, u32[]{:S(2)}) %collective-permute-start.3) | collective-permute-done | bytes 131104 | tf_op jit(solution)/shard_map/ppermute | solution.py:135
  32.9 0.0 copy-start.1
  32.9 0.9 %copy-done.1 = bf16[2,2,64,256]{3,2,1,0:T(8,128)(2,1)S(1)} copy-done((bf16[2,2,64,256]{3,2,1,0:T(8,128)(2,1)S(1)}, bf16[2,2,64,256]{3,2,1,0:T(8,128)(2,1)}, u32[]{:S(2)}) %copy-start.1) | copy-done | bytes 131096
  33.8 0.3 columns.1
  34.1 0.0 collective-permute-done.7.refs_1_
  34.1 1.1 %part.3.second = bf16[256,64]{1,0:T(8,128)(2,1)S(1)} custom-call(bf16[256,6912]{1,0:T(8,128)(2,1)S(1)} %columns.1, bf16[32,6912]{1,0:T(8,128)(2,1)S(1)} %collective-permute-done.6.refs_0_, bf16[32,6912]{1,0:T(8,128)(2,1)S(1)} %collective-permute-done.7.refs_1_), custom_call_target="tpu_custom_call" | custom-call | flops 226492416 | bytes 4423680 | tf_op jit(solution)/shard_map/part/pallas_call | solution.py:74
  35.2 0.0 collective-permute-done.5.refs_2_
  35.2 0.0 copy-done
  35.2 1.1 %part.2.first = bf16[256,128]{1,0:T(8,128)(2,1)S(1)} custom-call(bf16[256,6912]{1,0:T(8,128)(2,1)S(1)} %columns.1, bf16[64,6912]{1,0:T(8,128)(2,1)S(1)} %bitcast.6, bf16[32,6912]{1,0:T(8,128)(2,1)S(1)} %collective-permute-done.4.refs_1_, bf16[32,6912]{1,0:T(8,128)(2,1)S(1)} %collective-permute-done.5.refs_2_), custom_call_target="tpu_custom_call" | custom-call | flops 452984832 | bytes 5308416 | tf_op jit(solution)/shard_map/part/pallas_call | solution.py:74
  36.3 0.0 collective-permute-done.9.there
  36.3 1.9 %last.1 = bf16[256,256]{1,0:T(8,128)(2,1)} custom-call(bf16[256,6912]{1,0:T(8,128)(2,1)S(1)} %columns.1, bf16[256,128]{1,0:T(8,128)(2,1)S(1)} %part.2.first, bf16[256,64]{1,0:T(8,128)(2,1)S(1)} %part.3.second, bf16[32,6912]{1,0:T(8,128)(2,1)S(1)} %collective-permute-done.8.here, bf16[32,6912]{1,0:T(8,128)(2,1)S(1)} %collective-permute-done.9.there), custom_call_target="tpu_custom_call" | custom-call | flops 226492416 | bytes 4423680 | tf_op jit(solution)/shard_map/last/pallas_call | solution.py:114
  (3 shorter events, 0.0 us)
Async XLA Ops:
  1.2 8.1 %collective-permute-start.4 = (bf16[32,6912]{1,0:T(8,128)(2,1)S(1)}, bf16[32,6912]{1,0:T(8,128)(2,1)S(1)}, u32[]{:S(2)}, u32[]{:S(2)}) collective-permute-start(bf16[32,6912]{1,0:T(8,128)(2,1)S(1)} %get-tuple-element.6), channel_id=1, source_target_pairs={{0,8},{1,17},{2,10},{3,19},{4,12},{5,21},{6,14},{7,23},{8,0},{9,25... | collective-permute-start | bytes 1327112 | tf_op jit(solution)/shard_map/ppermute | solution.py:154
  3.3 18.2 %collective-permute-start.6 = (bf16[32,6912]{1,0:T(8,128)(2,1)S(1)}, bf16[32,6912]{1,0:T(8,128)(2,1)S(1)}, u32[]{:S(2)}, u32[]{:S(2)}) collective-permute-start(bf16[32,6912]{1,0:T(8,128)(2,1)S(1)} %get-tuple-element.5), channel_id=1, source_target_pairs={{0,8},{1,17},{2,10},{3,19},{4,12},{5,21},{6,14},{7,23},{8,0},{9,25... | collective-permute-start | bytes 1327112 | tf_op jit(solution)/shard_map/ppermute | solution.py:155
  9.3 12.8 %collective-permute-start.8 = (bf16[32,6912]{1,0:T(8,128)(2,1)S(1)}, bf16[32,6912]{1,0:T(8,128)(2,1)S(1)}, u32[]{:S(2)}, u32[]{:S(2)}) collective-permute-start(bf16[32,6912]{1,0:T(8,128)(2,1)S(1)} %collective-permute-done.4.refs_1_), channel_id=1, source_target_pairs={{0,16},{1,9},{2,18},{3,11},{4,20},{5,13},{6,22},{7,15},{8,24},{9,1... | collective-permute-start | bytes 1327112 | tf_op jit(solution)/shard_map/ppermute | solution.py:157
  11.6 8.9 %collective-permute-start = (bf16[1,2,64,256]{3,2,1,0:T(8,128)(2,1)S(1)}, bf16[1,2,64,256]{3,2,1,0:T(8,128)(2,1)S(1)}, u32[]{:S(2)}, u32[]{:S(2)}) collective-permute-start(bf16[1,2,64,256]{3,2,1,0:T(8,128)(2,1)S(1)} %get-tuple-element.10), channel_id=1, source_target_pairs={{0,8},{8,16},{16,24},{1,9},{9,17},{17,25},{2,10},{10,18},{18,26},{... | collective-permute-start | bytes 196616 | tf_op jit(solution)/shard_map/ppermute | solution.py:134
  13.6 8.6 %collective-permute-start.1 = (bf16[1,2,64,256]{3,2,1,0:T(8,128)(2,1)S(1)}, bf16[1,2,64,256]{3,2,1,0:T(8,128)(2,1)S(1)}, u32[]{:S(2)}, u32[]{:S(2)}) collective-permute-start(bf16[1,2,64,256]{3,2,1,0:T(8,128)(2,1)S(1)} %get-tuple-element.9), channel_id=1, source_target_pairs={{8,0},{16,8},{24,16},{9,1},{17,9},{25,17},{10,2},{18,10},{26,18},{... | collective-permute-start | bytes 196616 | tf_op jit(solution)/shard_map/ppermute | solution.py:135
  21.5 13.7 %collective-permute-start.5 = (bf16[32,6912]{1,0:T(8,128)(2,1)S(1)}, bf16[32,6912]{1,0:T(8,128)(2,1)S(1)}, u32[]{:S(2)}, u32[]{:S(2)}) collective-permute-start(bf16[32,6912]{1,0:T(8,128)(2,1)S(1)} %collective-permute-done.4.refs_1_), channel_id=1, source_target_pairs={{0,1},{1,0},{2,3},{3,2},{4,5},{5,4},{6,7},{7,6},{8,9},{9,8},{10,11... | collective-permute-start | bytes 1327112 | tf_op jit(solution)/shard_map/ppermute | solution.py:159
  21.6 12.5 %collective-permute-start.7 = (bf16[32,6912]{1,0:T(8,128)(2,1)S(1)}, bf16[32,6912]{1,0:T(8,128)(2,1)S(1)}, u32[]{:S(2)}, u32[]{:S(2)}) collective-permute-start(bf16[32,6912]{1,0:T(8,128)(2,1)S(1)} %collective-permute-done.6.refs_0_), channel_id=1, source_target_pairs={{0,1},{1,0},{2,3},{3,2},{4,5},{5,4},{6,7},{7,6},{8,9},{9,8},{10,11... | collective-permute-start | bytes 1327112 | tf_op jit(solution)/shard_map/ppermute | solution.py:160
  22.1 14.2 %collective-permute-start.9 = (bf16[32,6912]{1,0:T(8,128)(2,1)S(1)}, bf16[32,6912]{1,0:T(8,128)(2,1)S(1)}, u32[]{:S(2)}, u32[]{:S(2)}) collective-permute-start(bf16[32,6912]{1,0:T(8,128)(2,1)S(1)} %collective-permute-done.8.here), channel_id=1, source_target_pairs={{0,1},{1,0},{2,3},{3,2},{4,5},{5,4},{6,7},{7,6},{8,9},{9,8},{10,11... | collective-permute-start | bytes 1327112 | tf_op jit(solution)/shard_map/ppermute | solution.py:161
  22.2 6.4 %collective-permute-start.2 = (bf16[4,1,64,256]{3,2,1,0:T(8,128)(2,1)S(1)}, bf16[4,1,64,256]{3,2,1,0:T(8,128)(2,1)S(1)}, u32[]{:S(2)}, u32[]{:S(2)}) collective-permute-start(bf16[4,1,64,256]{3,2,1,0:T(8,128)(2,1)S(1)} %get-tuple-element.8), channel_id=1, source_target_pairs={{0,1},{1,2},{2,3},{3,4},{4,5},{5,6},{6,7},{8,9},{9,10},{10,11},{11... | collective-permute-start | bytes 393224 | tf_op jit(solution)/shard_map/ppermute | solution.py:134
  26.5 8.7 %copy-start = (bf16[6912,64]{0,1:T(8,128)(2,1)S(1)}, bf16[6912,64]{0,1:T(8,128)(2,1)}, u32[]{:S(2)}) copy-start(bf16[6912,64]{0,1:T(8,128)(2,1)} %param.3) | copy-start | bytes 2654212
  26.5 6.4 %collective-permute-start.3 = (bf16[4,1,64,256]{3,2,1,0:T(8,128)(2,1)S(1)}, bf16[4,1,64,256]{3,2,1,0:T(8,128)(2,1)S(1)}, u32[]{:S(2)}, u32[]{:S(2)}) collective-permute-start(bf16[4,1,64,256]{3,2,1,0:T(8,128)(2,1)S(1)} %get-tuple-element.7), channel_id=1, source_target_pairs={{1,0},{2,1},{3,2},{4,3},{5,4},{6,5},{7,6},{9,8},{10,9},{11,10},{12... | collective-permute-start | bytes 393224 | tf_op jit(solution)/shard_map/ppermute | solution.py:135
  32.9 0.9 %copy-start.1 = (bf16[2,2,64,256]{3,2,1,0:T(8,128)(2,1)S(1)}, bf16[2,2,64,256]{3,2,1,0:T(8,128)(2,1)}, u32[]{:S(2)}) copy-start(bf16[2,2,64,256]{3,2,1,0:T(8,128)(2,1)} %volume.1) | copy-start | bytes 393220

commit v2 on v0

v2 whole, which is shorter than its diff:
```python
import jax
import jax.numpy as jnp
from jax import lax
from jax.experimental import pallas as pl
from jax.experimental.pallas import tpu as pltpu
from jax.sharding import PartitionSpec as P

BOTH = ("slab", "chan")
VMEM_LIMIT = 24 * 1024 * 1024


def call(kernel, operands, outs, flops=0, places=None, scratch=()):
    size = sum(x.size * x.dtype.itemsize for x in (*operands, *outs))
    vmem = pl.BlockSpec(memory_space=pltpu.VMEM)
    return pl.pallas_call(
        kernel,
        out_shape=outs,
        in_specs=places or [vmem] * len(operands),
        out_specs=[vmem] * len(outs),
        scratch_shapes=scratch,
        compiler_params=pltpu.CompilerParams(vmem_limit_bytes=VMEM_LIMIT),
        cost_estimate=pl.CostEstimate(flops=flops, bytes_accessed=size, transcendentals=0),
        name=kernel.__name__,
    )(*operands)


def like(shape, array):
    return jax.ShapeDtypeStruct(shape, array.dtype)


def core_parity():
    return lax.rem(lax.axis_index("chan"), 2)


def slab_x():
    return lax.rem(lax.axis_index("slab"), 2)


def slab_y():
    return lax.div(lax.axis_index("slab"), 2)


def fetch(volume, kernel_rows, first, second, block, sems):
    count = first.shape[0]
    start = core_parity() * 2 * count
    copies = [
        pltpu.make_async_copy(kernel_rows.at[pl.ds(pl.multiple_of(start, count), count), :], first, sems.at[0]),
        pltpu.make_async_copy(kernel_rows.at[pl.ds(pl.multiple_of(start + count, count), count), :], second, sems.at[1]),
        pltpu.make_async_copy(volume, block, sems.at[2]),
    ]
    for copy in copies:
        copy.start()
    for copy in copies:
        copy.wait()


def border(block, across, out):
    plane = (block.shape[0] - 1) * (1 - slab_y())
    for r in range(block.shape[1]):
        out[0, r] = jnp.where(slab_x() == slab_y(), across[plane, r], block[plane, r])


def edges(block, across, to_core, to_chip):
    depth, rows = block.shape[:2]
    core = core_parity()
    for out, row in ((to_core, (rows - 1) * (1 - core)), (to_chip, (rows - 1) * core)):
        for d in range(depth):
            out[d, 0] = block[d, row]
            out[depth + d, 0] = across[d, row]


def outer_edges(outer, to_core, to_chip):
    rows = outer.shape[1]
    core = core_parity()
    for out, row in ((to_core, (rows - 1) * (1 - core)), (to_chip, (rows - 1) * core)):
        out[0, 0] = outer[0, row]


def extend(block, across, outer, from_core, from_chip, outer_core, outer_chip, lines):
    depth, rows = block.shape[:2]
    even_core = core_parity() == 0
    first, second = depth * slab_x() + 1, depth * (1 - slab_x()) + 1
    beyond = (2 * depth + 1) * (1 - slab_y())
    empty = (2 * depth + 1) * slab_y()
    for d in range(2 * depth + 1):
        if d < depth:
            target, source, core_row, chip_row = first + d, block.at[d], from_core[d, 0], from_chip[d, 0]
        elif d < 2 * depth:
            target, source, core_row, chip_row = second + d - depth, across.at[d - depth], from_core[d, 0], from_chip[d, 0]
        else:
            target, source, core_row, chip_row = beyond, outer.at[0], outer_core[0, 0], outer_chip[0, 0]
        lines[target, 0] = jnp.where(even_core, chip_row, core_row)
        for r in range(rows):
            lines[target, r + 1] = source[r]
        lines[target, rows + 1] = jnp.where(even_core, core_row, chip_row)
    lines[empty] = jnp.zeros(lines.shape[1:], lines.dtype)


def convolve(lines, base, depth, pieces):
    rows, cols, channels = lines.shape[1] - 2, *lines.shape[2:]
    voxels = depth * rows * cols
    width = sum(piece.shape[0] for piece in pieces)
    total = None
    for a in range(3):
        for b in range(3):
            moved = lines[pl.ds(base + a, depth), b : b + rows].reshape(voxels, channels)
            taps = [
                piece[:, (9 * a + 3 * b + e) * channels : (9 * a + 3 * b + e + 1) * channels]
                for e in range(3)
                for piece in pieces
            ]
            term = lax.dot_general(
                moved, jnp.concatenate(taps, axis=0), (((1,), (1,)), ((), ())), preferred_element_type=jnp.float32
            )
            total = term if total is None else total + term
    col = lax.rem(lax.broadcasted_iota(jnp.int32, (voxels, width), 0), cols)
    before = jnp.where(col == 0, 0.0, pltpu.roll(total[:, :width], 1, 0))
    after = jnp.where(col == cols - 1, 0.0, pltpu.roll(total[:, 2 * width :], voxels - 1, 0))
    return before + total[:, width : 2 * width] + after


def ordered(sums):
    half = sums.shape[1] // 2
    swapped = jnp.concatenate([sums[:, half:], sums[:, :half]], axis=1)
    return jnp.where(core_parity() == 0, sums, swapped)


def near(lines, kernel_rows, out):
    depth = (lines.shape[0] - 2) // 2
    out[...] = convolve(lines, depth * (1 - slab_x()), depth, [kernel_rows]).astype(out.dtype)


def back(lines, near_sums, *refs):
    depth = (lines.shape[0] - 2) // 2
    *pieces, out = refs
    sums = ordered(convolve(lines, depth * (1 - slab_x()), depth, pieces))
    out[...] = jnp.concatenate([near_sums[...], sums.astype(out.dtype)], axis=1)


def kept(lines, kernel_rows, *refs):
    depth = (lines.shape[0] - 2) // 2
    *pieces, out = refs
    width = kernel_rows.shape[0]
    sums = convolve(lines, depth * slab_x(), depth, [kernel_rows, *pieces])
    out[...] = jnp.concatenate([sums[:, :width], ordered(sums[:, width:])], axis=1).astype(out.dtype)


def join(kept_sums, returned, out):
    width = kept_sums.shape[1] // 2
    mine, theirs = kept_sums[...].astype(jnp.float32), returned[...].astype(jnp.float32)
    blocks = [mine[:, :width], theirs[:, :width], mine[:, width:], theirs[:, width:]]
    odd_x, odd_y = slab_x() == 1, slab_y() == 1
    blocks = [jnp.where(odd_x, blocks[j ^ 1], blocks[j]) for j in range(4)]
    blocks = [jnp.where(odd_y, blocks[j ^ 2], blocks[j]) for j in range(4)]
    out[...] = jnp.concatenate(blocks, axis=1).astype(out.dtype)


def four_slabs(volume, weights):
    chans = lax.axis_size("chan")
    depth, rows, cols, channels = volume.shape
    voxels = depth * rows * cols
    kernel_rows = weights.T
    width, depth_of_sum = kernel_rows.shape

    def send(array, target):
        every = [(s * chans + c, target(s, c)) for s in range(4) for c in range(chans)]
        pairs = [(source, s * chans + c) for source, (s, c) in every if 0 <= s < 4 and 0 <= c < chans]
        return lax.ppermute(array, BOTH, pairs)

    def across_x(s, c):
        return s ^ 1, c

    def across_y(s, c):
        return s ^ 2, c

    def other_core(s, c):
        return s, c ^ 1

    def next_chip(s, c):
        return s, c + (1 if c % 2 else -1)

    across = send(volume, across_x)
    piece = like((width // 4, depth_of_sum), weights)
    first, second, block = call(
        fetch,
        [pltpu.with_memory_space_constraint(x, pltpu.HBM) for x in (volume, kernel_rows)],
        [piece, piece, like(volume.shape, volume)],
        places=[pl.BlockSpec(memory_space=pltpu.HBM)] * 2,
        scratch=[pltpu.SemaphoreType.DMA((3,))],
    )
    here_first = send(first, across_y)
    second, across = lax.optimization_barrier((second, across))
    (plane,) = call(border, (block, across), [like((1, rows, cols, channels), volume)], 1000000000)
    outer = send(plane, across_y)
    here_second = send(second, across_y)
    edge, outer_edge = like((2 * depth, 1, cols, channels), volume), like((1, 1, cols, channels), volume)
    to_core, to_chip = call(edges, (block, across), [edge, edge])
    from_core, from_chip = send(to_core, other_core), send(to_chip, next_chip)
    outer, here_first = lax.optimization_barrier((outer, here_first))
    to_core, to_chip = call(outer_edges, (outer,), [outer_edge, outer_edge], 3000000000)
    outer_core, outer_chip = send(to_core, other_core), send(to_chip, next_chip)
    (lines,) = call(
        extend,
        (block, across, outer, from_core, from_chip, outer_core, outer_chip),
        [like((2 * depth + 2, rows + 2, cols, channels), volume)],
    )
    work = 2 * voxels * depth_of_sum * width
    (near_sums,) = call(near, (lines, kernel_rows), [like((voxels, width), volume)], work)
    there_first = send(here_first, other_core)
    here_second, held = lax.optimization_barrier((here_second, lines))
    there_second = send(here_second, other_core)
    pieces = (here_first, here_second, there_first, there_second)
    both = like((voxels, 2 * width), volume)
    (sent,) = call(back, (lines, near_sums, *pieces), [both], work)
    returned = send(sent, across_x)
    (mine,) = call(kept, (lines, kernel_rows, *pieces), [both], 2 * work)
    (out,) = call(join, (mine, returned), [like((voxels, 4 * width), volume)])
    return out.reshape(volume.shape)


def halo(block, axis, dim):
    count = lax.axis_size(axis)
    forward = [(i, i + 1) for i in range(count - 1)]
    backward = [(target, source) for source, target in forward]
    extent = block.shape[dim]
    low = lax.ppermute(lax.slice_in_dim(block, extent - 1, extent, axis=dim), axis, forward)
    high = lax.ppermute(lax.slice_in_dim(block, 0, 1, axis=dim), axis, backward)
    return jnp.concatenate([low, block, high], axis=dim)


def whole(lines, kernel_rows, out):
    out[...] = convolve(lines, 0, lines.shape[0] - 2, [kernel_rows]).astype(out.dtype)


def any_slabs(volume, weights):
    gathered = lax.all_gather(weights.T, "slab", axis=0, tiled=True)
    lines = halo(halo(volume, "slab", 0), "chan", 1)
    voxels, (width, depth_of_sum) = volume.size // volume.shape[-1], gathered.shape
    (out,) = call(whole, (lines, gathered), [like((voxels, width), volume)], 2 * voxels * depth_of_sum * width)
    return out.reshape(volume.shape)


def local(volume, weights):
    if lax.axis_size("slab") == 4 and lax.axis_size("chan") % 2 == 0:
        return four_slabs(volume, weights)
    return any_slabs(volume, weights)


def solution(mesh):
    placed = (P("slab", "chan", None, None), P(None, "slab"))
    return jax.shard_map(
        local, mesh=mesh, in_specs=placed, out_specs=P("slab", "chan", None, None), check_vma=False
    )
```

time: 72.7 us -> 25.7 us (0.35)
  waiting for transfers between devices: 39.2 us -> 6.97 us
  between operations: 13.7 us -> 0.1 us
  matrix products: 6.33 us -> 0 us
  Pallas kernels: 0 us -> 4.29 us
  starting transfers between devices: 10.5 us -> 14.2 us
  local copies, waits for them, and re-layouts: 2.38 us -> 0.01 us
    all_gather x1 -> x0, waiting for transfers between devices: 32.7 us -> none  [local(): gathered = lax.all_gather(weights, 'slab', axis=1, tiled=True)]
    dot_general x3 -> x0, matrix products: 6.33 us -> none  [local(): jnp.dot(columns, kernel_rows, preferred_element_type=jnp.float32)]
    pallas_call x0 -> x9, Pallas kernels: none -> 4.29 us  [call(): pl.pallas_call(kernel, out_shape=outs, in_specs=places or [vmem] * len(op...]
    ppermute x4 -> x11, starting transfers between devices: 10.5 us -> 14.2 us  [send(): return lax.ppermute(array, BOTH, pairs)]
    slice x3 -> x0, local copies, waits for them, and re-layouts: 1.23 us -> none  [the longest x1 0.88 us: extended_2(): lax.slice_in_dim(block, 0, width, axis=dim)]
    ppermute x4 -> x11, waiting for transfers between devices: 5.81 us -> 6.97 us  [send(): return lax.ppermute(array, BOTH, pairs)]
    unnamed x29 -> x2, local copies, waits for them, and re-layouts: 1.12 us -> 0.01 us
  transfers between devices with their start and end apart: 5 -> 11, of which waited for: 4 -> 5; matrix products, arithmetic and copies ran while one was open for 3% -> 0% of each run, Pallas kernels for 0% -> 11%
where the time goes in v2:
time: 25.7 us; the launch traced here: 25.5 us
  starting transfers between devices  14.2 us (55%)
  waiting for transfers between devices  6.97 us (27%)
  Pallas kernels  4.29 us (17%)
    ppermute x11, starting transfers between devices, send(): return lax.ppermute(array, BOTH, pairs)  14.2 us
    ppermute x11, waiting for transfers between devices, send(): return lax.ppermute(array, BOTH, pairs)  6.97 us
    pallas_call x9, Pallas kernels, call(): pl.pallas_call(kernel, out_shape=outs, in_specs=places or [vmem] * len(op...  4.29 us
  transfers between devices with their start and end apart: 11, of which 5 were waited for; matrix products, arithmetic and copies ran while one was open for 0% of the time, Pallas kernels for 11%

profile of v2, /device:TPU:0, one launch (start us, length us, event | category | flops | bytes accessed | tf_op | source)
XLA Modules:
  0.0 25.5 jit_solution(6011818785329811543)
XLA Ops:
  0.0 2.9 %collective-permute-start = (bf16[2,2,64,256]{3,2,1,0:T(8,128)(2,1)}, bf16[2,2,64,256]{3,2,1,0:T(8,128)(2,1)S(1)}, u32[]{:S(2)}, u32[]{:S(2)}) collective-permute-start(bf16[2,2,64,256]{3,2,1,0:T(8,128)(2,1)} %volume.1), channel_id=1, source_target_pairs={{0,8},{1,9},{2,10},{3,11},{4,12},{5,13},{6,14},{7,15},{8,0},{9,1},... | collective-permute-start | bytes 393224 | tf_op jit(solution)/shard_map/ppermute | solution.py:168
  2.9 1.1 %fetch.1 = (bf16[16,6912]{1,0:T(8,128)(2,1)S(1)}, bf16[16,6912]{1,0:T(8,128)(2,1)S(1)}, bf16[2,2,64,256]{3,2,1,0:T(8,128)(2,1)S(1)}) custom-call(bf16[2,2,64,256]{3,2,1,0:T(8,128)(2,1)} %volume.1, bf16[64,6912]{1,0:T(8,128)(2,1)} %bitcast.2), custom_call_target="tpu_custom_call" | custom-call | bytes 1589248 | tf_op jit(solution)/shard_map/fetch/pallas_call | solution.py:15
  4.1 1.6 %collective-permute-start.2 = (bf16[16,6912]{1,0:T(8,128)(2,1)S(1)}, bf16[16,6912]{1,0:T(8,128)(2,1)S(1)}, u32[]{:S(2)}, u32[]{:S(2)}) collective-permute-start(bf16[16,6912]{1,0:T(8,128)(2,1)S(1)} %get-tuple-element.20), channel_id=1, source_target_pairs={{0,16},{1,17},{2,18},{3,19},{4,20},{5,21},{6,22},{7,23},{8,24},{9,... | collective-permute-start | bytes 663560 | tf_op jit(solution)/shard_map/ppermute | solution.py:168
  5.7 1.0 %collective-permute-done.across = bf16[2,2,64,256]{3,2,1,0:T(8,128)(2,1)S(1)} collective-permute-done((bf16[2,2,64,256]{3,2,1,0:T(8,128)(2,1)}, bf16[2,2,64,256]{3,2,1,0:T(8,128)(2,1)S(1)}, u32[]{:S(2)}, u32[]{:S(2)}) %collective-permute-start) | collective-permute-done | bytes 131104 | tf_op jit(solution)/shard_map/ppermute | solution.py:168
  6.7 1.8 %collective-permute-start.1 = (bf16[1,2,64,256]{3,2,1,0:T(8,128)(2,1)S(1)}, bf16[1,2,64,256]{3,2,1,0:T(8,128)(2,1)S(1)}, u32[]{:S(2)}, u32[]{:S(2)}) collective-permute-start(bf16[1,2,64,256]{3,2,1,0:T(8,128)(2,1)S(1)} %border.1), channel_id=1, source_target_pairs={{0,16},{1,17},{2,18},{3,19},{4,20},{5,21},{6,22},{7,23},{8,24},{9,... | collective-permute-start | bytes 196616 | tf_op jit(solution)/shard_map/ppermute | solution.py:168
  8.5 0.1 collective-permute-start.3
  8.6 0.7 %collective-permute-start.4 = (bf16[4,1,64,256]{3,2,1,0:T(8,128)(2,1)S(1)}, bf16[4,1,64,256]{3,2,1,0:T(8,128)(2,1)S(1)}, u32[]{:S(2)}, u32[]{:S(2)}) collective-permute-start(bf16[4,1,64,256]{3,2,1,0:T(8,128)(2,1)S(1)} %get-tuple-element.23), channel_id=1, source_target_pairs={{1,2},{2,1},{3,4},{4,3},{5,6},{6,5},{9,10},{10,9},{11,12},{12,11},... | collective-permute-start | bytes 393224 | tf_op jit(solution)/shard_map/ppermute | solution.py:168
  9.3 0.3 %collective-permute-start.7 = (bf16[16,6912]{1,0:T(8,128)(2,1)S(1)}, bf16[16,6912]{1,0:T(8,128)(2,1)S(1)}, u32[]{:S(2)}, u32[]{:S(2)}) collective-permute-start(bf16[16,6912]{1,0:T(8,128)(2,1)S(1)} %get-tuple-element.27), channel_id=1, source_target_pairs={{0,16},{1,17},{2,18},{3,19},{4,20},{5,21},{6,22},{7,23},{8,24},{9,... | collective-permute-start | bytes 663560 | tf_op jit(solution)/shard_map/ppermute | solution.py:168
  9.6 2.9 %collective-permute-done.1.outer = bf16[1,2,64,256]{3,2,1,0:T(8,128)(2,1)S(1)} collective-permute-done((bf16[1,2,64,256]{3,2,1,0:T(8,128)(2,1)S(1)}, bf16[1,2,64,256]{3,2,1,0:T(8,128)(2,1)S(1)}, u32[]{:S(2)}, u32[]{:S(2)}) %collective-permute-start.1) | collective-permute-done | bytes 65568 | tf_op jit(solution)/shard_map/ppermute | solution.py:168
  12.4 0.0 collective-permute-done.2.refs_0_
  12.5 0.0 copy-start
  12.5 0.1 collective-permute-start.5
  12.6 0.8 %collective-permute-start.6 = (bf16[1,1,64,256]{3,2,1,0:T(8,128)(2,1)S(1)}, bf16[1,1,64,256]{3,2,1,0:T(8,128)(2,1)S(1)}, u32[]{:S(2)}, u32[]{:S(2)}) collective-permute-start(bf16[1,1,64,256]{3,2,1,0:T(8,128)(2,1)S(1)} %get-tuple-element.25), channel_id=1, source_target_pairs={{1,2},{2,1},{3,4},{4,3},{5,6},{6,5},{9,10},{10,9},{11,12},{12,11},... | collective-permute-start | bytes 98312 | tf_op jit(solution)/shard_map/ppermute | solution.py:168
  13.4 0.4 %collective-permute-done.5.outer_core = bf16[1,1,64,256]{3,2,1,0:T(8,128)(2,1)S(1)} collective-permute-done((bf16[1,1,64,256]{3,2,1,0:T(8,128)(2,1)S(1)}, bf16[1,1,64,256]{3,2,1,0:T(8,128)(2,1)S(1)}, u32[]{:S(2)}, u32[]{:S(2)}) %collective-permute-start.5) | collective-permute-done | bytes 32800 | tf_op jit(solution)/shard_map/ppermute | solution.py:168
  13.7 2.6 %collective-permute-start.8 = (bf16[16,6912]{1,0:T(8,128)(2,1)S(1)}, bf16[16,6912]{1,0:T(8,128)(2,1)S(1)}, u32[]{:S(2)}, u32[]{:S(2)}) collective-permute-start(bf16[16,6912]{1,0:T(8,128)(2,1)S(1)} %collective-permute-done.2.refs_0_), channel_id=1, source_target_pairs={{0,1},{1,0},{2,3},{3,2},{4,5},{5,4},{6,7},{7,6},{8,9},{9,8},{10,11... | collective-permute-start | bytes 663560 | tf_op jit(solution)/shard_map/ppermute | solution.py:168
  16.4 0.0 collective-permute-done.6.outer_chip
  16.4 0.0 collective-permute-done.3.from_core
  16.4 0.0 collective-permute-done.4.from_chip
  16.4 0.1 extend.1.lines
  16.5 0.0 collective-permute-done.7.refs_1_
  16.5 1.9 %collective-permute-start.9 = (bf16[16,6912]{1,0:T(8,128)(2,1)S(1)}, bf16[16,6912]{1,0:T(8,128)(2,1)S(1)}, u32[]{:S(2)}, u32[]{:S(2)}) collective-permute-start(bf16[16,6912]{1,0:T(8,128)(2,1)S(1)} %collective-permute-done.7.refs_1_), channel_id=1, source_target_pairs={{0,1},{1,0},{2,3},{3,2},{4,5},{5,4},{6,7},{7,6},{8,9},{9,8},{10,11... | collective-permute-start | bytes 663560 | tf_op jit(solution)/shard_map/ppermute | solution.py:168
  18.4 0.0 copy-done
  18.4 0.6 %near.1.near_sums = bf16[256,64]{1,0:T(8,128)(2,1)S(1)} custom-call(bf16[6,4,64,256]{3,2,1,0:T(8,128)(2,1)S(1)} %extend.1.lines, bf16[64,6912]{1,0:T(8,128)(2,1)S(1)} %bitcast.3), custom_call_target="tpu_custom_call" | custom-call | flops 226492416 | bytes 1703936 | tf_op jit(solution)/shard_map/near/pallas_call | solution.py:15
  19.0 0.0 collective-permute-done.8.refs_2_
  19.0 0.5 %collective-permute-done.9.refs_3_ = bf16[16,6912]{1,0:T(8,128)(2,1)S(1)} collective-permute-done((bf16[16,6912]{1,0:T(8,128)(2,1)S(1)}, bf16[16,6912]{1,0:T(8,128)(2,1)S(1)}, u32[]{:S(2)}, u32[]{:S(2)}) %collective-permute-start.9) | collective-permute-done | bytes 221216 | tf_op jit(solution)/shard_map/ppermute | solution.py:168
  19.5 0.7 %back.1 = bf16[256,128]{1,0:T(8,128)(2,1)S(1)} custom-call(bf16[6,4,64,256]{3,2,1,0:T(8,128)(2,1)S(1)} %extend.1.lines, bf16[256,64]{1,0:T(8,128)(2,1)S(1)} %near.1.near_sums, bf16[16,6912]{1,0:T(8,128)(2,1)S(1)} %collective-permute-done.2.refs_0_, bf16[16,6912]{1,0:T(8,128)(2,1)S(1)} %collective-permute-done.7.refs_1_, ...), custom_call_target="tpu_custom_call" | custom-call | flops 226492416 | bytes 1769472 | tf_op jit(solution)/shard_map/back/pallas_call | solution.py:15
  20.2 1.3 %collective-permute-start.10 = (bf16[256,128]{1,0:T(8,128)(2,1)S(1)}, bf16[256,128]{1,0:T(8,128)(2,1)S(1)}, u32[]{:S(2)}, u32[]{:S(2)}) collective-permute-start(bf16[256,128]{1,0:T(8,128)(2,1)S(1)} %back.1), channel_id=1, source_target_pairs={{0,8},{1,9},{2,10},{3,11},{4,12},{5,13},{6,14},{7,15},{8,0},{9,1},... | collective-permute-start | bytes 196616 | tf_op jit(solution)/shard_map/ppermute | solution.py:168
  21.5 0.9 %kept.1.kept_sums = bf16[256,128]{1,0:T(8,128)(2,1)S(1)} custom-call(bf16[6,4,64,256]{3,2,1,0:T(8,128)(2,1)S(1)} %extend.1.lines, bf16[64,6912]{1,0:T(8,128)(2,1)S(1)} %bitcast.4, bf16[16,6912]{1,0:T(8,128)(2,1)S(1)} %collective-permute-done.2.refs_0_, bf16[16,6912]{1,0:T(8,128)(2,1)S(1)} %collective-permute-done.7.refs_1_, ...), custom_call_target="tpu_custom_call" | custom-call | flops 452984832 | bytes 2621440 | tf_op jit(solution)/shard_map/kept/pallas_call | solution.py:15
  22.5 2.2 %collective-permute-done.10.returned = bf16[256,128]{1,0:T(8,128)(2,1)S(1)} collective-permute-done((bf16[256,128]{1,0:T(8,128)(2,1)S(1)}, bf16[256,128]{1,0:T(8,128)(2,1)S(1)}, u32[]{:S(2)}, u32[]{:S(2)}) %collective-permute-start.10) | collective-permute-done | bytes 65568 | tf_op jit(solution)/shard_map/ppermute | solution.py:168
  24.7 0.8 %join.1 = bf16[256,256]{1,0:T(8,128)(2,1)} custom-call(bf16[256,128]{1,0:T(8,128)(2,1)S(1)} %kept.1.kept_sums, bf16[256,128]{1,0:T(8,128)(2,1)S(1)} %collective-permute-done.10.returned), custom_call_target="tpu_custom_call" | custom-call | bytes 262144 | tf_op jit(solution)/shard_map/join/pallas_call | solution.py:15
  (3 shorter events, 0.0 us)
Async XLA Ops:
  0.0 6.6 %collective-permute-start = (bf16[2,2,64,256]{3,2,1,0:T(8,128)(2,1)}, bf16[2,2,64,256]{3,2,1,0:T(8,128)(2,1)S(1)}, u32[]{:S(2)}, u32[]{:S(2)}) collective-permute-start(bf16[2,2,64,256]{3,2,1,0:T(8,128)(2,1)} %volume.1), channel_id=1, source_target_pairs={{0,8},{1,9},{2,10},{3,11},{4,12},{5,13},{6,14},{7,15},{8,0},{9,1},... | collective-permute-start | bytes 393224 | tf_op jit(solution)/shard_map/ppermute | solution.py:168
  4.1 8.4 %collective-permute-start.2 = (bf16[16,6912]{1,0:T(8,128)(2,1)S(1)}, bf16[16,6912]{1,0:T(8,128)(2,1)S(1)}, u32[]{:S(2)}, u32[]{:S(2)}) collective-permute-start(bf16[16,6912]{1,0:T(8,128)(2,1)S(1)} %get-tuple-element.20), channel_id=1, source_target_pairs={{0,16},{1,17},{2,18},{3,19},{4,20},{5,21},{6,22},{7,23},{8,24},{9,... | collective-permute-start | bytes 663560 | tf_op jit(solution)/shard_map/ppermute | solution.py:168
  6.7 5.8 %collective-permute-start.1 = (bf16[1,2,64,256]{3,2,1,0:T(8,128)(2,1)S(1)}, bf16[1,2,64,256]{3,2,1,0:T(8,128)(2,1)S(1)}, u32[]{:S(2)}, u32[]{:S(2)}) collective-permute-start(bf16[1,2,64,256]{3,2,1,0:T(8,128)(2,1)S(1)} %border.1), channel_id=1, source_target_pairs={{0,16},{1,17},{2,18},{3,19},{4,20},{5,21},{6,22},{7,23},{8,24},{9,... | collective-permute-start | bytes 196616 | tf_op jit(solution)/shard_map/ppermute | solution.py:168
  8.5 7.9 %collective-permute-start.3 = (bf16[4,1,64,256]{3,2,1,0:T(8,128)(2,1)S(1)}, bf16[4,1,64,256]{3,2,1,0:T(8,128)(2,1)S(1)}, u32[]{:S(2)}, u32[]{:S(2)}) collective-permute-start(bf16[4,1,64,256]{3,2,1,0:T(8,128)(2,1)S(1)} %get-tuple-element.22), channel_id=1, source_target_pairs={{0,1},{1,0},{2,3},{3,2},{4,5},{5,4},{6,7},{7,6},{8,9},{9,8},{10,11... | collective-permute-start | bytes 393224 | tf_op jit(solution)/shard_map/ppermute | solution.py:168
  8.6 7.8 %collective-permute-start.4 = (bf16[4,1,64,256]{3,2,1,0:T(8,128)(2,1)S(1)}, bf16[4,1,64,256]{3,2,1,0:T(8,128)(2,1)S(1)}, u32[]{:S(2)}, u32[]{:S(2)}) collective-permute-start(bf16[4,1,64,256]{3,2,1,0:T(8,128)(2,1)S(1)} %get-tuple-element.23), channel_id=1, source_target_pairs={{1,2},{2,1},{3,4},{4,3},{5,6},{6,5},{9,10},{10,9},{11,12},{12,11},... | collective-permute-start | bytes 393224 | tf_op jit(solution)/shard_map/ppermute | solution.py:168
  9.3 7.2 %collective-permute-start.7 = (bf16[16,6912]{1,0:T(8,128)(2,1)S(1)}, bf16[16,6912]{1,0:T(8,128)(2,1)S(1)}, u32[]{:S(2)}, u32[]{:S(2)}) collective-permute-start(bf16[16,6912]{1,0:T(8,128)(2,1)S(1)} %get-tuple-element.27), channel_id=1, source_target_pairs={{0,16},{1,17},{2,18},{3,19},{4,20},{5,21},{6,22},{7,23},{8,24},{9,... | collective-permute-start | bytes 663560 | tf_op jit(solution)/shard_map/ppermute | solution.py:168
  12.5 6.0 %copy-start = (bf16[6912,64]{0,1:T(8,128)(2,1)S(1)}, bf16[6912,64]{0,1:T(8,128)(2,1)}, u32[]{:S(2)}) copy-start(bf16[6912,64]{0,1:T(8,128)(2,1)} %param.3) | copy-start | bytes 2654212
  12.5 1.3 %collective-permute-start.5 = (bf16[1,1,64,256]{3,2,1,0:T(8,128)(2,1)S(1)}, bf16[1,1,64,256]{3,2,1,0:T(8,128)(2,1)S(1)}, u32[]{:S(2)}, u32[]{:S(2)}) collective-permute-start(bf16[1,1,64,256]{3,2,1,0:T(8,128)(2,1)S(1)} %get-tuple-element.24), channel_id=1, source_target_pairs={{0,1},{1,0},{2,3},{3,2},{4,5},{5,4},{6,7},{7,6},{8,9},{9,8},{10,11... | collective-permute-start | bytes 98312 | tf_op jit(solution)/shard_map/ppermute | solution.py:168
  12.6 3.8 %collective-permute-start.6 = (bf16[1,1,64,256]{3,2,1,0:T(8,128)(2,1)S(1)}, bf16[1,1,64,256]{3,2,1,0:T(8,128)(2,1)S(1)}, u32[]{:S(2)}, u32[]{:S(2)}) collective-permute-start(bf16[1,1,64,256]{3,2,1,0:T(8,128)(2,1)S(1)} %get-tuple-element.25), channel_id=1, source_target_pairs={{1,2},{2,1},{3,4},{4,3},{5,6},{6,5},{9,10},{10,9},{11,12},{12,11},... | collective-permute-start | bytes 98312 | tf_op jit(solution)/shard_map/ppermute | solution.py:168
  13.7 5.3 %collective-permute-start.8 = (bf16[16,6912]{1,0:T(8,128)(2,1)S(1)}, bf16[16,6912]{1,0:T(8,128)(2,1)S(1)}, u32[]{:S(2)}, u32[]{:S(2)}) collective-permute-start(bf16[16,6912]{1,0:T(8,128)(2,1)S(1)} %collective-permute-done.2.refs_0_), channel_id=1, source_target_pairs={{0,1},{1,0},{2,3},{3,2},{4,5},{5,4},{6,7},{7,6},{8,9},{9,8},{10,11... | collective-permute-start | bytes 663560 | tf_op jit(solution)/shard_map/ppermute | solution.py:168
  16.5 3.0 %collective-permute-start.9 = (bf16[16,6912]{1,0:T(8,128)(2,1)S(1)}, bf16[16,6912]{1,0:T(8,128)(2,1)S(1)}, u32[]{:S(2)}, u32[]{:S(2)}) collective-permute-start(bf16[16,6912]{1,0:T(8,128)(2,1)S(1)} %collective-permute-done.7.refs_1_), channel_id=1, source_target_pairs={{0,1},{1,0},{2,3},{3,2},{4,5},{5,4},{6,7},{7,6},{8,9},{9,8},{10,11... | collective-permute-start | bytes 663560 | tf_op jit(solution)/shard_map/ppermute | solution.py:168
  20.2 4.4 %collective-permute-start.10 = (bf16[256,128]{1,0:T(8,128)(2,1)S(1)}, bf16[256,128]{1,0:T(8,128)(2,1)S(1)}, u32[]{:S(2)}, u32[]{:S(2)}) collective-permute-start(bf16[256,128]{1,0:T(8,128)(2,1)S(1)} %back.1), channel_id=1, source_target_pairs={{0,8},{1,9},{2,10},{3,11},{4,12},{5,13},{6,14},{7,15},{8,0},{9,1},... | collective-permute-start | bytes 196616 | tf_op jit(solution)/shard_map/ppermute | solution.py:168

commit v3 on v2

--- a/solution.py
+++ b/solution.py
@@ -7,6 +7,7 @@
 
 BOTH = ("slab", "chan")
 VMEM_LIMIT = 24 * 1024 * 1024
+EARLY_TAPS = 9
 
 
 def call(kernel, operands, outs, flops=0, places=None, scratch=()):
@@ -41,11 +42,11 @@
 
 
 def fetch(volume, kernel_rows, first, second, block, sems):
-    count = first.shape[0]
-    start = core_parity() * 2 * count
+    count, early = first.shape
+    rows = pl.ds(pl.multiple_of(core_parity() * count, count), count)
     copies = [
-        pltpu.make_async_copy(kernel_rows.at[pl.ds(pl.multiple_of(start, count), count), :], first, sems.at[0]),
-        pltpu.make_async_copy(kernel_rows.at[pl.ds(pl.multiple_of(start + count, count), count), :], second, sems.at[1]),
+        pltpu.make_async_copy(kernel_rows.at[rows, pl.ds(0, early)], first, sems.at[0]),
+        pltpu.make_async_copy(kernel_rows.at[rows, pl.ds(early, second.shape[1])], second, sems.at[1]),
         pltpu.make_async_copy(volume, block, sems.at[2]),
     ]
     for copy in copies:
@@ -96,23 +97,26 @@
     lines[empty] = jnp.zeros(lines.shape[1:], lines.dtype)
 
 
-def convolve(lines, base, depth, pieces):
+def convolve(lines, base, depth, kernel_rows, pieces):
     rows, cols, channels = lines.shape[1] - 2, *lines.shape[2:]
     voxels = depth * rows * cols
-    width = sum(piece.shape[0] for piece in pieces)
     total = None
-    for a in range(3):
-        for b in range(3):
-            moved = lines[pl.ds(base + a, depth), b : b + rows].reshape(voxels, channels)
-            taps = [
-                piece[:, (9 * a + 3 * b + e) * channels : (9 * a + 3 * b + e + 1) * channels]
-                for e in range(3)
-                for piece in pieces
-            ]
-            term = lax.dot_general(
-                moved, jnp.concatenate(taps, axis=0), (((1,), (1,)), ((), ())), preferred_element_type=jnp.float32
-            )
-            total = term if total is None else total + term
+    for tap in range(0, 27, 3):
+        a, b = tap // 9, tap // 3 % 3
+        moved = lines[pl.ds(base + a, depth), b : b + rows].reshape(voxels, channels)
+        stack = []
+        for e in range(3):
+            at = (tap + e) * channels
+            stack.append(kernel_rows[:, at : at + channels])
+            for first, second in pieces:
+                early = first.shape[1]
+                array, start = (first, at) if at < early else (second, at - early)
+                stack.append(array[:, start : start + channels])
+        term = lax.dot_general(
+            moved, jnp.concatenate(stack, axis=0), (((1,), (1,)), ((), ())), preferred_element_type=jnp.float32
+        )
+        total = term if total is None else total + term
+    width = total.shape[1] // 3
     col = lax.rem(lax.broadcasted_iota(jnp.int32, (voxels, width), 0), cols)
     before = jnp.where(col == 0, 0.0, pltpu.roll(total[:, :width], 1, 0))
     after = jnp.where(col == cols - 1, 0.0, pltpu.roll(total[:, 2 * width :], voxels - 1, 0))
@@ -125,34 +129,35 @@
     return jnp.where(core_parity() == 0, sums, swapped)
 
 
-def near(lines, kernel_rows, out):
-    depth = (lines.shape[0] - 2) // 2
-    out[...] = convolve(lines, depth * (1 - slab_x()), depth, [kernel_rows]).astype(out.dtype)
-
-
-def back(lines, near_sums, *refs):
-    depth = (lines.shape[0] - 2) // 2
+def both_slabs(lines, base, kernel_rows, pieces, out):
+    width = kernel_rows.shape[0]
+    here_first, here_second, there_first, there_second = pieces
+    pieces = ((here_first, here_second), (there_first, there_second))
+    sums = convolve(lines, base, (lines.shape[0] - 2) // 2, kernel_rows, pieces)
+    near, far = sums[:, :width], ordered(sums[:, width:])
+    even = jnp.concatenate([near, far], axis=1)
+    out[...] = jnp.where(slab_x() == 0, even, jnp.concatenate([far, near], axis=1)).astype(out.dtype)
+
+
+def back(lines, kernel_rows, *refs):
     *pieces, out = refs
-    sums = ordered(convolve(lines, depth * (1 - slab_x()), depth, pieces))
-    out[...] = jnp.concatenate([near_sums[...], sums.astype(out.dtype)], axis=1)
+    both_slabs(lines, (lines.shape[0] - 2) // 2 * (1 - slab_x()), kernel_rows, pieces, out)
 
 
 def kept(lines, kernel_rows, *refs):
-    depth = (lines.shape[0] - 2) // 2
     *pieces, out = refs
-    width = kernel_rows.shape[0]
-    sums = convolve(lines, depth * slab_x(), depth, [kernel_rows, *pieces])
-    out[...] = jnp.concatenate([sums[:, :width], ordered(sums[:, width:])], axis=1).astype(out.dtype)
+    both_slabs(lines, (lines.shape[0] - 2) // 2 * slab_x(), kernel_rows, pieces, out)
 
 
 def join(kept_sums, returned, out):
-    width = kept_sums.shape[1] // 2
+    voxels, width = kept_sums.shape
     mine, theirs = kept_sums[...].astype(jnp.float32), returned[...].astype(jnp.float32)
-    blocks = [mine[:, :width], theirs[:, :width], mine[:, width:], theirs[:, width:]]
-    odd_x, odd_y = slab_x() == 1, slab_y() == 1
-    blocks = [jnp.where(odd_x, blocks[j ^ 1], blocks[j]) for j in range(4)]
-    blocks = [jnp.where(odd_y, blocks[j ^ 2], blocks[j]) for j in range(4)]
-    out[...] = jnp.concatenate(blocks, axis=1).astype(out.dtype)
+    here = lax.div(lax.broadcasted_iota(jnp.int32, (voxels, width), 1), width // 2) == slab_x()
+    near, far = jnp.where(here, mine, theirs), jnp.where(here, theirs, mine)
+    near_at = pl.multiple_of(slab_y() * width, width)
+    far_at = pl.multiple_of((1 - slab_y()) * width, width)
+    out[:, pl.ds(near_at, width)] = near.astype(out.dtype)
+    out[:, pl.ds(far_at, width)] = pltpu.roll(far, width // 2, 1).astype(out.dtype)
 
 
 def four_slabs(volume, weights):
@@ -180,11 +185,12 @@
         return s, c + (1 if c % 2 else -1)
 
     across = send(volume, across_x)
-    piece = like((width // 4, depth_of_sum), weights)
+    early = EARLY_TAPS * channels
+    pieces = [like((width // 2, early), weights), like((width // 2, depth_of_sum - early), weights)]
     first, second, block = call(
         fetch,
         [pltpu.with_memory_space_constraint(x, pltpu.HBM) for x in (volume, kernel_rows)],
-        [piece, piece, like(volume.shape, volume)],
+        [*pieces, like(volume.shape, volume)],
         places=[pl.BlockSpec(memory_space=pltpu.HBM)] * 2,
         scratch=[pltpu.SemaphoreType.DMA((3,))],
     )
@@ -199,19 +205,19 @@
     outer, here_first = lax.optimization_barrier((outer, here_first))
     to_core, to_chip = call(outer_edges, (outer,), [outer_edge, outer_edge], 3000000000)
     outer_core, outer_chip = send(to_core, other_core), send(to_chip, next_chip)
+    there_first = send(here_first, other_core)
+    here_second, outer_core = lax.optimization_barrier((here_second, outer_core))
+    there_second = send(here_second, other_core)
     (lines,) = call(
         extend,
         (block, across, outer, from_core, from_chip, outer_core, outer_chip),
         [like((2 * depth + 2, rows + 2, cols, channels), volume)],
+        3000000000,
     )
     work = 2 * voxels * depth_of_sum * width
-    (near_sums,) = call(near, (lines, kernel_rows), [like((voxels, width), volume)], work)
-    there_first = send(here_first, other_core)
-    here_second, held = lax.optimization_barrier((here_second, lines))
-    there_second = send(here_second, other_core)
     pieces = (here_first, here_second, there_first, there_second)
     both = like((voxels, 2 * width), volume)
-    (sent,) = call(back, (lines, near_sums, *pieces), [both], work)
+    (sent,) = call(back, (lines, kernel_rows, *pieces), [both], 2 * work)
     returned = send(sent, across_x)
     (mine,) = call(kept, (lines, kernel_rows, *pieces), [both], 2 * work)
     (out,) = call(join, (mine, returned), [like((voxels, 4 * width), volume)])
@@ -229,7 +235,7 @@
 
 
 def whole(lines, kernel_rows, out):
-    out[...] = convolve(lines, 0, lines.shape[0] - 2, [kernel_rows]).astype(out.dtype)
+    out[...] = convolve(lines, 0, lines.shape[0] - 2, kernel_rows, ()).astype(out.dtype)
 
 
 def any_slabs(volume, weights):

time: 25.7 us -> 25.2 us (0.981)
  starting transfers between devices: 14.2 us -> 11 us
  waiting for transfers between devices: 6.97 us -> 10 us
  Pallas kernels: 4.29 us -> 3.99 us
    ppermute x11, starting transfers between devices: 14.2 us -> 11 us  [send(): return lax.ppermute(array, BOTH, pairs)]
    ppermute x11, waiting for transfers between devices: 6.97 us -> 10 us  [send(): return lax.ppermute(array, BOTH, pairs)]
    pallas_call x9 -> x8, Pallas kernels: 4.29 us -> 3.99 us  [call(): pl.pallas_call(kernel, out_shape=outs, in_specs=places or [vmem] * len(op...]
  transfers between devices with their start and end apart: 11 -> 11, of which waited for: 5 -> 7; matrix products, arithmetic and copies ran while one was open for 0% -> 0% of each run, Pallas kernels for 11% -> 9%
where the time goes in v3:
time: 25.2 us; the launch traced here: 25 us
  starting transfers between devices  11 us (44%)
  waiting for transfers between devices  10 us (40%)
  Pallas kernels  3.99 us (16%)
    ppermute x11, starting transfers between devices, send(): return lax.ppermute(array, BOTH, pairs)  11 us
    ppermute x11, waiting for transfers between devices, send(): return lax.ppermute(array, BOTH, pairs)  10 us
    pallas_call x8, Pallas kernels, call(): pl.pallas_call(kernel, out_shape=outs, in_specs=places or [vmem] * len(op...  3.99 us
  transfers between devices with their start and end apart: 11, of which 7 were waited for; matrix products, arithmetic and copies ran while one was open for 0% of the time, Pallas kernels for 9%

profile of v3, /device:TPU:0, one launch (start us, length us, event | category | flops | bytes accessed | tf_op | source)
XLA Modules:
  0.0 25.0 jit_solution(761332278888689366)
XLA Ops:
  0.0 2.9 %collective-permute-start = (bf16[2,2,64,256]{3,2,1,0:T(8,128)(2,1)}, bf16[2,2,64,256]{3,2,1,0:T(8,128)(2,1)S(1)}, u32[]{:S(2)}, u32[]{:S(2)}) collective-permute-start(bf16[2,2,64,256]{3,2,1,0:T(8,128)(2,1)} %volume.1), channel_id=1, source_target_pairs={{0,8},{1,9},{2,10},{3,11},{4,12},{5,13},{6,14},{7,15},{8,0},{9,1},... | collective-permute-start | bytes 393224 | tf_op jit(solution)/shard_map/ppermute | solution.py:173
  2.9 1.1 %fetch.1 = (bf16[32,2304]{1,0:T(8,128)(2,1)S(1)}, bf16[32,4608]{1,0:T(8,128)(2,1)S(1)}, bf16[2,2,64,256]{3,2,1,0:T(8,128)(2,1)S(1)}) custom-call(bf16[2,2,64,256]{3,2,1,0:T(8,128)(2,1)} %volume.1, bf16[64,6912]{1,0:T(8,128)(2,1)} %bitcast.2), custom_call_target="tpu_custom_call" | custom-call | bytes 1589248 | tf_op jit(solution)/shard_map/fetch/pallas_call | solution.py:16
  4.0 1.6 %collective-permute-start.2 = (bf16[32,2304]{1,0:T(8,128)(2,1)S(1)}, bf16[32,2304]{1,0:T(8,128)(2,1)S(1)}, u32[]{:S(2)}, u32[]{:S(2)}) collective-permute-start(bf16[32,2304]{1,0:T(8,128)(2,1)S(1)} %get-tuple-element.21), channel_id=1, source_target_pairs={{0,16},{1,17},{2,18},{3,19},{4,20},{5,21},{6,22},{7,23},{8,24},{9,... | collective-permute-start | bytes 442376 | tf_op jit(solution)/shard_map/ppermute | solution.py:173
  5.6 1.0 %collective-permute-done.across = bf16[2,2,64,256]{3,2,1,0:T(8,128)(2,1)S(1)} collective-permute-done((bf16[2,2,64,256]{3,2,1,0:T(8,128)(2,1)}, bf16[2,2,64,256]{3,2,1,0:T(8,128)(2,1)S(1)}, u32[]{:S(2)}, u32[]{:S(2)}) %collective-permute-start) | collective-permute-done | bytes 131104 | tf_op jit(solution)/shard_map/ppermute | solution.py:173
  6.7 1.8 %collective-permute-start.1 = (bf16[1,2,64,256]{3,2,1,0:T(8,128)(2,1)S(1)}, bf16[1,2,64,256]{3,2,1,0:T(8,128)(2,1)S(1)}, u32[]{:S(2)}, u32[]{:S(2)}) collective-permute-start(bf16[1,2,64,256]{3,2,1,0:T(8,128)(2,1)S(1)} %border.1), channel_id=1, source_target_pairs={{0,16},{1,17},{2,18},{3,19},{4,20},{5,21},{6,22},{7,23},{8,24},{9,... | collective-permute-start | bytes 196616 | tf_op jit(solution)/shard_map/ppermute | solution.py:173
  8.5 0.3 %collective-permute-start.5 = (bf16[32,4608]{1,0:T(8,128)(2,1)S(1)}, bf16[32,4608]{1,0:T(8,128)(2,1)S(1)}, u32[]{:S(2)}, u32[]{:S(2)}) collective-permute-start(bf16[32,4608]{1,0:T(8,128)(2,1)S(1)} %get-tuple-element.25), channel_id=1, source_target_pairs={{0,16},{1,17},{2,18},{3,19},{4,20},{5,21},{6,22},{7,23},{8,24},{9,... | collective-permute-start | bytes 884744 | tf_op jit(solution)/shard_map/ppermute | solution.py:173
  8.8 0.0 collective-permute-start.3
  8.8 0.7 %collective-permute-start.4 = (bf16[4,1,64,256]{3,2,1,0:T(8,128)(2,1)S(1)}, bf16[4,1,64,256]{3,2,1,0:T(8,128)(2,1)S(1)}, u32[]{:S(2)}, u32[]{:S(2)}) collective-permute-start(bf16[4,1,64,256]{3,2,1,0:T(8,128)(2,1)S(1)} %get-tuple-element.24), channel_id=1, source_target_pairs={{1,2},{2,1},{3,4},{4,3},{5,6},{6,5},{9,10},{10,9},{11,12},{12,11},... | collective-permute-start | bytes 393224 | tf_op jit(solution)/shard_map/ppermute | solution.py:173
  9.5 0.7 %collective-permute-done.2.refs_0_ = bf16[32,2304]{1,0:T(8,128)(2,1)S(1)} collective-permute-done((bf16[32,2304]{1,0:T(8,128)(2,1)S(1)}, bf16[32,2304]{1,0:T(8,128)(2,1)S(1)}, u32[]{:S(2)}, u32[]{:S(2)}) %collective-permute-start.2) | collective-permute-done | bytes 147488 | tf_op jit(solution)/shard_map/ppermute | solution.py:173
  10.2 1.5 %collective-permute-done.1.outer = bf16[1,2,64,256]{3,2,1,0:T(8,128)(2,1)S(1)} collective-permute-done((bf16[1,2,64,256]{3,2,1,0:T(8,128)(2,1)S(1)}, bf16[1,2,64,256]{3,2,1,0:T(8,128)(2,1)S(1)}, u32[]{:S(2)}, u32[]{:S(2)}) %collective-permute-start.1) | collective-permute-done | bytes 65568 | tf_op jit(solution)/shard_map/ppermute | solution.py:173
  11.8 1.0 %collective-permute-start.6 = (bf16[1,1,64,256]{3,2,1,0:T(8,128)(2,1)S(1)}, bf16[1,1,64,256]{3,2,1,0:T(8,128)(2,1)S(1)}, u32[]{:S(2)}, u32[]{:S(2)}) collective-permute-start(bf16[1,1,64,256]{3,2,1,0:T(8,128)(2,1)S(1)} %get-tuple-element.26), channel_id=1, source_target_pairs={{0,1},{1,0},{2,3},{3,2},{4,5},{5,4},{6,7},{7,6},{8,9},{9,8},{10,11... | collective-permute-start | bytes 98312 | tf_op jit(solution)/shard_map/ppermute | solution.py:173
  12.8 0.0 copy-start
  12.8 0.8 %collective-permute-start.7 = (bf16[1,1,64,256]{3,2,1,0:T(8,128)(2,1)S(1)}, bf16[1,1,64,256]{3,2,1,0:T(8,128)(2,1)S(1)}, u32[]{:S(2)}, u32[]{:S(2)}) collective-permute-start(bf16[1,1,64,256]{3,2,1,0:T(8,128)(2,1)S(1)} %get-tuple-element.28), channel_id=1, source_target_pairs={{1,2},{2,1},{3,4},{4,3},{5,6},{6,5},{9,10},{10,9},{11,12},{12,11},... | collective-permute-start | bytes 98312 | tf_op jit(solution)/shard_map/ppermute | solution.py:173
  13.6 0.1 collective-permute-done.6.outer_core
  13.7 3.5 %collective-permute-done.5.refs_1_ = bf16[32,4608]{1,0:T(8,128)(2,1)S(1)} collective-permute-done((bf16[32,4608]{1,0:T(8,128)(2,1)S(1)}, bf16[32,4608]{1,0:T(8,128)(2,1)S(1)}, u32[]{:S(2)}, u32[]{:S(2)}) %collective-permute-start.5) | collective-permute-done | bytes 294944 | tf_op jit(solution)/shard_map/ppermute | solution.py:173
  17.1 0.0 collective-permute-start.9
  17.1 0.5 %collective-permute-start.8 = (bf16[32,2304]{1,0:T(8,128)(2,1)S(1)}, bf16[32,2304]{1,0:T(8,128)(2,1)S(1)}, u32[]{:S(2)}, u32[]{:S(2)}) collective-permute-start(bf16[32,2304]{1,0:T(8,128)(2,1)S(1)} %collective-permute-done.2.refs_0_), channel_id=1, source_target_pairs={{0,1},{1,0},{2,3},{3,2},{4,5},{5,4},{6,7},{7,6},{8,9},{9,8},{10,11... | collective-permute-start | bytes 442376 | tf_op jit(solution)/shard_map/ppermute | solution.py:173
  17.6 0.0 collective-permute-done.7.outer_chip
  17.6 0.0 collective-permute-done.3.from_core
  17.7 0.0 collective-permute-done.4.from_chip
  17.7 0.1 extend.1.lines
  17.7 1.2 %collective-permute-done.8.refs_2_ = bf16[32,2304]{1,0:T(8,128)(2,1)S(1)} collective-permute-done((bf16[32,2304]{1,0:T(8,128)(2,1)S(1)}, bf16[32,2304]{1,0:T(8,128)(2,1)S(1)}, u32[]{:S(2)}, u32[]{:S(2)}) %collective-permute-start.8) | collective-permute-done | bytes 147488 | tf_op jit(solution)/shard_map/ppermute | solution.py:173
  18.9 0.0 collective-permute-done.9.refs_3_
  18.9 0.0 copy-done
  18.9 1.0 %back.1 = bf16[256,128]{1,0:T(8,128)(2,1)S(1)} custom-call(bf16[6,4,64,256]{3,2,1,0:T(8,128)(2,1)S(1)} %extend.1.lines, bf16[64,6912]{1,0:T(8,128)(2,1)S(1)} %bitcast.3, bf16[32,2304]{1,0:T(8,128)(2,1)S(1)} %collective-permute-done.2.refs_0_, bf16[32,4608]{1,0:T(8,128)(2,1)S(1)} %collective-permute-done.5.refs_1_, ...), custom_call_target="tpu_custom_call" | custom-call | flops 452984832 | bytes 2621440 | tf_op jit(solution)/shard_map/back/pallas_call | solution.py:16
  20.0 1.3 %collective-permute-start.10 = (bf16[256,128]{1,0:T(8,128)(2,1)S(1)}, bf16[256,128]{1,0:T(8,128)(2,1)S(1)}, u32[]{:S(2)}, u32[]{:S(2)}) collective-permute-start(bf16[256,128]{1,0:T(8,128)(2,1)S(1)} %back.1), channel_id=1, source_target_pairs={{0,8},{1,9},{2,10},{3,11},{4,12},{5,13},{6,14},{7,15},{8,0},{9,1},... | collective-permute-start | bytes 196616 | tf_op jit(solution)/shard_map/ppermute | solution.py:173
  21.3 1.0 %kept.1.kept_sums = bf16[256,128]{1,0:T(8,128)(2,1)S(1)} custom-call(bf16[6,4,64,256]{3,2,1,0:T(8,128)(2,1)S(1)} %extend.1.lines, bf16[64,6912]{1,0:T(8,128)(2,1)S(1)} %bitcast.4, bf16[32,2304]{1,0:T(8,128)(2,1)S(1)} %collective-permute-done.2.refs_0_, bf16[32,4608]{1,0:T(8,128)(2,1)S(1)} %collective-permute-done.5.refs_1_, ...), custom_call_target="tpu_custom_call" | custom-call | flops 452984832 | bytes 2621440 | tf_op jit(solution)/shard_map/kept/pallas_call | solution.py:16
  22.3 2.0 %collective-permute-done.10.returned = bf16[256,128]{1,0:T(8,128)(2,1)S(1)} collective-permute-done((bf16[256,128]{1,0:T(8,128)(2,1)S(1)}, bf16[256,128]{1,0:T(8,128)(2,1)S(1)}, u32[]{:S(2)}, u32[]{:S(2)}) %collective-permute-start.10) | collective-permute-done | bytes 65568 | tf_op jit(solution)/shard_map/ppermute | solution.py:173
  24.3 0.8 %join.1 = bf16[256,256]{1,0:T(8,128)(2,1)} custom-call(bf16[256,128]{1,0:T(8,128)(2,1)S(1)} %kept.1.kept_sums, bf16[256,128]{1,0:T(8,128)(2,1)S(1)} %collective-permute-done.10.returned), custom_call_target="tpu_custom_call" | custom-call | bytes 262144 | tf_op jit(solution)/shard_map/join/pallas_call | solution.py:16
  (3 shorter events, 0.0 us)
Async XLA Ops:
  0.0 6.6 %collective-permute-start = (bf16[2,2,64,256]{3,2,1,0:T(8,128)(2,1)}, bf16[2,2,64,256]{3,2,1,0:T(8,128)(2,1)S(1)}, u32[]{:S(2)}, u32[]{:S(2)}) collective-permute-start(bf16[2,2,64,256]{3,2,1,0:T(8,128)(2,1)} %volume.1), channel_id=1, source_target_pairs={{0,8},{1,9},{2,10},{3,11},{4,12},{5,13},{6,14},{7,15},{8,0},{9,1},... | collective-permute-start | bytes 393224 | tf_op jit(solution)/shard_map/ppermute | solution.py:173
  4.0 6.2 %collective-permute-start.2 = (bf16[32,2304]{1,0:T(8,128)(2,1)S(1)}, bf16[32,2304]{1,0:T(8,128)(2,1)S(1)}, u32[]{:S(2)}, u32[]{:S(2)}) collective-permute-start(bf16[32,2304]{1,0:T(8,128)(2,1)S(1)} %get-tuple-element.21), channel_id=1, source_target_pairs={{0,16},{1,17},{2,18},{3,19},{4,20},{5,21},{6,22},{7,23},{8,24},{9,... | collective-permute-start | bytes 442376 | tf_op jit(solution)/shard_map/ppermute | solution.py:173
  6.7 5.1 %collective-permute-start.1 = (bf16[1,2,64,256]{3,2,1,0:T(8,128)(2,1)S(1)}, bf16[1,2,64,256]{3,2,1,0:T(8,128)(2,1)S(1)}, u32[]{:S(2)}, u32[]{:S(2)}) collective-permute-start(bf16[1,2,64,256]{3,2,1,0:T(8,128)(2,1)S(1)} %border.1), channel_id=1, source_target_pairs={{0,16},{1,17},{2,18},{3,19},{4,20},{5,21},{6,22},{7,23},{8,24},{9,... | collective-permute-start | bytes 196616 | tf_op jit(solution)/shard_map/ppermute | solution.py:173
  8.5 8.6 %collective-permute-start.5 = (bf16[32,4608]{1,0:T(8,128)(2,1)S(1)}, bf16[32,4608]{1,0:T(8,128)(2,1)S(1)}, u32[]{:S(2)}, u32[]{:S(2)}) collective-permute-start(bf16[32,4608]{1,0:T(8,128)(2,1)S(1)} %get-tuple-element.25), channel_id=1, source_target_pairs={{0,16},{1,17},{2,18},{3,19},{4,20},{5,21},{6,22},{7,23},{8,24},{9,... | collective-permute-start | bytes 884744 | tf_op jit(solution)/shard_map/ppermute | solution.py:173
  8.8 8.8 %collective-permute-start.3 = (bf16[4,1,64,256]{3,2,1,0:T(8,128)(2,1)S(1)}, bf16[4,1,64,256]{3,2,1,0:T(8,128)(2,1)S(1)}, u32[]{:S(2)}, u32[]{:S(2)}) collective-permute-start(bf16[4,1,64,256]{3,2,1,0:T(8,128)(2,1)S(1)} %get-tuple-element.23), channel_id=1, source_target_pairs={{0,1},{1,0},{2,3},{3,2},{4,5},{5,4},{6,7},{7,6},{8,9},{9,8},{10,11... | collective-permute-start | bytes 393224 | tf_op jit(solution)/shard_map/ppermute | solution.py:173
  8.8 8.8 %collective-permute-start.4 = (bf16[4,1,64,256]{3,2,1,0:T(8,128)(2,1)S(1)}, bf16[4,1,64,256]{3,2,1,0:T(8,128)(2,1)S(1)}, u32[]{:S(2)}, u32[]{:S(2)}) collective-permute-start(bf16[4,1,64,256]{3,2,1,0:T(8,128)(2,1)S(1)} %get-tuple-element.24), channel_id=1, source_target_pairs={{1,2},{2,1},{3,4},{4,3},{5,6},{6,5},{9,10},{10,9},{11,12},{12,11},... | collective-permute-start | bytes 393224 | tf_op jit(solution)/shard_map/ppermute | solution.py:173
  11.8 1.9 %collective-permute-start.6 = (bf16[1,1,64,256]{3,2,1,0:T(8,128)(2,1)S(1)}, bf16[1,1,64,256]{3,2,1,0:T(8,128)(2,1)S(1)}, u32[]{:S(2)}, u32[]{:S(2)}) collective-permute-start(bf16[1,1,64,256]{3,2,1,0:T(8,128)(2,1)S(1)} %get-tuple-element.26), channel_id=1, source_target_pairs={{0,1},{1,0},{2,3},{3,2},{4,5},{5,4},{6,7},{7,6},{8,9},{9,8},{10,11... | collective-permute-start | bytes 98312 | tf_op jit(solution)/shard_map/ppermute | solution.py:173
  12.8 6.1 %copy-start = (bf16[6912,64]{0,1:T(8,128)(2,1)S(1)}, bf16[6912,64]{0,1:T(8,128)(2,1)}, u32[]{:S(2)}) copy-start(bf16[6912,64]{0,1:T(8,128)(2,1)} %param.3) | copy-start | bytes 2654212
  12.8 4.8 %collective-permute-start.7 = (bf16[1,1,64,256]{3,2,1,0:T(8,128)(2,1)S(1)}, bf16[1,1,64,256]{3,2,1,0:T(8,128)(2,1)S(1)}, u32[]{:S(2)}, u32[]{:S(2)}) collective-permute-start(bf16[1,1,64,256]{3,2,1,0:T(8,128)(2,1)S(1)} %get-tuple-element.28), channel_id=1, source_target_pairs={{1,2},{2,1},{3,4},{4,3},{5,6},{6,5},{9,10},{10,9},{11,12},{12,11},... | collective-permute-start | bytes 98312 | tf_op jit(solution)/shard_map/ppermute | solution.py:173
  17.1 1.8 %collective-permute-start.9 = (bf16[32,4608]{1,0:T(8,128)(2,1)S(1)}, bf16[32,4608]{1,0:T(8,128)(2,1)S(1)}, u32[]{:S(2)}, u32[]{:S(2)}) collective-permute-start(bf16[32,4608]{1,0:T(8,128)(2,1)S(1)} %collective-permute-done.5.refs_1_), channel_id=1, source_target_pairs={{0,1},{1,0},{2,3},{3,2},{4,5},{5,4},{6,7},{7,6},{8,9},{9,8},{10,11... | collective-permute-start | bytes 884744 | tf_op jit(solution)/shard_map/ppermute | solution.py:173
  17.1 1.8 %collective-permute-start.8 = (bf16[32,2304]{1,0:T(8,128)(2,1)S(1)}, bf16[32,2304]{1,0:T(8,128)(2,1)S(1)}, u32[]{:S(2)}, u32[]{:S(2)}) collective-permute-start(bf16[32,2304]{1,0:T(8,128)(2,1)S(1)} %collective-permute-done.2.refs_0_), channel_id=1, source_target_pairs={{0,1},{1,0},{2,3},{3,2},{4,5},{5,4},{6,7},{7,6},{8,9},{9,8},{10,11... | collective-permute-start | bytes 442376 | tf_op jit(solution)/shard_map/ppermute | solution.py:173
  20.0 4.3 %collective-permute-start.10 = (bf16[256,128]{1,0:T(8,128)(2,1)S(1)}, bf16[256,128]{1,0:T(8,128)(2,1)S(1)}, u32[]{:S(2)}, u32[]{:S(2)}) collective-permute-start(bf16[256,128]{1,0:T(8,128)(2,1)S(1)} %back.1), channel_id=1, source_target_pairs={{0,8},{1,9},{2,10},{3,11},{4,12},{5,13},{6,14},{7,15},{8,0},{9,1},... | collective-permute-start | bytes 196616 | tf_op jit(solution)/shard_map/ppermute | solution.py:173

commit v4 on v3

--- a/solution.py
+++ b/solution.py
@@ -97,25 +97,21 @@
     lines[empty] = jnp.zeros(lines.shape[1:], lines.dtype)
 
 
-def convolve(lines, base, depth, kernel_rows, pieces):
+def convolve(lines, base, depth, groups):
     rows, cols, channels = lines.shape[1] - 2, *lines.shape[2:]
     voxels = depth * rows * cols
     total = None
-    for tap in range(0, 27, 3):
-        a, b = tap // 9, tap // 3 % 3
-        moved = lines[pl.ds(base + a, depth), b : b + rows].reshape(voxels, channels)
-        stack = []
-        for e in range(3):
-            at = (tap + e) * channels
-            stack.append(kernel_rows[:, at : at + channels])
-            for first, second in pieces:
-                early = first.shape[1]
-                array, start = (first, at) if at < early else (second, at - early)
-                stack.append(array[:, start : start + channels])
-        term = lax.dot_general(
-            moved, jnp.concatenate(stack, axis=0), (((1,), (1,)), ((), ())), preferred_element_type=jnp.float32
-        )
-        total = term if total is None else total + term
+    for taps, arrays in groups:
+        for tap in taps[::3]:
+            a, b, start = tap // 9, tap // 3 % 3, (tap - taps[0]) * channels
+            moved = lines[pl.ds(base + a, depth), b : b + rows].reshape(voxels, channels)
+            stack = [
+                array[:, start + e * channels : start + (e + 1) * channels] for e in range(3) for array in arrays
+            ]
+            term = lax.dot_general(
+                moved, jnp.concatenate(stack, axis=0), (((1,), (1,)), ((), ())), preferred_element_type=jnp.float32
+            )
+            total = term if total is None else total + term
     width = total.shape[1] // 3
     col = lax.rem(lax.broadcasted_iota(jnp.int32, (voxels, width), 0), cols)
     before = jnp.where(col == 0, 0.0, pltpu.roll(total[:, :width], 1, 0))
@@ -129,24 +125,34 @@
     return jnp.where(core_parity() == 0, sums, swapped)
 
 
-def both_slabs(lines, base, kernel_rows, pieces, out):
-    width = kernel_rows.shape[0]
-    here_first, here_second, there_first, there_second = pieces
-    pieces = ((here_first, here_second), (there_first, there_second))
-    sums = convolve(lines, base, (lines.shape[0] - 2) // 2, kernel_rows, pieces)
-    near, far = sums[:, :width], ordered(sums[:, width:])
-    even = jnp.concatenate([near, far], axis=1)
-    out[...] = jnp.where(slab_x() == 0, even, jnp.concatenate([far, near], axis=1)).astype(out.dtype)
-
-
-def back(lines, kernel_rows, *refs):
-    *pieces, out = refs
-    both_slabs(lines, (lines.shape[0] - 2) // 2 * (1 - slab_x()), kernel_rows, pieces, out)
-
-
-def kept(lines, kernel_rows, *refs):
-    *pieces, out = refs
-    both_slabs(lines, (lines.shape[0] - 2) // 2 * slab_x(), kernel_rows, pieces, out)
+def pair_depth(lines):
+    return (lines.shape[0] - 2) // 2
+
+
+def arranged(near, far):
+    far = ordered(far)
+    return jnp.where(slab_x() == 0, jnp.concatenate([near, far], axis=1), jnp.concatenate([far, near], axis=1))
+
+
+def back_early(lines, kernel_rows, here, there, near, far):
+    depth, early = pair_depth(lines), here.shape[1] // lines.shape[3]
+    base = depth * (1 - slab_x())
+    near[...] = convolve(lines, base, depth, [(range(27), [kernel_rows])])
+    far[...] = convolve(lines, base, depth, [(range(early), [here, there])])
+
+
+def back(lines, near, far, here, there, out):
+    depth, late = pair_depth(lines), here.shape[1] // lines.shape[3]
+    rest = convolve(lines, depth * (1 - slab_x()), depth, [(range(27 - late, 27), [here, there])])
+    out[...] = arranged(near[...], far[...] + rest).astype(out.dtype)
+
+
+def kept(lines, kernel_rows, here_first, there_first, here_second, there_second, out):
+    depth, early = pair_depth(lines), here_first.shape[1] // lines.shape[3]
+    base, width = depth * slab_x(), kernel_rows.shape[0]
+    near = convolve(lines, base, depth, [(range(27), [kernel_rows])])
+    groups = [(range(early), [here_first, there_first]), (range(early, 27), [here_second, there_second])]
+    out[...] = arranged(near, convolve(lines, base, depth, groups)).astype(out.dtype)
 
 
 def join(kept_sums, returned, out):
@@ -200,11 +206,12 @@
     outer = send(plane, across_y)
     here_second = send(second, across_y)
     edge, outer_edge = like((2 * depth, 1, cols, channels), volume), like((1, 1, cols, channels), volume)
-    to_core, to_chip = call(edges, (block, across), [edge, edge])
+    to_core, to_chip = call(edges, (block, across), [edge, edge], 5000000000)
     from_core, from_chip = send(to_core, other_core), send(to_chip, next_chip)
     outer, here_first = lax.optimization_barrier((outer, here_first))
-    to_core, to_chip = call(outer_edges, (outer,), [outer_edge, outer_edge], 3000000000)
+    to_core, to_chip = call(outer_edges, (outer,), [outer_edge, outer_edge], 8000000000)
     outer_core, outer_chip = send(to_core, other_core), send(to_chip, next_chip)
+    here_first, to_chip_held = lax.optimization_barrier((here_first, outer_core))
     there_first = send(here_first, other_core)
     here_second, outer_core = lax.optimization_barrier((here_second, outer_core))
     there_second = send(here_second, other_core)
@@ -215,11 +222,13 @@
         3000000000,
     )
     work = 2 * voxels * depth_of_sum * width
-    pieces = (here_first, here_second, there_first, there_second)
-    both = like((voxels, 2 * width), volume)
-    (sent,) = call(back, (lines, kernel_rows, *pieces), [both], 2 * work)
+    both, sums = like((voxels, 2 * width), volume), jax.ShapeDtypeStruct((voxels, width), jnp.float32)
+    near, far = call(back_early, (lines, kernel_rows, here_first, there_first), [sums, sums], work)
+    (sent,) = call(back, (lines, near, far, here_second, there_second), [both], work)
     returned = send(sent, across_x)
-    (mine,) = call(kept, (lines, kernel_rows, *pieces), [both], 2 * work)
+    (mine,) = call(
+        kept, (lines, kernel_rows, here_first, there_first, here_second, there_second), [both], 2 * work
+    )
     (out,) = call(join, (mine, returned), [like((voxels, 4 * width), volume)])
     return out.reshape(volume.shape)
 
@@ -235,7 +244,7 @@
 
 
 def whole(lines, kernel_rows, out):
-    out[...] = convolve(lines, 0, lines.shape[0] - 2, kernel_rows, ()).astype(out.dtype)
+    out[...] = convolve(lines, 0, lines.shape[0] - 2, [(range(27), [kernel_rows])]).astype(out.dtype)
 
 
 def any_slabs(volume, weights):

time: 25.2 us -> 24.6 us (0.976)
  waiting for transfers between devices: 10 us -> 6.72 us
  starting transfers between devices: 11 us -> 13.4 us
    ppermute x11, waiting for transfers between devices: 10 us -> 6.72 us  [send(): return lax.ppermute(array, BOTH, pairs)]
    ppermute x11, starting transfers between devices: 11 us -> 13.4 us  [send(): return lax.ppermute(array, BOTH, pairs)]
    pallas_call x8 -> x9, Pallas kernels: 3.99 us -> 4.2 us  [call(): pl.pallas_call(kernel, out_shape=outs, in_specs=places or [vmem] * len(op...]
  transfers between devices with their start and end apart: 11 -> 11, of which waited for: 7 -> 8; matrix products, arithmetic and copies ran while one was open for 0% -> 0% of each run, Pallas kernels for 9% -> 12%
where the time goes in v4:
time: 24.6 us; the launch traced here: 24.4 us
  starting transfers between devices  13.4 us (54%)
  waiting for transfers between devices  6.72 us (27%)
  Pallas kernels  4.2 us (17%)
    ppermute x11, starting transfers between devices, send(): return lax.ppermute(array, BOTH, pairs)  13.4 us
    ppermute x11, waiting for transfers between devices, send(): return lax.ppermute(array, BOTH, pairs)  6.72 us
    pallas_call x9, Pallas kernels, call(): pl.pallas_call(kernel, out_shape=outs, in_specs=places or [vmem] * len(op...  4.2 us
  transfers between devices with their start and end apart: 11, of which 8 were waited for; matrix products, arithmetic and copies ran while one was open for 0% of the time, Pallas kernels for 12%

profile of v4, /device:TPU:0, one launch (start us, length us, event | category | flops | bytes accessed | tf_op | source)
XLA Modules:
  0.0 24.4 jit_solution(14822969217011570552)
XLA Ops:
  0.0 2.9 %collective-permute-start = (bf16[2,2,64,256]{3,2,1,0:T(8,128)(2,1)}, bf16[2,2,64,256]{3,2,1,0:T(8,128)(2,1)S(1)}, u32[]{:S(2)}, u32[]{:S(2)}) collective-permute-start(bf16[2,2,64,256]{3,2,1,0:T(8,128)(2,1)} %volume.1), channel_id=1, source_target_pairs={{0,8},{1,9},{2,10},{3,11},{4,12},{5,13},{6,14},{7,15},{8,0},{9,1},... | collective-permute-start | bytes 393224 | tf_op jit(solution)/shard_map/ppermute | solution.py:179
  2.9 1.1 %fetch.1 = (bf16[32,2304]{1,0:T(8,128)(2,1)S(1)}, bf16[32,4608]{1,0:T(8,128)(2,1)S(1)}, bf16[2,2,64,256]{3,2,1,0:T(8,128)(2,1)S(1)}) custom-call(bf16[2,2,64,256]{3,2,1,0:T(8,128)(2,1)} %volume.1, bf16[64,6912]{1,0:T(8,128)(2,1)} %bitcast.2), custom_call_target="tpu_custom_call" | custom-call | bytes 1589248 | tf_op jit(solution)/shard_map/fetch/pallas_call | solution.py:16
  4.0 1.6 %collective-permute-start.2 = (bf16[32,2304]{1,0:T(8,128)(2,1)S(1)}, bf16[32,2304]{1,0:T(8,128)(2,1)S(1)}, u32[]{:S(2)}, u32[]{:S(2)}) collective-permute-start(bf16[32,2304]{1,0:T(8,128)(2,1)S(1)} %get-tuple-element.24), channel_id=1, source_target_pairs={{0,16},{1,17},{2,18},{3,19},{4,20},{5,21},{6,22},{7,23},{8,24},{9,... | collective-permute-start | bytes 442376 | tf_op jit(solution)/shard_map/ppermute | solution.py:179
  5.6 1.0 %collective-permute-done.across = bf16[2,2,64,256]{3,2,1,0:T(8,128)(2,1)S(1)} collective-permute-done((bf16[2,2,64,256]{3,2,1,0:T(8,128)(2,1)}, bf16[2,2,64,256]{3,2,1,0:T(8,128)(2,1)S(1)}, u32[]{:S(2)}, u32[]{:S(2)}) %collective-permute-start) | collective-permute-done | bytes 131104 | tf_op jit(solution)/shard_map/ppermute | solution.py:179
  6.7 1.8 %collective-permute-start.1 = (bf16[1,2,64,256]{3,2,1,0:T(8,128)(2,1)S(1)}, bf16[1,2,64,256]{3,2,1,0:T(8,128)(2,1)S(1)}, u32[]{:S(2)}, u32[]{:S(2)}) collective-permute-start(bf16[1,2,64,256]{3,2,1,0:T(8,128)(2,1)S(1)} %border.1), channel_id=1, source_target_pairs={{0,16},{1,17},{2,18},{3,19},{4,20},{5,21},{6,22},{7,23},{8,24},{9,... | collective-permute-start | bytes 196616 | tf_op jit(solution)/shard_map/ppermute | solution.py:179
  8.5 0.3 %collective-permute-start.5 = (bf16[32,4608]{1,0:T(8,128)(2,1)S(1)}, bf16[32,4608]{1,0:T(8,128)(2,1)S(1)}, u32[]{:S(2)}, u32[]{:S(2)}) collective-permute-start(bf16[32,4608]{1,0:T(8,128)(2,1)S(1)} %get-tuple-element.28), channel_id=1, source_target_pairs={{0,16},{1,17},{2,18},{3,19},{4,20},{5,21},{6,22},{7,23},{8,24},{9,... | collective-permute-start | bytes 884744 | tf_op jit(solution)/shard_map/ppermute | solution.py:179
  8.8 0.0 collective-permute-start.3
  8.8 0.7 %collective-permute-start.4 = (bf16[4,1,64,256]{3,2,1,0:T(8,128)(2,1)S(1)}, bf16[4,1,64,256]{3,2,1,0:T(8,128)(2,1)S(1)}, u32[]{:S(2)}, u32[]{:S(2)}) collective-permute-start(bf16[4,1,64,256]{3,2,1,0:T(8,128)(2,1)S(1)} %get-tuple-element.27), channel_id=1, source_target_pairs={{1,2},{2,1},{3,4},{4,3},{5,6},{6,5},{9,10},{10,9},{11,12},{12,11},... | collective-permute-start | bytes 393224 | tf_op jit(solution)/shard_map/ppermute | solution.py:179
  9.5 0.7 %collective-permute-done.2.here_first.here = bf16[32,2304]{1,0:T(8,128)(2,1)S(1)} collective-permute-done((bf16[32,2304]{1,0:T(8,128)(2,1)S(1)}, bf16[32,2304]{1,0:T(8,128)(2,1)S(1)}, u32[]{:S(2)}, u32[]{:S(2)}) %collective-permute-start.2) | collective-permute-done | bytes 147488 | tf_op jit(solution)/shard_map/ppermute | solution.py:179
  10.2 1.5 %collective-permute-done.1.outer = bf16[1,2,64,256]{3,2,1,0:T(8,128)(2,1)S(1)} collective-permute-done((bf16[1,2,64,256]{3,2,1,0:T(8,128)(2,1)S(1)}, bf16[1,2,64,256]{3,2,1,0:T(8,128)(2,1)S(1)}, u32[]{:S(2)}, u32[]{:S(2)}) %collective-permute-start.1) | collective-permute-done | bytes 65568 | tf_op jit(solution)/shard_map/ppermute | solution.py:179
  11.8 1.0 %collective-permute-start.6 = (bf16[1,1,64,256]{3,2,1,0:T(8,128)(2,1)S(1)}, bf16[1,1,64,256]{3,2,1,0:T(8,128)(2,1)S(1)}, u32[]{:S(2)}, u32[]{:S(2)}) collective-permute-start(bf16[1,1,64,256]{3,2,1,0:T(8,128)(2,1)S(1)} %get-tuple-element.29), channel_id=1, source_target_pairs={{0,1},{1,0},{2,3},{3,2},{4,5},{5,4},{6,7},{7,6},{8,9},{9,8},{10,11... | collective-permute-start | bytes 98312 | tf_op jit(solution)/shard_map/ppermute | solution.py:179
  12.8 0.0 copy-start
  12.8 0.8 %collective-permute-start.7 = (bf16[1,1,64,256]{3,2,1,0:T(8,128)(2,1)S(1)}, bf16[1,1,64,256]{3,2,1,0:T(8,128)(2,1)S(1)}, u32[]{:S(2)}, u32[]{:S(2)}) collective-permute-start(bf16[1,1,64,256]{3,2,1,0:T(8,128)(2,1)S(1)} %get-tuple-element.31), channel_id=1, source_target_pairs={{1,2},{2,1},{3,4},{4,3},{5,6},{6,5},{9,10},{10,9},{11,12},{12,11},... | collective-permute-start | bytes 98312 | tf_op jit(solution)/shard_map/ppermute | solution.py:179
  13.6 0.1 collective-permute-done.6.outer_core
  13.7 2.9 %collective-permute-start.8 = (bf16[32,2304]{1,0:T(8,128)(2,1)S(1)}, bf16[32,2304]{1,0:T(8,128)(2,1)S(1)}, u32[]{:S(2)}, u32[]{:S(2)}) collective-permute-start(bf16[32,2304]{1,0:T(8,128)(2,1)S(1)} %collective-permute-done.2.here_first.here), channel_id=1, source_target_pairs={{0,1},{1,0},{2,3},{3,2},{4,5},{5,4},{6,7},{7,6},{8,9},{9,8},{10,11... | collective-permute-start | bytes 442376 | tf_op jit(solution)/shard_map/ppermute | solution.py:179
  16.6 0.5 %collective-permute-done.5.here_second.here = bf16[32,4608]{1,0:T(8,128)(2,1)S(1)} collective-permute-done((bf16[32,4608]{1,0:T(8,128)(2,1)S(1)}, bf16[32,4608]{1,0:T(8,128)(2,1)S(1)}, u32[]{:S(2)}, u32[]{:S(2)}) %collective-permute-start.5) | collective-permute-done | bytes 294944 | tf_op jit(solution)/shard_map/ppermute | solution.py:179
  17.1 0.0 collective-permute-start.9
  17.1 0.0 collective-permute-done.7.outer_chip
  17.1 0.0 collective-permute-done.3.from_core
  17.1 0.0 collective-permute-done.4.from_chip
  17.2 0.1 extend.1.lines
  17.2 0.4 %collective-permute-done.8.there_first.there = bf16[32,2304]{1,0:T(8,128)(2,1)S(1)} collective-permute-done((bf16[32,2304]{1,0:T(8,128)(2,1)S(1)}, bf16[32,2304]{1,0:T(8,128)(2,1)S(1)}, u32[]{:S(2)}, u32[]{:S(2)}) %collective-permute-start.8) | collective-permute-done | bytes 147488 | tf_op jit(solution)/shard_map/ppermute | solution.py:179
  17.6 0.0 copy-done
  17.6 0.7 %back_early.1 = (f32[256,64]{1,0:T(8,128)S(1)}, f32[256,64]{1,0:T(8,128)S(1)}) custom-call(bf16[6,4,64,256]{3,2,1,0:T(8,128)(2,1)S(1)} %extend.1.lines, bf16[64,6912]{1,0:T(8,128)(2,1)S(1)} %bitcast.3, bf16[32,2304]{1,0:T(8,128)(2,1)S(1)} %collective-permute-done.2.here_first.here, bf16[32,2304]{1,0:T(8,128)(2,1)S(1)} %collective-permute-done.8.there_first.there), custom_call_target="tpu_custom_call" | custom-call | flops 226492416 | bytes 2097152 | tf_op jit(solution)/shard_map/back_early/pallas_call | solution.py:16
  18.3 0.4 %collective-permute-done.9.there_second.there = bf16[32,4608]{1,0:T(8,128)(2,1)S(1)} collective-permute-done((bf16[32,4608]{1,0:T(8,128)(2,1)S(1)}, bf16[32,4608]{1,0:T(8,128)(2,1)S(1)}, u32[]{:S(2)}, u32[]{:S(2)}) %collective-permute-start.9) | collective-permute-done | bytes 294944 | tf_op jit(solution)/shard_map/ppermute | solution.py:179
  18.7 0.6 %back.1 = bf16[256,128]{1,0:T(8,128)(2,1)S(1)} custom-call(bf16[6,4,64,256]{3,2,1,0:T(8,128)(2,1)S(1)} %extend.1.lines, f32[256,64]{1,0:T(8,128)S(1)} %get-tuple-element.35.near, f32[256,64]{1,0:T(8,128)S(1)} %get-tuple-element.36.far, bf16[32,4608]{1,0:T(8,128)(2,1)S(1)} %collective-permute-done.5.here_second.here, ...), custom_call_target="tpu_custom_call" | custom-call | flops 226492416 | bytes 1572864 | tf_op jit(solution)/shard_map/back/pallas_call | solution.py:16
  19.3 1.3 %collective-permute-start.10 = (bf16[256,128]{1,0:T(8,128)(2,1)S(1)}, bf16[256,128]{1,0:T(8,128)(2,1)S(1)}, u32[]{:S(2)}, u32[]{:S(2)}) collective-permute-start(bf16[256,128]{1,0:T(8,128)(2,1)S(1)} %back.1), channel_id=1, source_target_pairs={{0,8},{1,9},{2,10},{3,11},{4,12},{5,13},{6,14},{7,15},{8,0},{9,1},... | collective-permute-start | bytes 196616 | tf_op jit(solution)/shard_map/ppermute | solution.py:179
  20.6 1.0 %kept.1.kept_sums = bf16[256,128]{1,0:T(8,128)(2,1)S(1)} custom-call(bf16[6,4,64,256]{3,2,1,0:T(8,128)(2,1)S(1)} %extend.1.lines, bf16[64,6912]{1,0:T(8,128)(2,1)S(1)} %bitcast.4, bf16[32,2304]{1,0:T(8,128)(2,1)S(1)} %collective-permute-done.2.here_first.here, bf16[32,2304]{1,0:T(8,128)(2,1)S(1)} %collective-permute-done.8.there_first.there, ...), custom_call_target="tpu_custom_call" | custom-call | flops 452984832 | bytes 2621440 | tf_op jit(solution)/shard_map/kept/pallas_call | solution.py:16
  21.6 2.0 %collective-permute-done.10.returned = bf16[256,128]{1,0:T(8,128)(2,1)S(1)} collective-permute-done((bf16[256,128]{1,0:T(8,128)(2,1)S(1)}, bf16[256,128]{1,0:T(8,128)(2,1)S(1)}, u32[]{:S(2)}, u32[]{:S(2)}) %collective-permute-start.10) | collective-permute-done | bytes 65568 | tf_op jit(solution)/shard_map/ppermute | solution.py:179
  23.7 0.8 %join.1 = bf16[256,256]{1,0:T(8,128)(2,1)} custom-call(bf16[256,128]{1,0:T(8,128)(2,1)S(1)} %kept.1.kept_sums, bf16[256,128]{1,0:T(8,128)(2,1)S(1)} %collective-permute-done.10.returned), custom_call_target="tpu_custom_call" | custom-call | bytes 262144 | tf_op jit(solution)/shard_map/join/pallas_call | solution.py:16
  (3 shorter events, 0.0 us)
Async XLA Ops:
  0.0 6.6 %collective-permute-start = (bf16[2,2,64,256]{3,2,1,0:T(8,128)(2,1)}, bf16[2,2,64,256]{3,2,1,0:T(8,128)(2,1)S(1)}, u32[]{:S(2)}, u32[]{:S(2)}) collective-permute-start(bf16[2,2,64,256]{3,2,1,0:T(8,128)(2,1)} %volume.1), channel_id=1, source_target_pairs={{0,8},{1,9},{2,10},{3,11},{4,12},{5,13},{6,14},{7,15},{8,0},{9,1},... | collective-permute-start | bytes 393224 | tf_op jit(solution)/shard_map/ppermute | solution.py:179
  4.0 6.2 %collective-permute-start.2 = (bf16[32,2304]{1,0:T(8,128)(2,1)S(1)}, bf16[32,2304]{1,0:T(8,128)(2,1)S(1)}, u32[]{:S(2)}, u32[]{:S(2)}) collective-permute-start(bf16[32,2304]{1,0:T(8,128)(2,1)S(1)} %get-tuple-element.24), channel_id=1, source_target_pairs={{0,16},{1,17},{2,18},{3,19},{4,20},{5,21},{6,22},{7,23},{8,24},{9,... | collective-permute-start | bytes 442376 | tf_op jit(solution)/shard_map/ppermute | solution.py:179
  6.7 5.1 %collective-permute-start.1 = (bf16[1,2,64,256]{3,2,1,0:T(8,128)(2,1)S(1)}, bf16[1,2,64,256]{3,2,1,0:T(8,128)(2,1)S(1)}, u32[]{:S(2)}, u32[]{:S(2)}) collective-permute-start(bf16[1,2,64,256]{3,2,1,0:T(8,128)(2,1)S(1)} %border.1), channel_id=1, source_target_pairs={{0,16},{1,17},{2,18},{3,19},{4,20},{5,21},{6,22},{7,23},{8,24},{9,... | collective-permute-start | bytes 196616 | tf_op jit(solution)/shard_map/ppermute | solution.py:179
  8.5 8.6 %collective-permute-start.5 = (bf16[32,4608]{1,0:T(8,128)(2,1)S(1)}, bf16[32,4608]{1,0:T(8,128)(2,1)S(1)}, u32[]{:S(2)}, u32[]{:S(2)}) collective-permute-start(bf16[32,4608]{1,0:T(8,128)(2,1)S(1)} %get-tuple-element.28), channel_id=1, source_target_pairs={{0,16},{1,17},{2,18},{3,19},{4,20},{5,21},{6,22},{7,23},{8,24},{9,... | collective-permute-start | bytes 884744 | tf_op jit(solution)/shard_map/ppermute | solution.py:179
  8.8 8.3 %collective-permute-start.3 = (bf16[4,1,64,256]{3,2,1,0:T(8,128)(2,1)S(1)}, bf16[4,1,64,256]{3,2,1,0:T(8,128)(2,1)S(1)}, u32[]{:S(2)}, u32[]{:S(2)}) collective-permute-start(bf16[4,1,64,256]{3,2,1,0:T(8,128)(2,1)S(1)} %get-tuple-element.26), channel_id=1, source_target_pairs={{0,1},{1,0},{2,3},{3,2},{4,5},{5,4},{6,7},{7,6},{8,9},{9,8},{10,11... | collective-permute-start | bytes 393224 | tf_op jit(solution)/shard_map/ppermute | solution.py:179
  8.8 8.3 %collective-permute-start.4 = (bf16[4,1,64,256]{3,2,1,0:T(8,128)(2,1)S(1)}, bf16[4,1,64,256]{3,2,1,0:T(8,128)(2,1)S(1)}, u32[]{:S(2)}, u32[]{:S(2)}) collective-permute-start(bf16[4,1,64,256]{3,2,1,0:T(8,128)(2,1)S(1)} %get-tuple-element.27), channel_id=1, source_target_pairs={{1,2},{2,1},{3,4},{4,3},{5,6},{6,5},{9,10},{10,9},{11,12},{12,11},... | collective-permute-start | bytes 393224 | tf_op jit(solution)/shard_map/ppermute | solution.py:179
  11.8 1.9 %collective-permute-start.6 = (bf16[1,1,64,256]{3,2,1,0:T(8,128)(2,1)S(1)}, bf16[1,1,64,256]{3,2,1,0:T(8,128)(2,1)S(1)}, u32[]{:S(2)}, u32[]{:S(2)}) collective-permute-start(bf16[1,1,64,256]{3,2,1,0:T(8,128)(2,1)S(1)} %get-tuple-element.29), channel_id=1, source_target_pairs={{0,1},{1,0},{2,3},{3,2},{4,5},{5,4},{6,7},{7,6},{8,9},{9,8},{10,11... | collective-permute-start | bytes 98312 | tf_op jit(solution)/shard_map/ppermute | solution.py:179
  12.8 4.8 %copy-start = (bf16[6912,64]{0,1:T(8,128)(2,1)S(1)}, bf16[6912,64]{0,1:T(8,128)(2,1)}, u32[]{:S(2)}) copy-start(bf16[6912,64]{0,1:T(8,128)(2,1)} %param.3) | copy-start | bytes 2654212
  12.8 4.3 %collective-permute-start.7 = (bf16[1,1,64,256]{3,2,1,0:T(8,128)(2,1)S(1)}, bf16[1,1,64,256]{3,2,1,0:T(8,128)(2,1)S(1)}, u32[]{:S(2)}, u32[]{:S(2)}) collective-permute-start(bf16[1,1,64,256]{3,2,1,0:T(8,128)(2,1)S(1)} %get-tuple-element.31), channel_id=1, source_target_pairs={{1,2},{2,1},{3,4},{4,3},{5,6},{6,5},{9,10},{10,9},{11,12},{12,11},... | collective-permute-start | bytes 98312 | tf_op jit(solution)/shard_map/ppermute | solution.py:179
  13.7 4.0 %collective-permute-start.8 = (bf16[32,2304]{1,0:T(8,128)(2,1)S(1)}, bf16[32,2304]{1,0:T(8,128)(2,1)S(1)}, u32[]{:S(2)}, u32[]{:S(2)}) collective-permute-start(bf16[32,2304]{1,0:T(8,128)(2,1)S(1)} %collective-permute-done.2.here_first.here), channel_id=1, source_target_pairs={{0,1},{1,0},{2,3},{3,2},{4,5},{5,4},{6,7},{7,6},{8,9},{9,8},{10,11... | collective-permute-start | bytes 442376 | tf_op jit(solution)/shard_map/ppermute | solution.py:179
  17.1 1.6 %collective-permute-start.9 = (bf16[32,4608]{1,0:T(8,128)(2,1)S(1)}, bf16[32,4608]{1,0:T(8,128)(2,1)S(1)}, u32[]{:S(2)}, u32[]{:S(2)}) collective-permute-start(bf16[32,4608]{1,0:T(8,128)(2,1)S(1)} %collective-permute-done.5.here_second.here), channel_id=1, source_target_pairs={{0,1},{1,0},{2,3},{3,2},{4,5},{5,4},{6,7},{7,6},{8,9},{9,8},{10,11... | collective-permute-start | bytes 884744 | tf_op jit(solution)/shard_map/ppermute | solution.py:179
  19.3 4.3 %collective-permute-start.10 = (bf16[256,128]{1,0:T(8,128)(2,1)S(1)}, bf16[256,128]{1,0:T(8,128)(2,1)S(1)}, u32[]{:S(2)}, u32[]{:S(2)}) collective-permute-start(bf16[256,128]{1,0:T(8,128)(2,1)S(1)} %back.1), channel_id=1, source_target_pairs={{0,8},{1,9},{2,10},{3,11},{4,12},{5,13},{6,14},{7,15},{8,0},{9,1},... | collective-permute-start | bytes 196616 | tf_op jit(solution)/shard_map/ppermute | solution.py:179

commit v5 on v4

--- a/solution.py
+++ b/solution.py
@@ -8,6 +8,7 @@
 BOTH = ("slab", "chan")
 VMEM_LIMIT = 24 * 1024 * 1024
 EARLY_TAPS = 9
+BORDER_COST, OUTER_EDGE_COST, EXTEND_COST = 10**9, 3 * 10**9, 3 * 10**9
 
 
 def call(kernel, operands, outs, flops=0, places=None, scratch=()):
@@ -70,11 +71,8 @@
             out[depth + d, 0] = across[d, row]
 
 
-def outer_edges(outer, to_core, to_chip):
-    rows = outer.shape[1]
-    core = core_parity()
-    for out, row in ((to_core, (rows - 1) * (1 - core)), (to_chip, (rows - 1) * core)):
-        out[0, 0] = outer[0, row]
+def outer_edge(outer, to_core):
+    to_core[0, 0] = outer[0, (outer.shape[1] - 1) * (1 - core_parity())]
 
 
 def extend(block, across, outer, from_core, from_chip, outer_core, outer_chip, lines):
@@ -89,7 +87,8 @@
         elif d < 2 * depth:
             target, source, core_row, chip_row = second + d - depth, across.at[d - depth], from_core[d, 0], from_chip[d, 0]
         else:
-            target, source, core_row, chip_row = beyond, outer.at[0], outer_core[0, 0], outer_chip[0, 0]
+            target, source = beyond, outer.at[0]
+            core_row, chip_row = outer_core[0, 0], outer_chip[0, (rows - 1) * (1 - core_parity())]
         lines[target, 0] = jnp.where(even_core, chip_row, core_row)
         for r in range(rows):
             lines[target, r + 1] = source[r]
@@ -202,16 +201,17 @@
     )
     here_first = send(first, across_y)
     second, across = lax.optimization_barrier((second, across))
-    (plane,) = call(border, (block, across), [like((1, rows, cols, channels), volume)], 1000000000)
+    (plane,) = call(border, (block, across), [like((1, rows, cols, channels), volume)], BORDER_COST)
     outer = send(plane, across_y)
     here_second = send(second, across_y)
-    edge, outer_edge = like((2 * depth, 1, cols, channels), volume), like((1, 1, cols, channels), volume)
-    to_core, to_chip = call(edges, (block, across), [edge, edge], 5000000000)
+    edge, line = like((2 * depth, 1, cols, channels), volume), like((1, 1, cols, channels), volume)
+    to_core, to_chip = call(edges, (block, across), [edge, edge])
     from_core, from_chip = send(to_core, other_core), send(to_chip, next_chip)
     outer, here_first = lax.optimization_barrier((outer, here_first))
-    to_core, to_chip = call(outer_edges, (outer,), [outer_edge, outer_edge], 8000000000)
-    outer_core, outer_chip = send(to_core, other_core), send(to_chip, next_chip)
-    here_first, to_chip_held = lax.optimization_barrier((here_first, outer_core))
+    outer_chip = send(outer, next_chip)
+    (to_core,) = call(outer_edge, (outer,), [line], OUTER_EDGE_COST)
+    outer_core = send(to_core, other_core)
+    here_first, outer_core = lax.optimization_barrier((here_first, outer_core))
     there_first = send(here_first, other_core)
     here_second, outer_core = lax.optimization_barrier((here_second, outer_core))
     there_second = send(here_second, other_core)
@@ -219,7 +219,7 @@
         extend,
         (block, across, outer, from_core, from_chip, outer_core, outer_chip),
         [like((2 * depth + 2, rows + 2, cols, channels), volume)],
-        3000000000,
+        EXTEND_COST,
     )
     work = 2 * voxels * depth_of_sum * width
     both, sums = like((voxels, 2 * width), volume), jax.ShapeDtypeStruct((voxels, width), jnp.float32)

time: 24.6 us -> 24.6 us (level)
  waiting for transfers between devices: 6.72 us -> 7.24 us
  starting transfers between devices: 13.4 us -> 12.9 us
    ppermute x11, waiting for transfers between devices: 6.72 us -> 7.24 us  [send(): return lax.ppermute(array, BOTH, pairs)]
    ppermute x11, starting transfers between devices: 13.4 us -> 12.9 us  [send(): return lax.ppermute(array, BOTH, pairs)]
where the time goes in v5:
time: 24.6 us; the launch traced here: 24.5 us
  starting transfers between devices  12.9 us (52%)
  waiting for transfers between devices  7.24 us (29%)
  Pallas kernels  4.22 us (17%)
    ppermute x11, starting transfers between devices, send(): return lax.ppermute(array, BOTH, pairs)  12.9 us
    ppermute x11, waiting for transfers between devices, send(): return lax.ppermute(array, BOTH, pairs)  7.24 us
    pallas_call x9, Pallas kernels, call(): pl.pallas_call(kernel, out_shape=outs, in_specs=places or [vmem] * len(op...  4.22 us
  transfers between devices with their start and end apart: 11, of which 8 were waited for; matrix products, arithmetic and copies ran while one was open for 0% of the time, Pallas kernels for 12%

profile of v5, /device:TPU:0, one launch (start us, length us, event | category | flops | bytes accessed | tf_op | source)
XLA Modules:
  0.0 24.5 jit_solution(8391878981872193188)
XLA Ops:
  0.0 2.9 %collective-permute-start = (bf16[2,2,64,256]{3,2,1,0:T(8,128)(2,1)}, bf16[2,2,64,256]{3,2,1,0:T(8,128)(2,1)S(1)}, u32[]{:S(2)}, u32[]{:S(2)}) collective-permute-start(bf16[2,2,64,256]{3,2,1,0:T(8,128)(2,1)} %volume.1), channel_id=1, source_target_pairs={{0,8},{1,9},{2,10},{3,11},{4,12},{5,13},{6,14},{7,15},{8,0},{9,1},... | collective-permute-start | bytes 393224 | tf_op jit(solution)/shard_map/ppermute | solution.py:178
  2.9 1.1 %fetch.1 = (bf16[32,2304]{1,0:T(8,128)(2,1)S(1)}, bf16[32,4608]{1,0:T(8,128)(2,1)S(1)}, bf16[2,2,64,256]{3,2,1,0:T(8,128)(2,1)S(1)}) custom-call(bf16[2,2,64,256]{3,2,1,0:T(8,128)(2,1)} %volume.1, bf16[64,6912]{1,0:T(8,128)(2,1)} %bitcast.2), custom_call_target="tpu_custom_call" | custom-call | bytes 1589248 | tf_op jit(solution)/shard_map/fetch/pallas_call | solution.py:17
  4.0 1.6 %collective-permute-start.2 = (bf16[32,2304]{1,0:T(8,128)(2,1)S(1)}, bf16[32,2304]{1,0:T(8,128)(2,1)S(1)}, u32[]{:S(2)}, u32[]{:S(2)}) collective-permute-start(bf16[32,2304]{1,0:T(8,128)(2,1)S(1)} %get-tuple-element.23), channel_id=1, source_target_pairs={{0,16},{1,17},{2,18},{3,19},{4,20},{5,21},{6,22},{7,23},{8,24},{9,... | collective-permute-start | bytes 442376 | tf_op jit(solution)/shard_map/ppermute | solution.py:178
  5.6 1.0 %collective-permute-done.across = bf16[2,2,64,256]{3,2,1,0:T(8,128)(2,1)S(1)} collective-permute-done((bf16[2,2,64,256]{3,2,1,0:T(8,128)(2,1)}, bf16[2,2,64,256]{3,2,1,0:T(8,128)(2,1)S(1)}, u32[]{:S(2)}, u32[]{:S(2)}) %collective-permute-start) | collective-permute-done | bytes 131104 | tf_op jit(solution)/shard_map/ppermute | solution.py:178
  6.7 1.8 %collective-permute-start.1 = (bf16[1,2,64,256]{3,2,1,0:T(8,128)(2,1)S(1)}, bf16[1,2,64,256]{3,2,1,0:T(8,128)(2,1)S(1)}, u32[]{:S(2)}, u32[]{:S(2)}) collective-permute-start(bf16[1,2,64,256]{3,2,1,0:T(8,128)(2,1)S(1)} %border.1), channel_id=1, source_target_pairs={{0,16},{1,17},{2,18},{3,19},{4,20},{5,21},{6,22},{7,23},{8,24},{9,... | collective-permute-start | bytes 196616 | tf_op jit(solution)/shard_map/ppermute | solution.py:178
  8.5 0.3 %collective-permute-start.5 = (bf16[32,4608]{1,0:T(8,128)(2,1)S(1)}, bf16[32,4608]{1,0:T(8,128)(2,1)S(1)}, u32[]{:S(2)}, u32[]{:S(2)}) collective-permute-start(bf16[32,4608]{1,0:T(8,128)(2,1)S(1)} %get-tuple-element.27), channel_id=1, source_target_pairs={{0,16},{1,17},{2,18},{3,19},{4,20},{5,21},{6,22},{7,23},{8,24},{9,... | collective-permute-start | bytes 884744 | tf_op jit(solution)/shard_map/ppermute | solution.py:178
  8.8 0.0 collective-permute-start.3
  8.8 0.7 %collective-permute-start.4 = (bf16[4,1,64,256]{3,2,1,0:T(8,128)(2,1)S(1)}, bf16[4,1,64,256]{3,2,1,0:T(8,128)(2,1)S(1)}, u32[]{:S(2)}, u32[]{:S(2)}) collective-permute-start(bf16[4,1,64,256]{3,2,1,0:T(8,128)(2,1)S(1)} %get-tuple-element.26), channel_id=1, source_target_pairs={{1,2},{2,1},{3,4},{4,3},{5,6},{6,5},{9,10},{10,9},{11,12},{12,11},... | collective-permute-start | bytes 393224 | tf_op jit(solution)/shard_map/ppermute | solution.py:178
  9.5 0.7 %collective-permute-done.2.here_first.here = bf16[32,2304]{1,0:T(8,128)(2,1)S(1)} collective-permute-done((bf16[32,2304]{1,0:T(8,128)(2,1)S(1)}, bf16[32,2304]{1,0:T(8,128)(2,1)S(1)}, u32[]{:S(2)}, u32[]{:S(2)}) %collective-permute-start.2) | collective-permute-done | bytes 147488 | tf_op jit(solution)/shard_map/ppermute | solution.py:178
  10.2 1.5 %collective-permute-done.1.outer = bf16[1,2,64,256]{3,2,1,0:T(8,128)(2,1)S(1)} collective-permute-done((bf16[1,2,64,256]{3,2,1,0:T(8,128)(2,1)S(1)}, bf16[1,2,64,256]{3,2,1,0:T(8,128)(2,1)S(1)}, u32[]{:S(2)}, u32[]{:S(2)}) %collective-permute-start.1) | collective-permute-done | bytes 65568 | tf_op jit(solution)/shard_map/ppermute | solution.py:178
  11.8 0.7 %collective-permute-start.7 = (bf16[1,2,64,256]{3,2,1,0:T(8,128)(2,1)S(1)}, bf16[1,2,64,256]{3,2,1,0:T(8,128)(2,1)S(1)}, u32[]{:S(2)}, u32[]{:S(2)}) collective-permute-start(bf16[1,2,64,256]{3,2,1,0:T(8,128)(2,1)S(1)} %collective-permute-done.1.outer), channel_id=1, source_target_pairs={{1,2},{2,1},{3,4},{4,3},{5,6},{6,5},{9,10},{10,9},{11,12},{12,11},... | collective-permute-start | bytes 196616 | tf_op jit(solution)/shard_map/ppermute | solution.py:178
  12.4 0.0 copy-start
  12.4 3.3 %collective-permute-start.6 = (bf16[1,1,64,256]{3,2,1,0:T(8,128)(2,1)S(1)}, bf16[1,1,64,256]{3,2,1,0:T(8,128)(2,1)S(1)}, u32[]{:S(2)}, u32[]{:S(2)}) collective-permute-start(bf16[1,1,64,256]{3,2,1,0:T(8,128)(2,1)S(1)} %outer_edge.1), channel_id=1, source_target_pairs={{0,1},{1,0},{2,3},{3,2},{4,5},{5,4},{6,7},{7,6},{8,9},{9,8},{10,11... | collective-permute-start | bytes 98312 | tf_op jit(solution)/shard_map/ppermute | solution.py:178
  15.7 0.9 %collective-permute-done.6.outer_core = bf16[1,1,64,256]{3,2,1,0:T(8,128)(2,1)S(1)} collective-permute-done((bf16[1,1,64,256]{3,2,1,0:T(8,128)(2,1)S(1)}, bf16[1,1,64,256]{3,2,1,0:T(8,128)(2,1)S(1)}, u32[]{:S(2)}, u32[]{:S(2)}) %collective-permute-start.6) | collective-permute-done | bytes 32800 | tf_op jit(solution)/shard_map/ppermute | solution.py:178
  16.6 0.3 %collective-permute-start.8 = (bf16[32,2304]{1,0:T(8,128)(2,1)S(1)}, bf16[32,2304]{1,0:T(8,128)(2,1)S(1)}, u32[]{:S(2)}, u32[]{:S(2)}) collective-permute-start(bf16[32,2304]{1,0:T(8,128)(2,1)S(1)} %collective-permute-done.2.here_first.here), channel_id=1, source_target_pairs={{0,1},{1,0},{2,3},{3,2},{4,5},{5,4},{6,7},{7,6},{8,9},{9,8},{10,11... | collective-permute-start | bytes 442376 | tf_op jit(solution)/shard_map/ppermute | solution.py:178
  16.9 0.2 collective-permute-done.5.here_second.here
  17.1 0.0 collective-permute-start.9
  17.1 0.0 collective-permute-done.7.outer_chip
  17.1 0.0 collective-permute-done.3.from_core
  17.1 0.0 collective-permute-done.4.from_chip
  17.2 0.1 extend.1.lines
  17.2 0.7 %collective-permute-done.8.there_first.there = bf16[32,2304]{1,0:T(8,128)(2,1)S(1)} collective-permute-done((bf16[32,2304]{1,0:T(8,128)(2,1)S(1)}, bf16[32,2304]{1,0:T(8,128)(2,1)S(1)}, u32[]{:S(2)}, u32[]{:S(2)}) %collective-permute-start.8) | collective-permute-done | bytes 147488 | tf_op jit(solution)/shard_map/ppermute | solution.py:178
  17.9 0.0 copy-done
  17.9 0.7 %back_early.1 = (f32[256,64]{1,0:T(8,128)S(1)}, f32[256,64]{1,0:T(8,128)S(1)}) custom-call(bf16[6,4,64,256]{3,2,1,0:T(8,128)(2,1)S(1)} %extend.1.lines, bf16[64,6912]{1,0:T(8,128)(2,1)S(1)} %bitcast.3, bf16[32,2304]{1,0:T(8,128)(2,1)S(1)} %collective-permute-done.2.here_first.here, bf16[32,2304]{1,0:T(8,128)(2,1)S(1)} %collective-permute-done.8.there_first.there), custom_call_target="tpu_custom_call" | custom-call | flops 226492416 | bytes 2097152 | tf_op jit(solution)/shard_map/back_early/pallas_call | solution.py:17
  18.6 0.1 collective-permute-done.9.there_second.there
  18.7 0.6 %back.1 = bf16[256,128]{1,0:T(8,128)(2,1)S(1)} custom-call(bf16[6,4,64,256]{3,2,1,0:T(8,128)(2,1)S(1)} %extend.1.lines, f32[256,64]{1,0:T(8,128)S(1)} %get-tuple-element.33.near, f32[256,64]{1,0:T(8,128)S(1)} %get-tuple-element.34.far, bf16[32,4608]{1,0:T(8,128)(2,1)S(1)} %collective-permute-done.5.here_second.here, ...), custom_call_target="tpu_custom_call" | custom-call | flops 226492416 | bytes 1572864 | tf_op jit(solution)/shard_map/back/pallas_call | solution.py:17
  19.3 1.3 %collective-permute-start.10 = (bf16[256,128]{1,0:T(8,128)(2,1)S(1)}, bf16[256,128]{1,0:T(8,128)(2,1)S(1)}, u32[]{:S(2)}, u32[]{:S(2)}) collective-permute-start(bf16[256,128]{1,0:T(8,128)(2,1)S(1)} %back.1), channel_id=1, source_target_pairs={{0,8},{1,9},{2,10},{3,11},{4,12},{5,13},{6,14},{7,15},{8,0},{9,1},... | collective-permute-start | bytes 196616 | tf_op jit(solution)/shard_map/ppermute | solution.py:178
  20.7 1.0 %kept.1.kept_sums = bf16[256,128]{1,0:T(8,128)(2,1)S(1)} custom-call(bf16[6,4,64,256]{3,2,1,0:T(8,128)(2,1)S(1)} %extend.1.lines, bf16[64,6912]{1,0:T(8,128)(2,1)S(1)} %bitcast.4, bf16[32,2304]{1,0:T(8,128)(2,1)S(1)} %collective-permute-done.2.here_first.here, bf16[32,2304]{1,0:T(8,128)(2,1)S(1)} %collective-permute-done.8.there_first.there, ...), custom_call_target="tpu_custom_call" | custom-call | flops 452984832 | bytes 2621440 | tf_op jit(solution)/shard_map/kept/pallas_call | solution.py:17
  21.7 2.1 %collective-permute-done.10.returned = bf16[256,128]{1,0:T(8,128)(2,1)S(1)} collective-permute-done((bf16[256,128]{1,0:T(8,128)(2,1)S(1)}, bf16[256,128]{1,0:T(8,128)(2,1)S(1)}, u32[]{:S(2)}, u32[]{:S(2)}) %collective-permute-start.10) | collective-permute-done | bytes 65568 | tf_op jit(solution)/shard_map/ppermute | solution.py:178
  23.7 0.8 %join.1 = bf16[256,256]{1,0:T(8,128)(2,1)} custom-call(bf16[256,128]{1,0:T(8,128)(2,1)S(1)} %kept.1.kept_sums, bf16[256,128]{1,0:T(8,128)(2,1)S(1)} %collective-permute-done.10.returned), custom_call_target="tpu_custom_call" | custom-call | bytes 262144 | tf_op jit(solution)/shard_map/join/pallas_call | solution.py:17
  (3 shorter events, 0.0 us)
Async XLA Ops:
  0.0 6.6 %collective-permute-start = (bf16[2,2,64,256]{3,2,1,0:T(8,128)(2,1)}, bf16[2,2,64,256]{3,2,1,0:T(8,128)(2,1)S(1)}, u32[]{:S(2)}, u32[]{:S(2)}) collective-permute-start(bf16[2,2,64,256]{3,2,1,0:T(8,128)(2,1)} %volume.1), channel_id=1, source_target_pairs={{0,8},{1,9},{2,10},{3,11},{4,12},{5,13},{6,14},{7,15},{8,0},{9,1},... | collective-permute-start | bytes 393224 | tf_op jit(solution)/shard_map/ppermute | solution.py:178
  4.0 6.2 %collective-permute-start.2 = (bf16[32,2304]{1,0:T(8,128)(2,1)S(1)}, bf16[32,2304]{1,0:T(8,128)(2,1)S(1)}, u32[]{:S(2)}, u32[]{:S(2)}) collective-permute-start(bf16[32,2304]{1,0:T(8,128)(2,1)S(1)} %get-tuple-element.23), channel_id=1, source_target_pairs={{0,16},{1,17},{2,18},{3,19},{4,20},{5,21},{6,22},{7,23},{8,24},{9,... | collective-permute-start | bytes 442376 | tf_op jit(solution)/shard_map/ppermute | solution.py:178
  6.7 5.1 %collective-permute-start.1 = (bf16[1,2,64,256]{3,2,1,0:T(8,128)(2,1)S(1)}, bf16[1,2,64,256]{3,2,1,0:T(8,128)(2,1)S(1)}, u32[]{:S(2)}, u32[]{:S(2)}) collective-permute-start(bf16[1,2,64,256]{3,2,1,0:T(8,128)(2,1)S(1)} %border.1), channel_id=1, source_target_pairs={{0,16},{1,17},{2,18},{3,19},{4,20},{5,21},{6,22},{7,23},{8,24},{9,... | collective-permute-start | bytes 196616 | tf_op jit(solution)/shard_map/ppermute | solution.py:178
  8.5 8.6 %collective-permute-start.5 = (bf16[32,4608]{1,0:T(8,128)(2,1)S(1)}, bf16[32,4608]{1,0:T(8,128)(2,1)S(1)}, u32[]{:S(2)}, u32[]{:S(2)}) collective-permute-start(bf16[32,4608]{1,0:T(8,128)(2,1)S(1)} %get-tuple-element.27), channel_id=1, source_target_pairs={{0,16},{1,17},{2,18},{3,19},{4,20},{5,21},{6,22},{7,23},{8,24},{9,... | collective-permute-start | bytes 884744 | tf_op jit(solution)/shard_map/ppermute | solution.py:178
  8.8 8.3 %collective-permute-start.3 = (bf16[4,1,64,256]{3,2,1,0:T(8,128)(2,1)S(1)}, bf16[4,1,64,256]{3,2,1,0:T(8,128)(2,1)S(1)}, u32[]{:S(2)}, u32[]{:S(2)}) collective-permute-start(bf16[4,1,64,256]{3,2,1,0:T(8,128)(2,1)S(1)} %get-tuple-element.25), channel_id=1, source_target_pairs={{0,1},{1,0},{2,3},{3,2},{4,5},{5,4},{6,7},{7,6},{8,9},{9,8},{10,11... | collective-permute-start | bytes 393224 | tf_op jit(solution)/shard_map/ppermute | solution.py:178
  8.8 8.3 %collective-permute-start.4 = (bf16[4,1,64,256]{3,2,1,0:T(8,128)(2,1)S(1)}, bf16[4,1,64,256]{3,2,1,0:T(8,128)(2,1)S(1)}, u32[]{:S(2)}, u32[]{:S(2)}) collective-permute-start(bf16[4,1,64,256]{3,2,1,0:T(8,128)(2,1)S(1)} %get-tuple-element.26), channel_id=1, source_target_pairs={{1,2},{2,1},{3,4},{4,3},{5,6},{6,5},{9,10},{10,9},{11,12},{12,11},... | collective-permute-start | bytes 393224 | tf_op jit(solution)/shard_map/ppermute | solution.py:178
  11.8 5.4 %collective-permute-start.7 = (bf16[1,2,64,256]{3,2,1,0:T(8,128)(2,1)S(1)}, bf16[1,2,64,256]{3,2,1,0:T(8,128)(2,1)S(1)}, u32[]{:S(2)}, u32[]{:S(2)}) collective-permute-start(bf16[1,2,64,256]{3,2,1,0:T(8,128)(2,1)S(1)} %collective-permute-done.1.outer), channel_id=1, source_target_pairs={{1,2},{2,1},{3,4},{4,3},{5,6},{6,5},{9,10},{10,9},{11,12},{12,11},... | collective-permute-start | bytes 196616 | tf_op jit(solution)/shard_map/ppermute | solution.py:178
  12.4 5.5 %copy-start = (bf16[6912,64]{0,1:T(8,128)(2,1)S(1)}, bf16[6912,64]{0,1:T(8,128)(2,1)}, u32[]{:S(2)}) copy-start(bf16[6912,64]{0,1:T(8,128)(2,1)} %param.3) | copy-start | bytes 2654212
  12.4 4.1 %collective-permute-start.6 = (bf16[1,1,64,256]{3,2,1,0:T(8,128)(2,1)S(1)}, bf16[1,1,64,256]{3,2,1,0:T(8,128)(2,1)S(1)}, u32[]{:S(2)}, u32[]{:S(2)}) collective-permute-start(bf16[1,1,64,256]{3,2,1,0:T(8,128)(2,1)S(1)} %outer_edge.1), channel_id=1, source_target_pairs={{0,1},{1,0},{2,3},{3,2},{4,5},{5,4},{6,7},{7,6},{8,9},{9,8},{10,11... | collective-permute-start | bytes 98312 | tf_op jit(solution)/shard_map/ppermute | solution.py:178
  16.6 1.4 %collective-permute-start.8 = (bf16[32,2304]{1,0:T(8,128)(2,1)S(1)}, bf16[32,2304]{1,0:T(8,128)(2,1)S(1)}, u32[]{:S(2)}, u32[]{:S(2)}) collective-permute-start(bf16[32,2304]{1,0:T(8,128)(2,1)S(1)} %collective-permute-done.2.here_first.here), channel_id=1, source_target_pairs={{0,1},{1,0},{2,3},{3,2},{4,5},{5,4},{6,7},{7,6},{8,9},{9,8},{10,11... | collective-permute-start | bytes 442376 | tf_op jit(solution)/shard_map/ppermute | solution.py:178
  17.1 1.6 %collective-permute-start.9 = (bf16[32,4608]{1,0:T(8,128)(2,1)S(1)}, bf16[32,4608]{1,0:T(8,128)(2,1)S(1)}, u32[]{:S(2)}, u32[]{:S(2)}) collective-permute-start(bf16[32,4608]{1,0:T(8,128)(2,1)S(1)} %collective-permute-done.5.here_second.here), channel_id=1, source_target_pairs={{0,1},{1,0},{2,3},{3,2},{4,5},{5,4},{6,7},{7,6},{8,9},{9,8},{10,11... | collective-permute-start | bytes 884744 | tf_op jit(solution)/shard_map/ppermute | solution.py:178
  19.3 4.4 %collective-permute-start.10 = (bf16[256,128]{1,0:T(8,128)(2,1)S(1)}, bf16[256,128]{1,0:T(8,128)(2,1)S(1)}, u32[]{:S(2)}, u32[]{:S(2)}) collective-permute-start(bf16[256,128]{1,0:T(8,128)(2,1)S(1)} %back.1), channel_id=1, source_target_pairs={{0,8},{1,9},{2,10},{3,11},{4,12},{5,13},{6,14},{7,15},{8,0},{9,1},... | collective-permute-start | bytes 196616 | tf_op jit(solution)/shard_map/ppermute | solution.py:178

commit v6 on v4

--- a/solution.py
+++ b/solution.py
@@ -8,6 +8,7 @@
 BOTH = ("slab", "chan")
 VMEM_LIMIT = 24 * 1024 * 1024
 EARLY_TAPS = 9
+BORDER_COST, EDGES_COST, OUTER_EDGES_COST, EXTEND_COST = 10**9, 5 * 10**9, 8 * 10**9, 3 * 10**9
 
 
 def call(kernel, operands, outs, flops=0, places=None, scratch=()):
@@ -202,16 +203,16 @@
     )
     here_first = send(first, across_y)
     second, across = lax.optimization_barrier((second, across))
-    (plane,) = call(border, (block, across), [like((1, rows, cols, channels), volume)], 1000000000)
+    (plane,) = call(border, (block, across), [like((1, rows, cols, channels), volume)], BORDER_COST)
     outer = send(plane, across_y)
     here_second = send(second, across_y)
     edge, outer_edge = like((2 * depth, 1, cols, channels), volume), like((1, 1, cols, channels), volume)
-    to_core, to_chip = call(edges, (block, across), [edge, edge], 5000000000)
+    to_core, to_chip = call(edges, (block, across), [edge, edge], EDGES_COST)
     from_core, from_chip = send(to_core, other_core), send(to_chip, next_chip)
     outer, here_first = lax.optimization_barrier((outer, here_first))
-    to_core, to_chip = call(outer_edges, (outer,), [outer_edge, outer_edge], 8000000000)
+    to_core, to_chip = call(outer_edges, (outer,), [outer_edge, outer_edge], OUTER_EDGES_COST)
     outer_core, outer_chip = send(to_core, other_core), send(to_chip, next_chip)
-    here_first, to_chip_held = lax.optimization_barrier((here_first, outer_core))
+    here_first, outer_core = lax.optimization_barrier((here_first, outer_core))
     there_first = send(here_first, other_core)
     here_second, outer_core = lax.optimization_barrier((here_second, outer_core))
     there_second = send(here_second, other_core)
@@ -219,7 +220,7 @@
         extend,
         (block, across, outer, from_core, from_chip, outer_core, outer_chip),
         [like((2 * depth + 2, rows + 2, cols, channels), volume)],
-        3000000000,
+        EXTEND_COST,
     )
     work = 2 * voxels * depth_of_sum * width
     both, sums = like((voxels, 2 * width), volume), jax.ShapeDtypeStruct((voxels, width), jnp.float32)

time: 24.6 us -> 24.6 us (level)
  no operation moved by 1% of the time
where the time goes in v6:
time: 24.6 us; the launch traced here: 24.4 us
  starting transfers between devices  13.4 us (54%)
  waiting for transfers between devices  6.72 us (27%)
  Pallas kernels  4.2 us (17%)
    ppermute x11, starting transfers between devices, send(): return lax.ppermute(array, BOTH, pairs)  13.4 us
    ppermute x11, waiting for transfers between devices, send(): return lax.ppermute(array, BOTH, pairs)  6.72 us
    pallas_call x9, Pallas kernels, call(): pl.pallas_call(kernel, out_shape=outs, in_specs=places or [vmem] * len(op...  4.2 us
  transfers between devices with their start and end apart: 11, of which 8 were waited for; matrix products, arithmetic and copies ran while one was open for 0% of the time, Pallas kernels for 12%

profile of v6, /device:TPU:0, one launch (start us, length us, event | category | flops | bytes accessed | tf_op | source)
XLA Modules:
  0.0 24.4 jit_solution(14822969217011570552)
XLA Ops:
  0.0 2.9 %collective-permute-start = (bf16[2,2,64,256]{3,2,1,0:T(8,128)(2,1)}, bf16[2,2,64,256]{3,2,1,0:T(8,128)(2,1)S(1)}, u32[]{:S(2)}, u32[]{:S(2)}) collective-permute-start(bf16[2,2,64,256]{3,2,1,0:T(8,128)(2,1)} %volume.1), channel_id=1, source_target_pairs={{0,8},{1,9},{2,10},{3,11},{4,12},{5,13},{6,14},{7,15},{8,0},{9,1},... | collective-permute-start | bytes 393224 | tf_op jit(solution)/shard_map/ppermute | solution.py:180
  2.9 1.1 %fetch.1 = (bf16[32,2304]{1,0:T(8,128)(2,1)S(1)}, bf16[32,4608]{1,0:T(8,128)(2,1)S(1)}, bf16[2,2,64,256]{3,2,1,0:T(8,128)(2,1)S(1)}) custom-call(bf16[2,2,64,256]{3,2,1,0:T(8,128)(2,1)} %volume.1, bf16[64,6912]{1,0:T(8,128)(2,1)} %bitcast.2), custom_call_target="tpu_custom_call" | custom-call | bytes 1589248 | tf_op jit(solution)/shard_map/fetch/pallas_call | solution.py:17
  4.0 1.6 %collective-permute-start.2 = (bf16[32,2304]{1,0:T(8,128)(2,1)S(1)}, bf16[32,2304]{1,0:T(8,128)(2,1)S(1)}, u32[]{:S(2)}, u32[]{:S(2)}) collective-permute-start(bf16[32,2304]{1,0:T(8,128)(2,1)S(1)} %get-tuple-element.25), channel_id=1, source_target_pairs={{0,16},{1,17},{2,18},{3,19},{4,20},{5,21},{6,22},{7,23},{8,24},{9,... | collective-permute-start | bytes 442376 | tf_op jit(solution)/shard_map/ppermute | solution.py:180
  5.6 1.0 %collective-permute-done.across = bf16[2,2,64,256]{3,2,1,0:T(8,128)(2,1)S(1)} collective-permute-done((bf16[2,2,64,256]{3,2,1,0:T(8,128)(2,1)}, bf16[2,2,64,256]{3,2,1,0:T(8,128)(2,1)S(1)}, u32[]{:S(2)}, u32[]{:S(2)}) %collective-permute-start) | collective-permute-done | bytes 131104 | tf_op jit(solution)/shard_map/ppermute | solution.py:180
  6.7 1.8 %collective-permute-start.1 = (bf16[1,2,64,256]{3,2,1,0:T(8,128)(2,1)S(1)}, bf16[1,2,64,256]{3,2,1,0:T(8,128)(2,1)S(1)}, u32[]{:S(2)}, u32[]{:S(2)}) collective-permute-start(bf16[1,2,64,256]{3,2,1,0:T(8,128)(2,1)S(1)} %border.1), channel_id=1, source_target_pairs={{0,16},{1,17},{2,18},{3,19},{4,20},{5,21},{6,22},{7,23},{8,24},{9,... | collective-permute-start | bytes 196616 | tf_op jit(solution)/shard_map/ppermute | solution.py:180
  8.5 0.3 %collective-permute-start.5 = (bf16[32,4608]{1,0:T(8,128)(2,1)S(1)}, bf16[32,4608]{1,0:T(8,128)(2,1)S(1)}, u32[]{:S(2)}, u32[]{:S(2)}) collective-permute-start(bf16[32,4608]{1,0:T(8,128)(2,1)S(1)} %get-tuple-element.29), channel_id=1, source_target_pairs={{0,16},{1,17},{2,18},{3,19},{4,20},{5,21},{6,22},{7,23},{8,24},{9,... | collective-permute-start | bytes 884744 | tf_op jit(solution)/shard_map/ppermute | solution.py:180
  8.8 0.0 collective-permute-start.3
  8.8 0.7 %collective-permute-start.4 = (bf16[4,1,64,256]{3,2,1,0:T(8,128)(2,1)S(1)}, bf16[4,1,64,256]{3,2,1,0:T(8,128)(2,1)S(1)}, u32[]{:S(2)}, u32[]{:S(2)}) collective-permute-start(bf16[4,1,64,256]{3,2,1,0:T(8,128)(2,1)S(1)} %get-tuple-element.28), channel_id=1, source_target_pairs={{1,2},{2,1},{3,4},{4,3},{5,6},{6,5},{9,10},{10,9},{11,12},{12,11},... | collective-permute-start | bytes 393224 | tf_op jit(solution)/shard_map/ppermute | solution.py:180
  9.5 0.7 %collective-permute-done.2.here_first.here = bf16[32,2304]{1,0:T(8,128)(2,1)S(1)} collective-permute-done((bf16[32,2304]{1,0:T(8,128)(2,1)S(1)}, bf16[32,2304]{1,0:T(8,128)(2,1)S(1)}, u32[]{:S(2)}, u32[]{:S(2)}) %collective-permute-start.2) | collective-permute-done | bytes 147488 | tf_op jit(solution)/shard_map/ppermute | solution.py:180
  10.2 1.5 %collective-permute-done.1.outer = bf16[1,2,64,256]{3,2,1,0:T(8,128)(2,1)S(1)} collective-permute-done((bf16[1,2,64,256]{3,2,1,0:T(8,128)(2,1)S(1)}, bf16[1,2,64,256]{3,2,1,0:T(8,128)(2,1)S(1)}, u32[]{:S(2)}, u32[]{:S(2)}) %collective-permute-start.1) | collective-permute-done | bytes 65568 | tf_op jit(solution)/shard_map/ppermute | solution.py:180
  11.8 1.0 %collective-permute-start.6 = (bf16[1,1,64,256]{3,2,1,0:T(8,128)(2,1)S(1)}, bf16[1,1,64,256]{3,2,1,0:T(8,128)(2,1)S(1)}, u32[]{:S(2)}, u32[]{:S(2)}) collective-permute-start(bf16[1,1,64,256]{3,2,1,0:T(8,128)(2,1)S(1)} %get-tuple-element.31), channel_id=1, source_target_pairs={{0,1},{1,0},{2,3},{3,2},{4,5},{5,4},{6,7},{7,6},{8,9},{9,8},{10,11... | collective-permute-start | bytes 98312 | tf_op jit(solution)/shard_map/ppermute | solution.py:180
  12.8 0.0 copy-start
  12.8 0.8 %collective-permute-start.7 = (bf16[1,1,64,256]{3,2,1,0:T(8,128)(2,1)S(1)}, bf16[1,1,64,256]{3,2,1,0:T(8,128)(2,1)S(1)}, u32[]{:S(2)}, u32[]{:S(2)}) collective-permute-start(bf16[1,1,64,256]{3,2,1,0:T(8,128)(2,1)S(1)} %get-tuple-element.34), channel_id=1, source_target_pairs={{1,2},{2,1},{3,4},{4,3},{5,6},{6,5},{9,10},{10,9},{11,12},{12,11},... | collective-permute-start | bytes 98312 | tf_op jit(solution)/shard_map/ppermute | solution.py:180
  13.6 0.1 collective-permute-done.6.outer_core
  13.7 2.9 %collective-permute-start.8 = (bf16[32,2304]{1,0:T(8,128)(2,1)S(1)}, bf16[32,2304]{1,0:T(8,128)(2,1)S(1)}, u32[]{:S(2)}, u32[]{:S(2)}) collective-permute-start(bf16[32,2304]{1,0:T(8,128)(2,1)S(1)} %collective-permute-done.2.here_first.here), channel_id=1, source_target_pairs={{0,1},{1,0},{2,3},{3,2},{4,5},{5,4},{6,7},{7,6},{8,9},{9,8},{10,11... | collective-permute-start | bytes 442376 | tf_op jit(solution)/shard_map/ppermute | solution.py:180
  16.6 0.5 %collective-permute-done.5.here_second.here = bf16[32,4608]{1,0:T(8,128)(2,1)S(1)} collective-permute-done((bf16[32,4608]{1,0:T(8,128)(2,1)S(1)}, bf16[32,4608]{1,0:T(8,128)(2,1)S(1)}, u32[]{:S(2)}, u32[]{:S(2)}) %collective-permute-start.5) | collective-permute-done | bytes 294944 | tf_op jit(solution)/shard_map/ppermute | solution.py:180
  17.1 0.0 collective-permute-start.9
  17.1 0.0 collective-permute-done.7.outer_chip
  17.1 0.0 collective-permute-done.3.from_core
  17.1 0.0 collective-permute-done.4.from_chip
  17.2 0.1 extend.1.lines
  17.2 0.4 %collective-permute-done.8.there_first.there = bf16[32,2304]{1,0:T(8,128)(2,1)S(1)} collective-permute-done((bf16[32,2304]{1,0:T(8,128)(2,1)S(1)}, bf16[32,2304]{1,0:T(8,128)(2,1)S(1)}, u32[]{:S(2)}, u32[]{:S(2)}) %collective-permute-start.8) | collective-permute-done | bytes 147488 | tf_op jit(solution)/shard_map/ppermute | solution.py:180
  17.6 0.0 copy-done
  17.6 0.7 %back_early.1 = (f32[256,64]{1,0:T(8,128)S(1)}, f32[256,64]{1,0:T(8,128)S(1)}) custom-call(bf16[6,4,64,256]{3,2,1,0:T(8,128)(2,1)S(1)} %extend.1.lines, bf16[64,6912]{1,0:T(8,128)(2,1)S(1)} %bitcast.3, bf16[32,2304]{1,0:T(8,128)(2,1)S(1)} %collective-permute-done.2.here_first.here, bf16[32,2304]{1,0:T(8,128)(2,1)S(1)} %collective-permute-done.8.there_first.there), custom_call_target="tpu_custom_call" | custom-call | flops 226492416 | bytes 2097152 | tf_op jit(solution)/shard_map/back_early/pallas_call | solution.py:17
  18.3 0.4 %collective-permute-done.9.there_second.there = bf16[32,4608]{1,0:T(8,128)(2,1)S(1)} collective-permute-done((bf16[32,4608]{1,0:T(8,128)(2,1)S(1)}, bf16[32,4608]{1,0:T(8,128)(2,1)S(1)}, u32[]{:S(2)}, u32[]{:S(2)}) %collective-permute-start.9) | collective-permute-done | bytes 294944 | tf_op jit(solution)/shard_map/ppermute | solution.py:180
  18.7 0.6 %back.1 = bf16[256,128]{1,0:T(8,128)(2,1)S(1)} custom-call(bf16[6,4,64,256]{3,2,1,0:T(8,128)(2,1)S(1)} %extend.1.lines, f32[256,64]{1,0:T(8,128)S(1)} %get-tuple-element.37.near, f32[256,64]{1,0:T(8,128)S(1)} %get-tuple-element.38.far, bf16[32,4608]{1,0:T(8,128)(2,1)S(1)} %collective-permute-done.5.here_second.here, ...), custom_call_target="tpu_custom_call" | custom-call | flops 226492416 | bytes 1572864 | tf_op jit(solution)/shard_map/back/pallas_call | solution.py:17
  19.3 1.3 %collective-permute-start.10 = (bf16[256,128]{1,0:T(8,128)(2,1)S(1)}, bf16[256,128]{1,0:T(8,128)(2,1)S(1)}, u32[]{:S(2)}, u32[]{:S(2)}) collective-permute-start(bf16[256,128]{1,0:T(8,128)(2,1)S(1)} %back.1), channel_id=1, source_target_pairs={{0,8},{1,9},{2,10},{3,11},{4,12},{5,13},{6,14},{7,15},{8,0},{9,1},... | collective-permute-start | bytes 196616 | tf_op jit(solution)/shard_map/ppermute | solution.py:180
  20.6 1.0 %kept.1.kept_sums = bf16[256,128]{1,0:T(8,128)(2,1)S(1)} custom-call(bf16[6,4,64,256]{3,2,1,0:T(8,128)(2,1)S(1)} %extend.1.lines, bf16[64,6912]{1,0:T(8,128)(2,1)S(1)} %bitcast.4, bf16[32,2304]{1,0:T(8,128)(2,1)S(1)} %collective-permute-done.2.here_first.here, bf16[32,2304]{1,0:T(8,128)(2,1)S(1)} %collective-permute-done.8.there_first.there, ...), custom_call_target="tpu_custom_call" | custom-call | flops 452984832 | bytes 2621440 | tf_op jit(solution)/shard_map/kept/pallas_call | solution.py:17
  21.6 2.0 %collective-permute-done.10.returned = bf16[256,128]{1,0:T(8,128)(2,1)S(1)} collective-permute-done((bf16[256,128]{1,0:T(8,128)(2,1)S(1)}, bf16[256,128]{1,0:T(8,128)(2,1)S(1)}, u32[]{:S(2)}, u32[]{:S(2)}) %collective-permute-start.10) | collective-permute-done | bytes 65568 | tf_op jit(solution)/shard_map/ppermute | solution.py:180
  23.7 0.8 %join.1 = bf16[256,256]{1,0:T(8,128)(2,1)} custom-call(bf16[256,128]{1,0:T(8,128)(2,1)S(1)} %kept.1.kept_sums, bf16[256,128]{1,0:T(8,128)(2,1)S(1)} %collective-permute-done.10.returned), custom_call_target="tpu_custom_call" | custom-call | bytes 262144 | tf_op jit(solution)/shard_map/join/pallas_call | solution.py:17
  (3 shorter events, 0.0 us)
Async XLA Ops:
  0.0 6.6 %collective-permute-start = (bf16[2,2,64,256]{3,2,1,0:T(8,128)(2,1)}, bf16[2,2,64,256]{3,2,1,0:T(8,128)(2,1)S(1)}, u32[]{:S(2)}, u32[]{:S(2)}) collective-permute-start(bf16[2,2,64,256]{3,2,1,0:T(8,128)(2,1)} %volume.1), channel_id=1, source_target_pairs={{0,8},{1,9},{2,10},{3,11},{4,12},{5,13},{6,14},{7,15},{8,0},{9,1},... | collective-permute-start | bytes 393224 | tf_op jit(solution)/shard_map/ppermute | solution.py:180
  4.0 6.2 %collective-permute-start.2 = (bf16[32,2304]{1,0:T(8,128)(2,1)S(1)}, bf16[32,2304]{1,0:T(8,128)(2,1)S(1)}, u32[]{:S(2)}, u32[]{:S(2)}) collective-permute-start(bf16[32,2304]{1,0:T(8,128)(2,1)S(1)} %get-tuple-element.25), channel_id=1, source_target_pairs={{0,16},{1,17},{2,18},{3,19},{4,20},{5,21},{6,22},{7,23},{8,24},{9,... | collective-permute-start | bytes 442376 | tf_op jit(solution)/shard_map/ppermute | solution.py:180
  6.7 5.1 %collective-permute-start.1 = (bf16[1,2,64,256]{3,2,1,0:T(8,128)(2,1)S(1)}, bf16[1,2,64,256]{3,2,1,0:T(8,128)(2,1)S(1)}, u32[]{:S(2)}, u32[]{:S(2)}) collective-permute-start(bf16[1,2,64,256]{3,2,1,0:T(8,128)(2,1)S(1)} %border.1), channel_id=1, source_target_pairs={{0,16},{1,17},{2,18},{3,19},{4,20},{5,21},{6,22},{7,23},{8,24},{9,... | collective-permute-start | bytes 196616 | tf_op jit(solution)/shard_map/ppermute | solution.py:180
  8.5 8.6 %collective-permute-start.5 = (bf16[32,4608]{1,0:T(8,128)(2,1)S(1)}, bf16[32,4608]{1,0:T(8,128)(2,1)S(1)}, u32[]{:S(2)}, u32[]{:S(2)}) collective-permute-start(bf16[32,4608]{1,0:T(8,128)(2,1)S(1)} %get-tuple-element.29), channel_id=1, source_target_pairs={{0,16},{1,17},{2,18},{3,19},{4,20},{5,21},{6,22},{7,23},{8,24},{9,... | collective-permute-start | bytes 884744 | tf_op jit(solution)/shard_map/ppermute | solution.py:180
  8.8 8.3 %collective-permute-start.3 = (bf16[4,1,64,256]{3,2,1,0:T(8,128)(2,1)S(1)}, bf16[4,1,64,256]{3,2,1,0:T(8,128)(2,1)S(1)}, u32[]{:S(2)}, u32[]{:S(2)}) collective-permute-start(bf16[4,1,64,256]{3,2,1,0:T(8,128)(2,1)S(1)} %get-tuple-element.27), channel_id=1, source_target_pairs={{0,1},{1,0},{2,3},{3,2},{4,5},{5,4},{6,7},{7,6},{8,9},{9,8},{10,11... | collective-permute-start | bytes 393224 | tf_op jit(solution)/shard_map/ppermute | solution.py:180
  8.8 8.3 %collective-permute-start.4 = (bf16[4,1,64,256]{3,2,1,0:T(8,128)(2,1)S(1)}, bf16[4,1,64,256]{3,2,1,0:T(8,128)(2,1)S(1)}, u32[]{:S(2)}, u32[]{:S(2)}) collective-permute-start(bf16[4,1,64,256]{3,2,1,0:T(8,128)(2,1)S(1)} %get-tuple-element.28), channel_id=1, source_target_pairs={{1,2},{2,1},{3,4},{4,3},{5,6},{6,5},{9,10},{10,9},{11,12},{12,11},... | collective-permute-start | bytes 393224 | tf_op jit(solution)/shard_map/ppermute | solution.py:180
  11.8 1.9 %collective-permute-start.6 = (bf16[1,1,64,256]{3,2,1,0:T(8,128)(2,1)S(1)}, bf16[1,1,64,256]{3,2,1,0:T(8,128)(2,1)S(1)}, u32[]{:S(2)}, u32[]{:S(2)}) collective-permute-start(bf16[1,1,64,256]{3,2,1,0:T(8,128)(2,1)S(1)} %get-tuple-element.31), channel_id=1, source_target_pairs={{0,1},{1,0},{2,3},{3,2},{4,5},{5,4},{6,7},{7,6},{8,9},{9,8},{10,11... | collective-permute-start | bytes 98312 | tf_op jit(solution)/shard_map/ppermute | solution.py:180
  12.8 4.8 %copy-start = (bf16[6912,64]{0,1:T(8,128)(2,1)S(1)}, bf16[6912,64]{0,1:T(8,128)(2,1)}, u32[]{:S(2)}) copy-start(bf16[6912,64]{0,1:T(8,128)(2,1)} %param.3) | copy-start | bytes 2654212
  12.8 4.3 %collective-permute-start.7 = (bf16[1,1,64,256]{3,2,1,0:T(8,128)(2,1)S(1)}, bf16[1,1,64,256]{3,2,1,0:T(8,128)(2,1)S(1)}, u32[]{:S(2)}, u32[]{:S(2)}) collective-permute-start(bf16[1,1,64,256]{3,2,1,0:T(8,128)(2,1)S(1)} %get-tuple-element.34), channel_id=1, source_target_pairs={{1,2},{2,1},{3,4},{4,3},{5,6},{6,5},{9,10},{10,9},{11,12},{12,11},... | collective-permute-start | bytes 98312 | tf_op jit(solution)/shard_map/ppermute | solution.py:180
  13.7 4.0 %collective-permute-start.8 = (bf16[32,2304]{1,0:T(8,128)(2,1)S(1)}, bf16[32,2304]{1,0:T(8,128)(2,1)S(1)}, u32[]{:S(2)}, u32[]{:S(2)}) collective-permute-start(bf16[32,2304]{1,0:T(8,128)(2,1)S(1)} %collective-permute-done.2.here_first.here), channel_id=1, source_target_pairs={{0,1},{1,0},{2,3},{3,2},{4,5},{5,4},{6,7},{7,6},{8,9},{9,8},{10,11... | collective-permute-start | bytes 442376 | tf_op jit(solution)/shard_map/ppermute | solution.py:180
  17.1 1.6 %collective-permute-start.9 = (bf16[32,4608]{1,0:T(8,128)(2,1)S(1)}, bf16[32,4608]{1,0:T(8,128)(2,1)S(1)}, u32[]{:S(2)}, u32[]{:S(2)}) collective-permute-start(bf16[32,4608]{1,0:T(8,128)(2,1)S(1)} %collective-permute-done.5.here_second.here), channel_id=1, source_target_pairs={{0,1},{1,0},{2,3},{3,2},{4,5},{5,4},{6,7},{7,6},{8,9},{9,8},{10,11... | collective-permute-start | bytes 884744 | tf_op jit(solution)/shard_map/ppermute | solution.py:180
  19.3 4.3 %collective-permute-start.10 = (bf16[256,128]{1,0:T(8,128)(2,1)S(1)}, bf16[256,128]{1,0:T(8,128)(2,1)S(1)}, u32[]{:S(2)}, u32[]{:S(2)}) collective-permute-start(bf16[256,128]{1,0:T(8,128)(2,1)S(1)} %back.1), channel_id=1, source_target_pairs={{0,8},{1,9},{2,10},{3,11},{4,12},{5,13},{6,14},{7,15},{8,0},{9,1},... | collective-permute-start | bytes 196616 | tf_op jit(solution)/shard_map/ppermute | solution.py:180

commit v7 on v5

--- a/solution.py
+++ b/solution.py
@@ -8,7 +8,7 @@
 BOTH = ("slab", "chan")
 VMEM_LIMIT = 24 * 1024 * 1024
 EARLY_TAPS = 9
-BORDER_COST, OUTER_EDGE_COST, EXTEND_COST = 10**9, 3 * 10**9, 3 * 10**9
+BORDER_COST, EDGES_COST, OUTER_EDGE_COST, EXTEND_COST = 10**9, 0, 3 * 10**9, 3 * 10**9
 
 
 def call(kernel, operands, outs, flops=0, places=None, scratch=()):
@@ -42,13 +42,22 @@
     return lax.div(lax.axis_index("slab"), 2)
 
 
-def fetch(volume, kernel_rows, first, second, block, sems):
-    count, early = first.shape
+def half_rows(kernel_rows, piece, start):
+    count = piece.shape[0]
     rows = pl.ds(pl.multiple_of(core_parity() * count, count), count)
+    return kernel_rows.at[rows, pl.ds(start, piece.shape[1])]
+
+
+def fetch(kernel_rows, first, sem):
+    copy = pltpu.make_async_copy(half_rows(kernel_rows, first, 0), first, sem)
+    copy.start()
+    copy.wait()
+
+
+def fetch_rest(volume, kernel_rows, first, second, block, sems):
     copies = [
-        pltpu.make_async_copy(kernel_rows.at[rows, pl.ds(0, early)], first, sems.at[0]),
-        pltpu.make_async_copy(kernel_rows.at[rows, pl.ds(early, second.shape[1])], second, sems.at[1]),
-        pltpu.make_async_copy(volume, block, sems.at[2]),
+        pltpu.make_async_copy(half_rows(kernel_rows, second, first.shape[1]), second, sems.at[0]),
+        pltpu.make_async_copy(volume, block, sems.at[1]),
     ]
     for copy in copies:
         copy.start()
@@ -192,20 +201,24 @@
     across = send(volume, across_x)
     early = EARLY_TAPS * channels
     pieces = [like((width // 2, early), weights), like((width // 2, depth_of_sum - early), weights)]
-    first, second, block = call(
-        fetch,
-        [pltpu.with_memory_space_constraint(x, pltpu.HBM) for x in (volume, kernel_rows)],
-        [*pieces, like(volume.shape, volume)],
-        places=[pl.BlockSpec(memory_space=pltpu.HBM)] * 2,
-        scratch=[pltpu.SemaphoreType.DMA((3,))],
-    )
+    hbm = pl.BlockSpec(memory_space=pltpu.HBM)
+    block_in_hbm, rows_in_hbm = [pltpu.with_memory_space_constraint(x, pltpu.HBM) for x in (volume, kernel_rows)]
+    (first,) = call(fetch, (rows_in_hbm,), pieces[:1], places=[hbm], scratch=[pltpu.SemaphoreType.DMA])
     here_first = send(first, across_y)
+    second, block = call(
+        fetch_rest,
+        (block_in_hbm, rows_in_hbm, first),
+        [pieces[1], like(volume.shape, volume)],
+        0,
+        places=[hbm, hbm, pl.BlockSpec(memory_space=pl.ANY)],
+        scratch=[pltpu.SemaphoreType.DMA((2,))],
+    )
     second, across = lax.optimization_barrier((second, across))
     (plane,) = call(border, (block, across), [like((1, rows, cols, channels), volume)], BORDER_COST)
     outer = send(plane, across_y)
     here_second = send(second, across_y)
     edge, line = like((2 * depth, 1, cols, channels), volume), like((1, 1, cols, channels), volume)
-    to_core, to_chip = call(edges, (block, across), [edge, edge])
+    to_core, to_chip = call(edges, (block, across), [edge, edge], EDGES_COST)
     from_core, from_chip = send(to_core, other_core), send(to_chip, next_chip)
     outer, here_first = lax.optimization_barrier((outer, here_first))
     outer_chip = send(outer, next_chip)

time: 24.6 us -> 24.7 us (level)
  waiting for transfers between devices: 7.24 us -> 6.18 us
  Pallas kernels: 4.22 us -> 5.05 us
  starting transfers between devices: 12.9 us -> 13.2 us
    ppermute x11, waiting for transfers between devices: 7.24 us -> 6.18 us  [send(): return lax.ppermute(array, BOTH, pairs)]
    pallas_call x9 -> x10, Pallas kernels: 4.22 us -> 5.05 us  [call(): pl.pallas_call(kernel, out_shape=outs, in_specs=places or [vmem] * len(op...]
  transfers between devices with their start and end apart: 11 -> 11, of which waited for: 8 -> 7; matrix products, arithmetic and copies ran while one was open for 0% -> 0% of each run, Pallas kernels for 12% -> 15%
where the time goes in v7:
time: 24.7 us; the launch traced here: 24.5 us
  starting transfers between devices  13.2 us (53%)
  waiting for transfers between devices  6.18 us (25%)
  Pallas kernels  5.05 us (20%)
    ppermute x11, starting transfers between devices, send(): return lax.ppermute(array, BOTH, pairs)  13.2 us
    ppermute x11, waiting for transfers between devices, send(): return lax.ppermute(array, BOTH, pairs)  6.18 us
    pallas_call x10, Pallas kernels, call(): pl.pallas_call(kernel, out_shape=outs, in_specs=places or [vmem] * len(op...  5.05 us
  transfers between devices with their start and end apart: 11, of which 7 were waited for; matrix products, arithmetic and copies ran while one was open for 0% of the time, Pallas kernels for 15%

profile of v7, /device:TPU:0, one launch (start us, length us, event | category | flops | bytes accessed | tf_op | source)
XLA Modules:
  0.0 24.5 jit_solution(15497373211368189610)
XLA Ops:
  0.0 2.9 %collective-permute-start = (bf16[2,2,64,256]{3,2,1,0:T(8,128)(2,1)}, bf16[2,2,64,256]{3,2,1,0:T(8,128)(2,1)S(1)}, u32[]{:S(2)}, u32[]{:S(2)}) collective-permute-start(bf16[2,2,64,256]{3,2,1,0:T(8,128)(2,1)} %volume.1), channel_id=1, source_target_pairs={{0,8},{1,9},{2,10},{3,11},{4,12},{5,13},{6,14},{7,15},{8,0},{9,1},... | collective-permute-start | bytes 393224 | tf_op jit(solution)/shard_map/ppermute | solution.py:187
  2.9 0.9 %fetch.1.first = bf16[32,2304]{1,0:T(8,128)(2,1)S(1)} custom-call(bf16[64,6912]{1,0:T(8,128)(2,1)} %bitcast.2), custom_call_target="tpu_custom_call" | custom-call | bytes 1032192 | tf_op jit(solution)/shard_map/fetch/pallas_call | solution.py:17
  3.9 1.6 %collective-permute-start.2 = (bf16[32,2304]{1,0:T(8,128)(2,1)S(1)}, bf16[32,2304]{1,0:T(8,128)(2,1)S(1)}, u32[]{:S(2)}, u32[]{:S(2)}) collective-permute-start(bf16[32,2304]{1,0:T(8,128)(2,1)S(1)} %fetch.1.first), channel_id=1, source_target_pairs={{0,16},{1,17},{2,18},{3,19},{4,20},{5,21},{6,22},{7,23},{8,24},{9,... | collective-permute-start | bytes 442376 | tf_op jit(solution)/shard_map/ppermute | solution.py:187
  5.5 1.0 %fetch_rest.1 = (bf16[32,4608]{1,0:T(8,128)(2,1)S(1)}, bf16[2,2,64,256]{3,2,1,0:T(8,128)(2,1)S(1)}) custom-call(bf16[2,2,64,256]{3,2,1,0:T(8,128)(2,1)} %volume.1, bf16[64,6912]{1,0:T(8,128)(2,1)} %bitcast.3, bf16[32,2304]{1,0:T(8,128)(2,1)S(1)} %fetch.1.first), custom_call_target="tpu_custom_call" | custom-call | bytes 1589248 | tf_op jit(solution)/shard_map/fetch_rest/pallas_call | solution.py:17
  6.5 0.2 collective-permute-done.across
  6.7 1.8 %collective-permute-start.1 = (bf16[1,2,64,256]{3,2,1,0:T(8,128)(2,1)S(1)}, bf16[1,2,64,256]{3,2,1,0:T(8,128)(2,1)S(1)}, u32[]{:S(2)}, u32[]{:S(2)}) collective-permute-start(bf16[1,2,64,256]{3,2,1,0:T(8,128)(2,1)S(1)} %border.1), channel_id=1, source_target_pairs={{0,16},{1,17},{2,18},{3,19},{4,20},{5,21},{6,22},{7,23},{8,24},{9,... | collective-permute-start | bytes 196616 | tf_op jit(solution)/shard_map/ppermute | solution.py:187
  8.5 0.3 %collective-permute-start.5 = (bf16[32,4608]{1,0:T(8,128)(2,1)S(1)}, bf16[32,4608]{1,0:T(8,128)(2,1)S(1)}, u32[]{:S(2)}, u32[]{:S(2)}) collective-permute-start(bf16[32,4608]{1,0:T(8,128)(2,1)S(1)} %get-tuple-element.25), channel_id=1, source_target_pairs={{0,16},{1,17},{2,18},{3,19},{4,20},{5,21},{6,22},{7,23},{8,24},{9,... | collective-permute-start | bytes 884744 | tf_op jit(solution)/shard_map/ppermute | solution.py:187
  8.8 0.0 collective-permute-start.3
  8.8 0.7 %collective-permute-start.4 = (bf16[4,1,64,256]{3,2,1,0:T(8,128)(2,1)S(1)}, bf16[4,1,64,256]{3,2,1,0:T(8,128)(2,1)S(1)}, u32[]{:S(2)}, u32[]{:S(2)}) collective-permute-start(bf16[4,1,64,256]{3,2,1,0:T(8,128)(2,1)S(1)} %get-tuple-element.24), channel_id=1, source_target_pairs={{1,2},{2,1},{3,4},{4,3},{5,6},{6,5},{9,10},{10,9},{11,12},{12,11},... | collective-permute-start | bytes 393224 | tf_op jit(solution)/shard_map/ppermute | solution.py:187
  9.5 0.4 %collective-permute-done.2.here_first.here = bf16[32,2304]{1,0:T(8,128)(2,1)S(1)} collective-permute-done((bf16[32,2304]{1,0:T(8,128)(2,1)S(1)}, bf16[32,2304]{1,0:T(8,128)(2,1)S(1)}, u32[]{:S(2)}, u32[]{:S(2)}) %collective-permute-start.2) | collective-permute-done | bytes 147488 | tf_op jit(solution)/shard_map/ppermute | solution.py:187
  9.9 1.9 %collective-permute-done.1.outer = bf16[1,2,64,256]{3,2,1,0:T(8,128)(2,1)S(1)} collective-permute-done((bf16[1,2,64,256]{3,2,1,0:T(8,128)(2,1)S(1)}, bf16[1,2,64,256]{3,2,1,0:T(8,128)(2,1)S(1)}, u32[]{:S(2)}, u32[]{:S(2)}) %collective-permute-start.1) | collective-permute-done | bytes 65568 | tf_op jit(solution)/shard_map/ppermute | solution.py:187
  11.8 0.7 %collective-permute-start.7 = (bf16[1,2,64,256]{3,2,1,0:T(8,128)(2,1)S(1)}, bf16[1,2,64,256]{3,2,1,0:T(8,128)(2,1)S(1)}, u32[]{:S(2)}, u32[]{:S(2)}) collective-permute-start(bf16[1,2,64,256]{3,2,1,0:T(8,128)(2,1)S(1)} %collective-permute-done.1.outer), channel_id=1, source_target_pairs={{1,2},{2,1},{3,4},{4,3},{5,6},{6,5},{9,10},{10,9},{11,12},{12,11},... | collective-permute-start | bytes 196616 | tf_op jit(solution)/shard_map/ppermute | solution.py:187
  12.4 0.0 copy-start
  12.4 3.3 %collective-permute-start.6 = (bf16[1,1,64,256]{3,2,1,0:T(8,128)(2,1)S(1)}, bf16[1,1,64,256]{3,2,1,0:T(8,128)(2,1)S(1)}, u32[]{:S(2)}, u32[]{:S(2)}) collective-permute-start(bf16[1,1,64,256]{3,2,1,0:T(8,128)(2,1)S(1)} %outer_edge.1), channel_id=1, source_target_pairs={{0,1},{1,0},{2,3},{3,2},{4,5},{5,4},{6,7},{7,6},{8,9},{9,8},{10,11... | collective-permute-start | bytes 98312 | tf_op jit(solution)/shard_map/ppermute | solution.py:187
  15.7 0.9 %collective-permute-done.6.outer_core = bf16[1,1,64,256]{3,2,1,0:T(8,128)(2,1)S(1)} collective-permute-done((bf16[1,1,64,256]{3,2,1,0:T(8,128)(2,1)S(1)}, bf16[1,1,64,256]{3,2,1,0:T(8,128)(2,1)S(1)}, u32[]{:S(2)}, u32[]{:S(2)}) %collective-permute-start.6) | collective-permute-done | bytes 32800 | tf_op jit(solution)/shard_map/ppermute | solution.py:187
  16.6 0.3 %collective-permute-start.8 = (bf16[32,2304]{1,0:T(8,128)(2,1)S(1)}, bf16[32,2304]{1,0:T(8,128)(2,1)S(1)}, u32[]{:S(2)}, u32[]{:S(2)}) collective-permute-start(bf16[32,2304]{1,0:T(8,128)(2,1)S(1)} %collective-permute-done.2.here_first.here), channel_id=1, source_target_pairs={{0,1},{1,0},{2,3},{3,2},{4,5},{5,4},{6,7},{7,6},{8,9},{9,8},{10,11... | collective-permute-start | bytes 442376 | tf_op jit(solution)/shard_map/ppermute | solution.py:187
  16.9 0.1 collective-permute-done.5.here_second.here
  17.0 0.1 collective-permute-start.9
  17.1 0.0 collective-permute-done.7.outer_chip
  17.1 0.0 collective-permute-done.3.from_core
  17.1 0.0 collective-permute-done.4.from_chip
  17.1 0.1 extend.1.lines
  17.2 0.8 %collective-permute-done.8.there_first.there = bf16[32,2304]{1,0:T(8,128)(2,1)S(1)} collective-permute-done((bf16[32,2304]{1,0:T(8,128)(2,1)S(1)}, bf16[32,2304]{1,0:T(8,128)(2,1)S(1)}, u32[]{:S(2)}, u32[]{:S(2)}) %collective-permute-start.8) | collective-permute-done | bytes 147488 | tf_op jit(solution)/shard_map/ppermute | solution.py:187
  17.9 0.0 copy-done
  17.9 0.7 %back_early.1 = (f32[256,64]{1,0:T(8,128)S(1)}, f32[256,64]{1,0:T(8,128)S(1)}) custom-call(bf16[6,4,64,256]{3,2,1,0:T(8,128)(2,1)S(1)} %extend.1.lines, bf16[64,6912]{1,0:T(8,128)(2,1)S(1)} %bitcast.4, bf16[32,2304]{1,0:T(8,128)(2,1)S(1)} %collective-permute-done.2.here_first.here, bf16[32,2304]{1,0:T(8,128)(2,1)S(1)} %collective-permute-done.8.there_first.there), custom_call_target="tpu_custom_call" | custom-call | flops 226492416 | bytes 2097152 | tf_op jit(solution)/shard_map/back_early/pallas_call | solution.py:17
  18.6 0.0 collective-permute-done.9.there_second.there
  18.6 0.6 %back.1 = bf16[256,128]{1,0:T(8,128)(2,1)S(1)} custom-call(bf16[6,4,64,256]{3,2,1,0:T(8,128)(2,1)S(1)} %extend.1.lines, f32[256,64]{1,0:T(8,128)S(1)} %get-tuple-element.31.near, f32[256,64]{1,0:T(8,128)S(1)} %get-tuple-element.32.far, bf16[32,4608]{1,0:T(8,128)(2,1)S(1)} %collective-permute-done.5.here_second.here, ...), custom_call_target="tpu_custom_call" | custom-call | flops 226492416 | bytes 1572864 | tf_op jit(solution)/shard_map/back/pallas_call | solution.py:17
  19.2 1.4 %collective-permute-start.10 = (bf16[256,128]{1,0:T(8,128)(2,1)S(1)}, bf16[256,128]{1,0:T(8,128)(2,1)S(1)}, u32[]{:S(2)}, u32[]{:S(2)}) collective-permute-start(bf16[256,128]{1,0:T(8,128)(2,1)S(1)} %back.1), channel_id=1, source_target_pairs={{0,8},{1,9},{2,10},{3,11},{4,12},{5,13},{6,14},{7,15},{8,0},{9,1},... | collective-permute-start | bytes 196616 | tf_op jit(solution)/shard_map/ppermute | solution.py:187
  20.7 1.0 %kept.1.kept_sums = bf16[256,128]{1,0:T(8,128)(2,1)S(1)} custom-call(bf16[6,4,64,256]{3,2,1,0:T(8,128)(2,1)S(1)} %extend.1.lines, bf16[64,6912]{1,0:T(8,128)(2,1)S(1)} %bitcast.5, bf16[32,2304]{1,0:T(8,128)(2,1)S(1)} %collective-permute-done.2.here_first.here, bf16[32,2304]{1,0:T(8,128)(2,1)S(1)} %collective-permute-done.8.there_first.there, ...), custom_call_target="tpu_custom_call" | custom-call | flops 452984832 | bytes 2621440 | tf_op jit(solution)/shard_map/kept/pallas_call | solution.py:17
  21.7 2.1 %collective-permute-done.10.returned = bf16[256,128]{1,0:T(8,128)(2,1)S(1)} collective-permute-done((bf16[256,128]{1,0:T(8,128)(2,1)S(1)}, bf16[256,128]{1,0:T(8,128)(2,1)S(1)}, u32[]{:S(2)}, u32[]{:S(2)}) %collective-permute-start.10) | collective-permute-done | bytes 65568 | tf_op jit(solution)/shard_map/ppermute | solution.py:187
  23.7 0.8 %join.1 = bf16[256,256]{1,0:T(8,128)(2,1)} custom-call(bf16[256,128]{1,0:T(8,128)(2,1)S(1)} %kept.1.kept_sums, bf16[256,128]{1,0:T(8,128)(2,1)S(1)} %collective-permute-done.10.returned), custom_call_target="tpu_custom_call" | custom-call | bytes 262144 | tf_op jit(solution)/shard_map/join/pallas_call | solution.py:17
  (3 shorter events, 0.0 us)
Async XLA Ops:
  0.0 6.6 %collective-permute-start = (bf16[2,2,64,256]{3,2,1,0:T(8,128)(2,1)}, bf16[2,2,64,256]{3,2,1,0:T(8,128)(2,1)S(1)}, u32[]{:S(2)}, u32[]{:S(2)}) collective-permute-start(bf16[2,2,64,256]{3,2,1,0:T(8,128)(2,1)} %volume.1), channel_id=1, source_target_pairs={{0,8},{1,9},{2,10},{3,11},{4,12},{5,13},{6,14},{7,15},{8,0},{9,1},... | collective-permute-start | bytes 393224 | tf_op jit(solution)/shard_map/ppermute | solution.py:187
  3.9 6.0 %collective-permute-start.2 = (bf16[32,2304]{1,0:T(8,128)(2,1)S(1)}, bf16[32,2304]{1,0:T(8,128)(2,1)S(1)}, u32[]{:S(2)}, u32[]{:S(2)}) collective-permute-start(bf16[32,2304]{1,0:T(8,128)(2,1)S(1)} %fetch.1.first), channel_id=1, source_target_pairs={{0,16},{1,17},{2,18},{3,19},{4,20},{5,21},{6,22},{7,23},{8,24},{9,... | collective-permute-start | bytes 442376 | tf_op jit(solution)/shard_map/ppermute | solution.py:187
  6.7 5.1 %collective-permute-start.1 = (bf16[1,2,64,256]{3,2,1,0:T(8,128)(2,1)S(1)}, bf16[1,2,64,256]{3,2,1,0:T(8,128)(2,1)S(1)}, u32[]{:S(2)}, u32[]{:S(2)}) collective-permute-start(bf16[1,2,64,256]{3,2,1,0:T(8,128)(2,1)S(1)} %border.1), channel_id=1, source_target_pairs={{0,16},{1,17},{2,18},{3,19},{4,20},{5,21},{6,22},{7,23},{8,24},{9,... | collective-permute-start | bytes 196616 | tf_op jit(solution)/shard_map/ppermute | solution.py:187
  8.5 8.4 %collective-permute-start.5 = (bf16[32,4608]{1,0:T(8,128)(2,1)S(1)}, bf16[32,4608]{1,0:T(8,128)(2,1)S(1)}, u32[]{:S(2)}, u32[]{:S(2)}) collective-permute-start(bf16[32,4608]{1,0:T(8,128)(2,1)S(1)} %get-tuple-element.25), channel_id=1, source_target_pairs={{0,16},{1,17},{2,18},{3,19},{4,20},{5,21},{6,22},{7,23},{8,24},{9,... | collective-permute-start | bytes 884744 | tf_op jit(solution)/shard_map/ppermute | solution.py:187
  8.8 8.2 %collective-permute-start.3 = (bf16[4,1,64,256]{3,2,1,0:T(8,128)(2,1)S(1)}, bf16[4,1,64,256]{3,2,1,0:T(8,128)(2,1)S(1)}, u32[]{:S(2)}, u32[]{:S(2)}) collective-permute-start(bf16[4,1,64,256]{3,2,1,0:T(8,128)(2,1)S(1)} %get-tuple-element.23), channel_id=1, source_target_pairs={{0,1},{1,0},{2,3},{3,2},{4,5},{5,4},{6,7},{7,6},{8,9},{9,8},{10,11... | collective-permute-start | bytes 393224 | tf_op jit(solution)/shard_map/ppermute | solution.py:187
  8.8 8.2 %collective-permute-start.4 = (bf16[4,1,64,256]{3,2,1,0:T(8,128)(2,1)S(1)}, bf16[4,1,64,256]{3,2,1,0:T(8,128)(2,1)S(1)}, u32[]{:S(2)}, u32[]{:S(2)}) collective-permute-start(bf16[4,1,64,256]{3,2,1,0:T(8,128)(2,1)S(1)} %get-tuple-element.24), channel_id=1, source_target_pairs={{1,2},{2,1},{3,4},{4,3},{5,6},{6,5},{9,10},{10,9},{11,12},{12,11},... | collective-permute-start | bytes 393224 | tf_op jit(solution)/shard_map/ppermute | solution.py:187
  11.8 5.3 %collective-permute-start.7 = (bf16[1,2,64,256]{3,2,1,0:T(8,128)(2,1)S(1)}, bf16[1,2,64,256]{3,2,1,0:T(8,128)(2,1)S(1)}, u32[]{:S(2)}, u32[]{:S(2)}) collective-permute-start(bf16[1,2,64,256]{3,2,1,0:T(8,128)(2,1)S(1)} %collective-permute-done.1.outer), channel_id=1, source_target_pairs={{1,2},{2,1},{3,4},{4,3},{5,6},{6,5},{9,10},{10,9},{11,12},{12,11},... | collective-permute-start | bytes 196616 | tf_op jit(solution)/shard_map/ppermute | solution.py:187
  12.4 5.5 %copy-start = (bf16[6912,64]{0,1:T(8,128)(2,1)S(1)}, bf16[6912,64]{0,1:T(8,128)(2,1)}, u32[]{:S(2)}) copy-start(bf16[6912,64]{0,1:T(8,128)(2,1)} %param.3) | copy-start | bytes 2654212
  12.4 4.1 %collective-permute-start.6 = (bf16[1,1,64,256]{3,2,1,0:T(8,128)(2,1)S(1)}, bf16[1,1,64,256]{3,2,1,0:T(8,128)(2,1)S(1)}, u32[]{:S(2)}, u32[]{:S(2)}) collective-permute-start(bf16[1,1,64,256]{3,2,1,0:T(8,128)(2,1)S(1)} %outer_edge.1), channel_id=1, source_target_pairs={{0,1},{1,0},{2,3},{3,2},{4,5},{5,4},{6,7},{7,6},{8,9},{9,8},{10,11... | collective-permute-start | bytes 98312 | tf_op jit(solution)/shard_map/ppermute | solution.py:187
  16.6 1.4 %collective-permute-start.8 = (bf16[32,2304]{1,0:T(8,128)(2,1)S(1)}, bf16[32,2304]{1,0:T(8,128)(2,1)S(1)}, u32[]{:S(2)}, u32[]{:S(2)}) collective-permute-start(bf16[32,2304]{1,0:T(8,128)(2,1)S(1)} %collective-permute-done.2.here_first.here), channel_id=1, source_target_pairs={{0,1},{1,0},{2,3},{3,2},{4,5},{5,4},{6,7},{7,6},{8,9},{9,8},{10,11... | collective-permute-start | bytes 442376 | tf_op jit(solution)/shard_map/ppermute | solution.py:187
  17.0 1.6 %collective-permute-start.9 = (bf16[32,4608]{1,0:T(8,128)(2,1)S(1)}, bf16[32,4608]{1,0:T(8,128)(2,1)S(1)}, u32[]{:S(2)}, u32[]{:S(2)}) collective-permute-start(bf16[32,4608]{1,0:T(8,128)(2,1)S(1)} %collective-permute-done.5.here_second.here), channel_id=1, source_target_pairs={{0,1},{1,0},{2,3},{3,2},{4,5},{5,4},{6,7},{7,6},{8,9},{9,8},{10,11... | collective-permute-start | bytes 884744 | tf_op jit(solution)/shard_map/ppermute | solution.py:187
  19.2 4.5 %collective-permute-start.10 = (bf16[256,128]{1,0:T(8,128)(2,1)S(1)}, bf16[256,128]{1,0:T(8,128)(2,1)S(1)}, u32[]{:S(2)}, u32[]{:S(2)}) collective-permute-start(bf16[256,128]{1,0:T(8,128)(2,1)S(1)} %back.1), channel_id=1, source_target_pairs={{0,8},{1,9},{2,10},{3,11},{4,12},{5,13},{6,14},{7,15},{8,0},{9,1},... | collective-permute-start | bytes 196616 | tf_op jit(solution)/shard_map/ppermute | solution.py:187

commit v8 on v7

--- a/solution.py
+++ b/solution.py
@@ -8,7 +8,7 @@
 BOTH = ("slab", "chan")
 VMEM_LIMIT = 24 * 1024 * 1024
 EARLY_TAPS = 9
-BORDER_COST, EDGES_COST, OUTER_EDGE_COST, EXTEND_COST = 10**9, 0, 3 * 10**9, 3 * 10**9
+BORDER_COST, EDGES_COST, OUTER_EDGES_COST, EXTEND_COST = 1 * 10**9, 5 * 10**9, 8 * 10**9, 3 * 10**9
 
 
 def call(kernel, operands, outs, flops=0, places=None, scratch=()):
@@ -80,8 +80,11 @@
             out[depth + d, 0] = across[d, row]
 
 
-def outer_edge(outer, to_core):
-    to_core[0, 0] = outer[0, (outer.shape[1] - 1) * (1 - core_parity())]
+def outer_edges(outer, to_core, to_chip):
+    rows = outer.shape[1]
+    core = core_parity()
+    for out, row in ((to_core, (rows - 1) * (1 - core)), (to_chip, (rows - 1) * core)):
+        out[0, 0] = outer[0, row]
 
 
 def extend(block, across, outer, from_core, from_chip, outer_core, outer_chip, lines):
@@ -96,8 +99,7 @@
         elif d < 2 * depth:
             target, source, core_row, chip_row = second + d - depth, across.at[d - depth], from_core[d, 0], from_chip[d, 0]
         else:
-            target, source = beyond, outer.at[0]
-            core_row, chip_row = outer_core[0, 0], outer_chip[0, (rows - 1) * (1 - core_parity())]
+            target, source, core_row, chip_row = beyond, outer.at[0], outer_core[0, 0], outer_chip[0, 0]
         lines[target, 0] = jnp.where(even_core, chip_row, core_row)
         for r in range(rows):
             lines[target, r + 1] = source[r]
@@ -217,13 +219,12 @@
     (plane,) = call(border, (block, across), [like((1, rows, cols, channels), volume)], BORDER_COST)
     outer = send(plane, across_y)
     here_second = send(second, across_y)
-    edge, line = like((2 * depth, 1, cols, channels), volume), like((1, 1, cols, channels), volume)
+    edge, outer_edge = like((2 * depth, 1, cols, channels), volume), like((1, 1, cols, channels), volume)
     to_core, to_chip = call(edges, (block, across), [edge, edge], EDGES_COST)
     from_core, from_chip = send(to_core, other_core), send(to_chip, next_chip)
     outer, here_first = lax.optimization_barrier((outer, here_first))
-    outer_chip = send(outer, next_chip)
-    (to_core,) = call(outer_edge, (outer,), [line], OUTER_EDGE_COST)
-    outer_core = send(to_core, other_core)
+    to_core, to_chip = call(outer_edges, (outer,), [outer_edge, outer_edge], OUTER_EDGES_COST)
+    outer_core, outer_chip = send(to_core, other_core), send(to_chip, next_chip)
     here_first, outer_core = lax.optimization_barrier((here_first, outer_core))
     there_first = send(here_first, other_core)
     here_second, outer_core = lax.optimization_barrier((here_second, outer_core))

time: 24.7 us -> 24.6 us (level)
  waiting for transfers between devices: 6.18 us -> 5.7 us
  starting transfers between devices: 13.2 us -> 13.6 us
    ppermute x11, waiting for transfers between devices: 6.18 us -> 5.7 us  [send(): return lax.ppermute(array, BOTH, pairs)]
    ppermute x11, starting transfers between devices: 13.2 us -> 13.6 us  [send(): return lax.ppermute(array, BOTH, pairs)]
  transfers between devices with their start and end apart: 11 -> 11, of which waited for: 7 -> 8; matrix products, arithmetic and copies ran while one was open for 0% -> 0% of each run, Pallas kernels for 15% -> 15%
where the time goes in v8:
time: 24.6 us; the launch traced here: 24.4 us
  starting transfers between devices  13.6 us (55%)
  waiting for transfers between devices  5.7 us (23%)
  Pallas kernels  5.04 us (20%)
    ppermute x11, starting transfers between devices, send(): return lax.ppermute(array, BOTH, pairs)  13.6 us
    ppermute x11, waiting for transfers between devices, send(): return lax.ppermute(array, BOTH, pairs)  5.7 us
    pallas_call x10, Pallas kernels, call(): pl.pallas_call(kernel, out_shape=outs, in_specs=places or [vmem] * len(op...  5.04 us
  transfers between devices with their start and end apart: 11, of which 8 were waited for; matrix products, arithmetic and copies ran while one was open for 0% of the time, Pallas kernels for 15%

profile of v8, /device:TPU:0, one launch (start us, length us, event | category | flops | bytes accessed | tf_op | source)
XLA Modules:
  0.0 24.4 jit_solution(13398830623649530123)
XLA Ops:
  0.0 2.9 %collective-permute-start = (bf16[2,2,64,256]{3,2,1,0:T(8,128)(2,1)}, bf16[2,2,64,256]{3,2,1,0:T(8,128)(2,1)S(1)}, u32[]{:S(2)}, u32[]{:S(2)}) collective-permute-start(bf16[2,2,64,256]{3,2,1,0:T(8,128)(2,1)} %volume.1), channel_id=1, source_target_pairs={{0,8},{1,9},{2,10},{3,11},{4,12},{5,13},{6,14},{7,15},{8,0},{9,1},... | collective-permute-start | bytes 393224 | tf_op jit(solution)/shard_map/ppermute | solution.py:189
  2.9 0.9 %fetch.1.first = bf16[32,2304]{1,0:T(8,128)(2,1)S(1)} custom-call(bf16[64,6912]{1,0:T(8,128)(2,1)} %bitcast.2), custom_call_target="tpu_custom_call" | custom-call | bytes 1032192 | tf_op jit(solution)/shard_map/fetch/pallas_call | solution.py:17
  3.9 1.6 %collective-permute-start.2 = (bf16[32,2304]{1,0:T(8,128)(2,1)S(1)}, bf16[32,2304]{1,0:T(8,128)(2,1)S(1)}, u32[]{:S(2)}, u32[]{:S(2)}) collective-permute-start(bf16[32,2304]{1,0:T(8,128)(2,1)S(1)} %fetch.1.first), channel_id=1, source_target_pairs={{0,16},{1,17},{2,18},{3,19},{4,20},{5,21},{6,22},{7,23},{8,24},{9,... | collective-permute-start | bytes 442376 | tf_op jit(solution)/shard_map/ppermute | solution.py:189
  5.5 1.0 %fetch_rest.1 = (bf16[32,4608]{1,0:T(8,128)(2,1)S(1)}, bf16[2,2,64,256]{3,2,1,0:T(8,128)(2,1)S(1)}) custom-call(bf16[2,2,64,256]{3,2,1,0:T(8,128)(2,1)} %volume.1, bf16[64,6912]{1,0:T(8,128)(2,1)} %bitcast.3, bf16[32,2304]{1,0:T(8,128)(2,1)S(1)} %fetch.1.first), custom_call_target="tpu_custom_call" | custom-call | bytes 1589248 | tf_op jit(solution)/shard_map/fetch_rest/pallas_call | solution.py:17
  6.5 0.2 collective-permute-done.across
  6.7 1.8 %collective-permute-start.1 = (bf16[1,2,64,256]{3,2,1,0:T(8,128)(2,1)S(1)}, bf16[1,2,64,256]{3,2,1,0:T(8,128)(2,1)S(1)}, u32[]{:S(2)}, u32[]{:S(2)}) collective-permute-start(bf16[1,2,64,256]{3,2,1,0:T(8,128)(2,1)S(1)} %border.1), channel_id=1, source_target_pairs={{0,16},{1,17},{2,18},{3,19},{4,20},{5,21},{6,22},{7,23},{8,24},{9,... | collective-permute-start | bytes 196616 | tf_op jit(solution)/shard_map/ppermute | solution.py:189
  8.5 0.3 %collective-permute-start.5 = (bf16[32,4608]{1,0:T(8,128)(2,1)S(1)}, bf16[32,4608]{1,0:T(8,128)(2,1)S(1)}, u32[]{:S(2)}, u32[]{:S(2)}) collective-permute-start(bf16[32,4608]{1,0:T(8,128)(2,1)S(1)} %get-tuple-element.27), channel_id=1, source_target_pairs={{0,16},{1,17},{2,18},{3,19},{4,20},{5,21},{6,22},{7,23},{8,24},{9,... | collective-permute-start | bytes 884744 | tf_op jit(solution)/shard_map/ppermute | solution.py:189
  8.8 0.0 collective-permute-start.3
  8.8 0.7 %collective-permute-start.4 = (bf16[4,1,64,256]{3,2,1,0:T(8,128)(2,1)S(1)}, bf16[4,1,64,256]{3,2,1,0:T(8,128)(2,1)S(1)}, u32[]{:S(2)}, u32[]{:S(2)}) collective-permute-start(bf16[4,1,64,256]{3,2,1,0:T(8,128)(2,1)S(1)} %get-tuple-element.26), channel_id=1, source_target_pairs={{1,2},{2,1},{3,4},{4,3},{5,6},{6,5},{9,10},{10,9},{11,12},{12,11},... | collective-permute-start | bytes 393224 | tf_op jit(solution)/shard_map/ppermute | solution.py:189
  9.5 0.4 %collective-permute-done.2.here_first.here = bf16[32,2304]{1,0:T(8,128)(2,1)S(1)} collective-permute-done((bf16[32,2304]{1,0:T(8,128)(2,1)S(1)}, bf16[32,2304]{1,0:T(8,128)(2,1)S(1)}, u32[]{:S(2)}, u32[]{:S(2)}) %collective-permute-start.2) | collective-permute-done | bytes 147488 | tf_op jit(solution)/shard_map/ppermute | solution.py:189
  9.9 1.9 %collective-permute-done.1.outer = bf16[1,2,64,256]{3,2,1,0:T(8,128)(2,1)S(1)} collective-permute-done((bf16[1,2,64,256]{3,2,1,0:T(8,128)(2,1)S(1)}, bf16[1,2,64,256]{3,2,1,0:T(8,128)(2,1)S(1)}, u32[]{:S(2)}, u32[]{:S(2)}) %collective-permute-start.1) | collective-permute-done | bytes 65568 | tf_op jit(solution)/shard_map/ppermute | solution.py:189
  11.8 1.0 %collective-permute-start.6 = (bf16[1,1,64,256]{3,2,1,0:T(8,128)(2,1)S(1)}, bf16[1,1,64,256]{3,2,1,0:T(8,128)(2,1)S(1)}, u32[]{:S(2)}, u32[]{:S(2)}) collective-permute-start(bf16[1,1,64,256]{3,2,1,0:T(8,128)(2,1)S(1)} %get-tuple-element.29), channel_id=1, source_target_pairs={{0,1},{1,0},{2,3},{3,2},{4,5},{5,4},{6,7},{7,6},{8,9},{9,8},{10,11... | collective-permute-start | bytes 98312 | tf_op jit(solution)/shard_map/ppermute | solution.py:189
  12.8 0.0 copy-start
  12.8 0.8 %collective-permute-start.7 = (bf16[1,1,64,256]{3,2,1,0:T(8,128)(2,1)S(1)}, bf16[1,1,64,256]{3,2,1,0:T(8,128)(2,1)S(1)}, u32[]{:S(2)}, u32[]{:S(2)}) collective-permute-start(bf16[1,1,64,256]{3,2,1,0:T(8,128)(2,1)S(1)} %get-tuple-element.32), channel_id=1, source_target_pairs={{1,2},{2,1},{3,4},{4,3},{5,6},{6,5},{9,10},{10,9},{11,12},{12,11},... | collective-permute-start | bytes 98312 | tf_op jit(solution)/shard_map/ppermute | solution.py:189
  13.6 0.1 collective-permute-done.6.outer_core
  13.7 2.9 %collective-permute-start.8 = (bf16[32,2304]{1,0:T(8,128)(2,1)S(1)}, bf16[32,2304]{1,0:T(8,128)(2,1)S(1)}, u32[]{:S(2)}, u32[]{:S(2)}) collective-permute-start(bf16[32,2304]{1,0:T(8,128)(2,1)S(1)} %collective-permute-done.2.here_first.here), channel_id=1, source_target_pairs={{0,1},{1,0},{2,3},{3,2},{4,5},{5,4},{6,7},{7,6},{8,9},{9,8},{10,11... | collective-permute-start | bytes 442376 | tf_op jit(solution)/shard_map/ppermute | solution.py:189
  16.6 0.4 %collective-permute-done.5.here_second.here = bf16[32,4608]{1,0:T(8,128)(2,1)S(1)} collective-permute-done((bf16[32,4608]{1,0:T(8,128)(2,1)S(1)}, bf16[32,4608]{1,0:T(8,128)(2,1)S(1)}, u32[]{:S(2)}, u32[]{:S(2)}) %collective-permute-start.5) | collective-permute-done | bytes 294944 | tf_op jit(solution)/shard_map/ppermute | solution.py:189
  17.0 0.0 collective-permute-start.9
  17.0 0.0 collective-permute-done.7.outer_chip
  17.0 0.0 collective-permute-done.3.from_core
  17.0 0.0 collective-permute-done.4.from_chip
  17.0 0.1 extend.1.lines
  17.1 0.5 %collective-permute-done.8.there_first.there = bf16[32,2304]{1,0:T(8,128)(2,1)S(1)} collective-permute-done((bf16[32,2304]{1,0:T(8,128)(2,1)S(1)}, bf16[32,2304]{1,0:T(8,128)(2,1)S(1)}, u32[]{:S(2)}, u32[]{:S(2)}) %collective-permute-start.8) | collective-permute-done | bytes 147488 | tf_op jit(solution)/shard_map/ppermute | solution.py:189
  17.6 0.0 copy-done
  17.6 0.7 %back_early.1 = (f32[256,64]{1,0:T(8,128)S(1)}, f32[256,64]{1,0:T(8,128)S(1)}) custom-call(bf16[6,4,64,256]{3,2,1,0:T(8,128)(2,1)S(1)} %extend.1.lines, bf16[64,6912]{1,0:T(8,128)(2,1)S(1)} %bitcast.4, bf16[32,2304]{1,0:T(8,128)(2,1)S(1)} %collective-permute-done.2.here_first.here, bf16[32,2304]{1,0:T(8,128)(2,1)S(1)} %collective-permute-done.8.there_first.there), custom_call_target="tpu_custom_call" | custom-call | flops 226492416 | bytes 2097152 | tf_op jit(solution)/shard_map/back_early/pallas_call | solution.py:17
  18.3 0.3 %collective-permute-done.9.there_second.there = bf16[32,4608]{1,0:T(8,128)(2,1)S(1)} collective-permute-done((bf16[32,4608]{1,0:T(8,128)(2,1)S(1)}, bf16[32,4608]{1,0:T(8,128)(2,1)S(1)}, u32[]{:S(2)}, u32[]{:S(2)}) %collective-permute-start.9) | collective-permute-done | bytes 294944 | tf_op jit(solution)/shard_map/ppermute | solution.py:189
  18.5 0.6 %back.1 = bf16[256,128]{1,0:T(8,128)(2,1)S(1)} custom-call(bf16[6,4,64,256]{3,2,1,0:T(8,128)(2,1)S(1)} %extend.1.lines, f32[256,64]{1,0:T(8,128)S(1)} %get-tuple-element.35.near, f32[256,64]{1,0:T(8,128)S(1)} %get-tuple-element.36.far, bf16[32,4608]{1,0:T(8,128)(2,1)S(1)} %collective-permute-done.5.here_second.here, ...), custom_call_target="tpu_custom_call" | custom-call | flops 226492416 | bytes 1572864 | tf_op jit(solution)/shard_map/back/pallas_call | solution.py:17
  19.1 1.5 %collective-permute-start.10 = (bf16[256,128]{1,0:T(8,128)(2,1)S(1)}, bf16[256,128]{1,0:T(8,128)(2,1)S(1)}, u32[]{:S(2)}, u32[]{:S(2)}) collective-permute-start(bf16[256,128]{1,0:T(8,128)(2,1)S(1)} %back.1), channel_id=1, source_target_pairs={{0,8},{1,9},{2,10},{3,11},{4,12},{5,13},{6,14},{7,15},{8,0},{9,1},... | collective-permute-start | bytes 196616 | tf_op jit(solution)/shard_map/ppermute | solution.py:189
  20.6 1.0 %kept.1.kept_sums = bf16[256,128]{1,0:T(8,128)(2,1)S(1)} custom-call(bf16[6,4,64,256]{3,2,1,0:T(8,128)(2,1)S(1)} %extend.1.lines, bf16[64,6912]{1,0:T(8,128)(2,1)S(1)} %bitcast.5, bf16[32,2304]{1,0:T(8,128)(2,1)S(1)} %collective-permute-done.2.here_first.here, bf16[32,2304]{1,0:T(8,128)(2,1)S(1)} %collective-permute-done.8.there_first.there, ...), custom_call_target="tpu_custom_call" | custom-call | flops 452984832 | bytes 2621440 | tf_op jit(solution)/shard_map/kept/pallas_call | solution.py:17
  21.6 2.0 %collective-permute-done.10.returned = bf16[256,128]{1,0:T(8,128)(2,1)S(1)} collective-permute-done((bf16[256,128]{1,0:T(8,128)(2,1)S(1)}, bf16[256,128]{1,0:T(8,128)(2,1)S(1)}, u32[]{:S(2)}, u32[]{:S(2)}) %collective-permute-start.10) | collective-permute-done | bytes 65568 | tf_op jit(solution)/shard_map/ppermute | solution.py:189
  23.7 0.8 %join.1 = bf16[256,256]{1,0:T(8,128)(2,1)} custom-call(bf16[256,128]{1,0:T(8,128)(2,1)S(1)} %kept.1.kept_sums, bf16[256,128]{1,0:T(8,128)(2,1)S(1)} %collective-permute-done.10.returned), custom_call_target="tpu_custom_call" | custom-call | bytes 262144 | tf_op jit(solution)/shard_map/join/pallas_call | solution.py:17
  (3 shorter events, 0.0 us)
Async XLA Ops:
  0.0 6.6 %collective-permute-start = (bf16[2,2,64,256]{3,2,1,0:T(8,128)(2,1)}, bf16[2,2,64,256]{3,2,1,0:T(8,128)(2,1)S(1)}, u32[]{:S(2)}, u32[]{:S(2)}) collective-permute-start(bf16[2,2,64,256]{3,2,1,0:T(8,128)(2,1)} %volume.1), channel_id=1, source_target_pairs={{0,8},{1,9},{2,10},{3,11},{4,12},{5,13},{6,14},{7,15},{8,0},{9,1},... | collective-permute-start | bytes 393224 | tf_op jit(solution)/shard_map/ppermute | solution.py:189
  3.9 6.0 %collective-permute-start.2 = (bf16[32,2304]{1,0:T(8,128)(2,1)S(1)}, bf16[32,2304]{1,0:T(8,128)(2,1)S(1)}, u32[]{:S(2)}, u32[]{:S(2)}) collective-permute-start(bf16[32,2304]{1,0:T(8,128)(2,1)S(1)} %fetch.1.first), channel_id=1, source_target_pairs={{0,16},{1,17},{2,18},{3,19},{4,20},{5,21},{6,22},{7,23},{8,24},{9,... | collective-permute-start | bytes 442376 | tf_op jit(solution)/shard_map/ppermute | solution.py:189
  6.7 5.1 %collective-permute-start.1 = (bf16[1,2,64,256]{3,2,1,0:T(8,128)(2,1)S(1)}, bf16[1,2,64,256]{3,2,1,0:T(8,128)(2,1)S(1)}, u32[]{:S(2)}, u32[]{:S(2)}) collective-permute-start(bf16[1,2,64,256]{3,2,1,0:T(8,128)(2,1)S(1)} %border.1), channel_id=1, source_target_pairs={{0,16},{1,17},{2,18},{3,19},{4,20},{5,21},{6,22},{7,23},{8,24},{9,... | collective-permute-start | bytes 196616 | tf_op jit(solution)/shard_map/ppermute | solution.py:189
  8.5 8.4 %collective-permute-start.5 = (bf16[32,4608]{1,0:T(8,128)(2,1)S(1)}, bf16[32,4608]{1,0:T(8,128)(2,1)S(1)}, u32[]{:S(2)}, u32[]{:S(2)}) collective-permute-start(bf16[32,4608]{1,0:T(8,128)(2,1)S(1)} %get-tuple-element.27), channel_id=1, source_target_pairs={{0,16},{1,17},{2,18},{3,19},{4,20},{5,21},{6,22},{7,23},{8,24},{9,... | collective-permute-start | bytes 884744 | tf_op jit(solution)/shard_map/ppermute | solution.py:189
  8.8 8.1 %collective-permute-start.3 = (bf16[4,1,64,256]{3,2,1,0:T(8,128)(2,1)S(1)}, bf16[4,1,64,256]{3,2,1,0:T(8,128)(2,1)S(1)}, u32[]{:S(2)}, u32[]{:S(2)}) collective-permute-start(bf16[4,1,64,256]{3,2,1,0:T(8,128)(2,1)S(1)} %get-tuple-element.25), channel_id=1, source_target_pairs={{0,1},{1,0},{2,3},{3,2},{4,5},{5,4},{6,7},{7,6},{8,9},{9,8},{10,11... | collective-permute-start | bytes 393224 | tf_op jit(solution)/shard_map/ppermute | solution.py:189
  8.8 8.1 %collective-permute-start.4 = (bf16[4,1,64,256]{3,2,1,0:T(8,128)(2,1)S(1)}, bf16[4,1,64,256]{3,2,1,0:T(8,128)(2,1)S(1)}, u32[]{:S(2)}, u32[]{:S(2)}) collective-permute-start(bf16[4,1,64,256]{3,2,1,0:T(8,128)(2,1)S(1)} %get-tuple-element.26), channel_id=1, source_target_pairs={{1,2},{2,1},{3,4},{4,3},{5,6},{6,5},{9,10},{10,9},{11,12},{12,11},... | collective-permute-start | bytes 393224 | tf_op jit(solution)/shard_map/ppermute | solution.py:189
  11.8 1.9 %collective-permute-start.6 = (bf16[1,1,64,256]{3,2,1,0:T(8,128)(2,1)S(1)}, bf16[1,1,64,256]{3,2,1,0:T(8,128)(2,1)S(1)}, u32[]{:S(2)}, u32[]{:S(2)}) collective-permute-start(bf16[1,1,64,256]{3,2,1,0:T(8,128)(2,1)S(1)} %get-tuple-element.29), channel_id=1, source_target_pairs={{0,1},{1,0},{2,3},{3,2},{4,5},{5,4},{6,7},{7,6},{8,9},{9,8},{10,11... | collective-permute-start | bytes 98312 | tf_op jit(solution)/shard_map/ppermute | solution.py:189
  12.8 4.8 %copy-start = (bf16[6912,64]{0,1:T(8,128)(2,1)S(1)}, bf16[6912,64]{0,1:T(8,128)(2,1)}, u32[]{:S(2)}) copy-start(bf16[6912,64]{0,1:T(8,128)(2,1)} %param.3) | copy-start | bytes 2654212
  12.8 4.2 %collective-permute-start.7 = (bf16[1,1,64,256]{3,2,1,0:T(8,128)(2,1)S(1)}, bf16[1,1,64,256]{3,2,1,0:T(8,128)(2,1)S(1)}, u32[]{:S(2)}, u32[]{:S(2)}) collective-permute-start(bf16[1,1,64,256]{3,2,1,0:T(8,128)(2,1)S(1)} %get-tuple-element.32), channel_id=1, source_target_pairs={{1,2},{2,1},{3,4},{4,3},{5,6},{6,5},{9,10},{10,9},{11,12},{12,11},... | collective-permute-start | bytes 98312 | tf_op jit(solution)/shard_map/ppermute | solution.py:189
  13.7 4.0 %collective-permute-start.8 = (bf16[32,2304]{1,0:T(8,128)(2,1)S(1)}, bf16[32,2304]{1,0:T(8,128)(2,1)S(1)}, u32[]{:S(2)}, u32[]{:S(2)}) collective-permute-start(bf16[32,2304]{1,0:T(8,128)(2,1)S(1)} %collective-permute-done.2.here_first.here), channel_id=1, source_target_pairs={{0,1},{1,0},{2,3},{3,2},{4,5},{5,4},{6,7},{7,6},{8,9},{9,8},{10,11... | collective-permute-start | bytes 442376 | tf_op jit(solution)/shard_map/ppermute | solution.py:189
  17.0 1.6 %collective-permute-start.9 = (bf16[32,4608]{1,0:T(8,128)(2,1)S(1)}, bf16[32,4608]{1,0:T(8,128)(2,1)S(1)}, u32[]{:S(2)}, u32[]{:S(2)}) collective-permute-start(bf16[32,4608]{1,0:T(8,128)(2,1)S(1)} %collective-permute-done.5.here_second.here), channel_id=1, source_target_pairs={{0,1},{1,0},{2,3},{3,2},{4,5},{5,4},{6,7},{7,6},{8,9},{9,8},{10,11... | collective-permute-start | bytes 884744 | tf_op jit(solution)/shard_map/ppermute | solution.py:189
  19.1 4.5 %collective-permute-start.10 = (bf16[256,128]{1,0:T(8,128)(2,1)S(1)}, bf16[256,128]{1,0:T(8,128)(2,1)S(1)}, u32[]{:S(2)}, u32[]{:S(2)}) collective-permute-start(bf16[256,128]{1,0:T(8,128)(2,1)S(1)} %back.1), channel_id=1, source_target_pairs={{0,8},{1,9},{2,10},{3,11},{4,12},{5,13},{6,14},{7,15},{8,0},{9,1},... | collective-permute-start | bytes 196616 | tf_op jit(solution)/shard_map/ppermute | solution.py:189

commit v9 on v8

--- a/solution.py
+++ b/solution.py
@@ -11,14 +11,14 @@
 BORDER_COST, EDGES_COST, OUTER_EDGES_COST, EXTEND_COST = 1 * 10**9, 5 * 10**9, 8 * 10**9, 3 * 10**9
 
 
-def call(kernel, operands, outs, flops=0, places=None, scratch=()):
+def call(kernel, operands, outs, flops=0, places=None, out_place=None, scratch=()):
     size = sum(x.size * x.dtype.itemsize for x in (*operands, *outs))
     vmem = pl.BlockSpec(memory_space=pltpu.VMEM)
     return pl.pallas_call(
         kernel,
         out_shape=outs,
         in_specs=places or [vmem] * len(operands),
-        out_specs=[vmem] * len(outs),
+        out_specs=[out_place or vmem] * len(outs),
         scratch_shapes=scratch,
         compiler_params=pltpu.CompilerParams(vmem_limit_bytes=VMEM_LIMIT),
         cost_estimate=pl.CostEstimate(flops=flops, bytes_accessed=size, transcendentals=0),
@@ -165,15 +165,20 @@
     out[...] = arranged(near, convolve(lines, base, depth, groups)).astype(out.dtype)
 
 
-def join(kept_sums, returned, out):
+def join(kept_sums, returned, out, tiles, sems):
     voxels, width = kept_sums.shape
     mine, theirs = kept_sums[...].astype(jnp.float32), returned[...].astype(jnp.float32)
     here = lax.div(lax.broadcasted_iota(jnp.int32, (voxels, width), 1), width // 2) == slab_x()
-    near, far = jnp.where(here, mine, theirs), jnp.where(here, theirs, mine)
     near_at = pl.multiple_of(slab_y() * width, width)
     far_at = pl.multiple_of((1 - slab_y()) * width, width)
-    out[:, pl.ds(near_at, width)] = near.astype(out.dtype)
-    out[:, pl.ds(far_at, width)] = pltpu.roll(far, width // 2, 1).astype(out.dtype)
+    near_copy = pltpu.make_async_copy(tiles.at[0], out.at[:, pl.ds(near_at, width)], sems.at[0])
+    far_copy = pltpu.make_async_copy(tiles.at[1], out.at[:, pl.ds(far_at, width)], sems.at[1])
+    tiles[0] = jnp.where(here, mine, theirs).astype(out.dtype)
+    near_copy.start()
+    tiles[1] = pltpu.roll(jnp.where(here, theirs, mine), width // 2, 1).astype(out.dtype)
+    far_copy.start()
+    near_copy.wait()
+    far_copy.wait()
 
 
 def four_slabs(volume, weights):
@@ -243,7 +248,13 @@
     (mine,) = call(
         kept, (lines, kernel_rows, here_first, there_first, here_second, there_second), [both], 2 * work
     )
-    (out,) = call(join, (mine, returned), [like((voxels, 4 * width), volume)])
+    (out,) = call(
+        join,
+        (mine, returned),
+        [like((voxels, 4 * width), volume)],
+        out_place=pl.BlockSpec(memory_space=pltpu.HBM),
+        scratch=[pltpu.VMEM((2, voxels, 2 * width), volume.dtype), pltpu.SemaphoreType.DMA((2,))],
+    )
     return out.reshape(volume.shape)
 
 

time: 24.6 us -> 24.6 us (level)
  no operation moved by 1% of the time
where the time goes in v9:
time: 24.6 us; the launch traced here: 24.4 us
  starting transfers between devices  13.6 us (55%)
  waiting for transfers between devices  5.7 us (23%)
  Pallas kernels  5.03 us (20%)
    ppermute x11, starting transfers between devices, send(): return lax.ppermute(array, BOTH, pairs)  13.6 us
    ppermute x11, waiting for transfers between devices, send(): return lax.ppermute(array, BOTH, pairs)  5.7 us
    pallas_call x10, Pallas kernels, call(): pl.pallas_call(kernel, out_shape=outs, in_specs=places or [vmem] * len(op...  5.03 us
  transfers between devices with their start and end apart: 11, of which 8 were waited for; matrix products, arithmetic and copies ran while one was open for 0% of the time, Pallas kernels for 15%

profile of v9, /device:TPU:0, one launch (start us, length us, event | category | flops | bytes accessed | tf_op | source)
XLA Modules:
  0.0 24.4 jit_solution(12540710124940380736)
XLA Ops:
  0.0 2.9 %collective-permute-start = (bf16[2,2,64,256]{3,2,1,0:T(8,128)(2,1)}, bf16[2,2,64,256]{3,2,1,0:T(8,128)(2,1)S(1)}, u32[]{:S(2)}, u32[]{:S(2)}) collective-permute-start(bf16[2,2,64,256]{3,2,1,0:T(8,128)(2,1)} %volume.1), channel_id=1, source_target_pairs={{0,8},{1,9},{2,10},{3,11},{4,12},{5,13},{6,14},{7,15},{8,0},{9,1},... | collective-permute-start | bytes 393224 | tf_op jit(solution)/shard_map/ppermute | solution.py:194
  2.9 0.9 %fetch.1.first = bf16[32,2304]{1,0:T(8,128)(2,1)S(1)} custom-call(bf16[64,6912]{1,0:T(8,128)(2,1)} %bitcast.2), custom_call_target="tpu_custom_call" | custom-call | bytes 1032192 | tf_op jit(solution)/shard_map/fetch/pallas_call | solution.py:17
  3.9 1.6 %collective-permute-start.2 = (bf16[32,2304]{1,0:T(8,128)(2,1)S(1)}, bf16[32,2304]{1,0:T(8,128)(2,1)S(1)}, u32[]{:S(2)}, u32[]{:S(2)}) collective-permute-start(bf16[32,2304]{1,0:T(8,128)(2,1)S(1)} %fetch.1.first), channel_id=1, source_target_pairs={{0,16},{1,17},{2,18},{3,19},{4,20},{5,21},{6,22},{7,23},{8,24},{9,... | collective-permute-start | bytes 442376 | tf_op jit(solution)/shard_map/ppermute | solution.py:194
  5.5 1.0 %fetch_rest.1 = (bf16[32,4608]{1,0:T(8,128)(2,1)S(1)}, bf16[2,2,64,256]{3,2,1,0:T(8,128)(2,1)S(1)}) custom-call(bf16[2,2,64,256]{3,2,1,0:T(8,128)(2,1)} %volume.1, bf16[64,6912]{1,0:T(8,128)(2,1)} %bitcast.3, bf16[32,2304]{1,0:T(8,128)(2,1)S(1)} %fetch.1.first), custom_call_target="tpu_custom_call" | custom-call | bytes 1589248 | tf_op jit(solution)/shard_map/fetch_rest/pallas_call | solution.py:17
  6.5 0.2 collective-permute-done.across
  6.7 1.8 %collective-permute-start.1 = (bf16[1,2,64,256]{3,2,1,0:T(8,128)(2,1)S(1)}, bf16[1,2,64,256]{3,2,1,0:T(8,128)(2,1)S(1)}, u32[]{:S(2)}, u32[]{:S(2)}) collective-permute-start(bf16[1,2,64,256]{3,2,1,0:T(8,128)(2,1)S(1)} %border.1), channel_id=1, source_target_pairs={{0,16},{1,17},{2,18},{3,19},{4,20},{5,21},{6,22},{7,23},{8,24},{9,... | collective-permute-start | bytes 196616 | tf_op jit(solution)/shard_map/ppermute | solution.py:194
  8.5 0.3 %collective-permute-start.5 = (bf16[32,4608]{1,0:T(8,128)(2,1)S(1)}, bf16[32,4608]{1,0:T(8,128)(2,1)S(1)}, u32[]{:S(2)}, u32[]{:S(2)}) collective-permute-start(bf16[32,4608]{1,0:T(8,128)(2,1)S(1)} %get-tuple-element.27), channel_id=1, source_target_pairs={{0,16},{1,17},{2,18},{3,19},{4,20},{5,21},{6,22},{7,23},{8,24},{9,... | collective-permute-start | bytes 884744 | tf_op jit(solution)/shard_map/ppermute | solution.py:194
  8.8 0.0 collective-permute-start.3
  8.8 0.7 %collective-permute-start.4 = (bf16[4,1,64,256]{3,2,1,0:T(8,128)(2,1)S(1)}, bf16[4,1,64,256]{3,2,1,0:T(8,128)(2,1)S(1)}, u32[]{:S(2)}, u32[]{:S(2)}) collective-permute-start(bf16[4,1,64,256]{3,2,1,0:T(8,128)(2,1)S(1)} %get-tuple-element.26), channel_id=1, source_target_pairs={{1,2},{2,1},{3,4},{4,3},{5,6},{6,5},{9,10},{10,9},{11,12},{12,11},... | collective-permute-start | bytes 393224 | tf_op jit(solution)/shard_map/ppermute | solution.py:194
  9.5 0.4 %collective-permute-done.2.here_first.here = bf16[32,2304]{1,0:T(8,128)(2,1)S(1)} collective-permute-done((bf16[32,2304]{1,0:T(8,128)(2,1)S(1)}, bf16[32,2304]{1,0:T(8,128)(2,1)S(1)}, u32[]{:S(2)}, u32[]{:S(2)}) %collective-permute-start.2) | collective-permute-done | bytes 147488 | tf_op jit(solution)/shard_map/ppermute | solution.py:194
  9.9 1.9 %collective-permute-done.1.outer = bf16[1,2,64,256]{3,2,1,0:T(8,128)(2,1)S(1)} collective-permute-done((bf16[1,2,64,256]{3,2,1,0:T(8,128)(2,1)S(1)}, bf16[1,2,64,256]{3,2,1,0:T(8,128)(2,1)S(1)}, u32[]{:S(2)}, u32[]{:S(2)}) %collective-permute-start.1) | collective-permute-done | bytes 65568 | tf_op jit(solution)/shard_map/ppermute | solution.py:194
  11.8 1.0 %collective-permute-start.6 = (bf16[1,1,64,256]{3,2,1,0:T(8,128)(2,1)S(1)}, bf16[1,1,64,256]{3,2,1,0:T(8,128)(2,1)S(1)}, u32[]{:S(2)}, u32[]{:S(2)}) collective-permute-start(bf16[1,1,64,256]{3,2,1,0:T(8,128)(2,1)S(1)} %get-tuple-element.29), channel_id=1, source_target_pairs={{0,1},{1,0},{2,3},{3,2},{4,5},{5,4},{6,7},{7,6},{8,9},{9,8},{10,11... | collective-permute-start | bytes 98312 | tf_op jit(solution)/shard_map/ppermute | solution.py:194
  12.8 0.0 copy-start
  12.8 0.8 %collective-permute-start.7 = (bf16[1,1,64,256]{3,2,1,0:T(8,128)(2,1)S(1)}, bf16[1,1,64,256]{3,2,1,0:T(8,128)(2,1)S(1)}, u32[]{:S(2)}, u32[]{:S(2)}) collective-permute-start(bf16[1,1,64,256]{3,2,1,0:T(8,128)(2,1)S(1)} %get-tuple-element.32), channel_id=1, source_target_pairs={{1,2},{2,1},{3,4},{4,3},{5,6},{6,5},{9,10},{10,9},{11,12},{12,11},... | collective-permute-start | bytes 98312 | tf_op jit(solution)/shard_map/ppermute | solution.py:194
  13.6 0.1 collective-permute-done.6.outer_core
  13.7 2.9 %collective-permute-start.8 = (bf16[32,2304]{1,0:T(8,128)(2,1)S(1)}, bf16[32,2304]{1,0:T(8,128)(2,1)S(1)}, u32[]{:S(2)}, u32[]{:S(2)}) collective-permute-start(bf16[32,2304]{1,0:T(8,128)(2,1)S(1)} %collective-permute-done.2.here_first.here), channel_id=1, source_target_pairs={{0,1},{1,0},{2,3},{3,2},{4,5},{5,4},{6,7},{7,6},{8,9},{9,8},{10,11... | collective-permute-start | bytes 442376 | tf_op jit(solution)/shard_map/ppermute | solution.py:194
  16.6 0.4 %collective-permute-done.5.here_second.here = bf16[32,4608]{1,0:T(8,128)(2,1)S(1)} collective-permute-done((bf16[32,4608]{1,0:T(8,128)(2,1)S(1)}, bf16[32,4608]{1,0:T(8,128)(2,1)S(1)}, u32[]{:S(2)}, u32[]{:S(2)}) %collective-permute-start.5) | collective-permute-done | bytes 294944 | tf_op jit(solution)/shard_map/ppermute | solution.py:194
  17.0 0.0 collective-permute-start.9
  17.0 0.0 collective-permute-done.7.outer_chip
  17.0 0.0 collective-permute-done.3.from_core
  17.0 0.0 collective-permute-done.4.from_chip
  17.0 0.1 extend.1.lines
  17.1 0.5 %collective-permute-done.8.there_first.there = bf16[32,2304]{1,0:T(8,128)(2,1)S(1)} collective-permute-done((bf16[32,2304]{1,0:T(8,128)(2,1)S(1)}, bf16[32,2304]{1,0:T(8,128)(2,1)S(1)}, u32[]{:S(2)}, u32[]{:S(2)}) %collective-permute-start.8) | collective-permute-done | bytes 147488 | tf_op jit(solution)/shard_map/ppermute | solution.py:194
  17.6 0.0 copy-done
  17.6 0.7 %back_early.1 = (f32[256,64]{1,0:T(8,128)S(1)}, f32[256,64]{1,0:T(8,128)S(1)}) custom-call(bf16[6,4,64,256]{3,2,1,0:T(8,128)(2,1)S(1)} %extend.1.lines, bf16[64,6912]{1,0:T(8,128)(2,1)S(1)} %bitcast.4, bf16[32,2304]{1,0:T(8,128)(2,1)S(1)} %collective-permute-done.2.here_first.here, bf16[32,2304]{1,0:T(8,128)(2,1)S(1)} %collective-permute-done.8.there_first.there), custom_call_target="tpu_custom_call" | custom-call | flops 226492416 | bytes 2097152 | tf_op jit(solution)/shard_map/back_early/pallas_call | solution.py:17
  18.3 0.3 %collective-permute-done.9.there_second.there = bf16[32,4608]{1,0:T(8,128)(2,1)S(1)} collective-permute-done((bf16[32,4608]{1,0:T(8,128)(2,1)S(1)}, bf16[32,4608]{1,0:T(8,128)(2,1)S(1)}, u32[]{:S(2)}, u32[]{:S(2)}) %collective-permute-start.9) | collective-permute-done | bytes 294944 | tf_op jit(solution)/shard_map/ppermute | solution.py:194
  18.5 0.6 %back.1 = bf16[256,128]{1,0:T(8,128)(2,1)S(1)} custom-call(bf16[6,4,64,256]{3,2,1,0:T(8,128)(2,1)S(1)} %extend.1.lines, f32[256,64]{1,0:T(8,128)S(1)} %get-tuple-element.35.near, f32[256,64]{1,0:T(8,128)S(1)} %get-tuple-element.36.far, bf16[32,4608]{1,0:T(8,128)(2,1)S(1)} %collective-permute-done.5.here_second.here, ...), custom_call_target="tpu_custom_call" | custom-call | flops 226492416 | bytes 1572864 | tf_op jit(solution)/shard_map/back/pallas_call | solution.py:17
  19.1 1.5 %collective-permute-start.10 = (bf16[256,128]{1,0:T(8,128)(2,1)S(1)}, bf16[256,128]{1,0:T(8,128)(2,1)S(1)}, u32[]{:S(2)}, u32[]{:S(2)}) collective-permute-start(bf16[256,128]{1,0:T(8,128)(2,1)S(1)} %back.1), channel_id=1, source_target_pairs={{0,8},{1,9},{2,10},{3,11},{4,12},{5,13},{6,14},{7,15},{8,0},{9,1},... | collective-permute-start | bytes 196616 | tf_op jit(solution)/shard_map/ppermute | solution.py:194
  20.6 1.0 %kept.1.kept_sums = bf16[256,128]{1,0:T(8,128)(2,1)S(1)} custom-call(bf16[6,4,64,256]{3,2,1,0:T(8,128)(2,1)S(1)} %extend.1.lines, bf16[64,6912]{1,0:T(8,128)(2,1)S(1)} %bitcast.5, bf16[32,2304]{1,0:T(8,128)(2,1)S(1)} %collective-permute-done.2.here_first.here, bf16[32,2304]{1,0:T(8,128)(2,1)S(1)} %collective-permute-done.8.there_first.there, ...), custom_call_target="tpu_custom_call" | custom-call | flops 452984832 | bytes 2621440 | tf_op jit(solution)/shard_map/kept/pallas_call | solution.py:17
  21.6 2.0 %collective-permute-done.10.returned = bf16[256,128]{1,0:T(8,128)(2,1)S(1)} collective-permute-done((bf16[256,128]{1,0:T(8,128)(2,1)S(1)}, bf16[256,128]{1,0:T(8,128)(2,1)S(1)}, u32[]{:S(2)}, u32[]{:S(2)}) %collective-permute-start.10) | collective-permute-done | bytes 65568 | tf_op jit(solution)/shard_map/ppermute | solution.py:194
  23.7 0.7 %join.1 = bf16[256,256]{1,0:T(8,128)(2,1)} custom-call(bf16[256,128]{1,0:T(8,128)(2,1)S(1)} %kept.1.kept_sums, bf16[256,128]{1,0:T(8,128)(2,1)S(1)} %collective-permute-done.10.returned), custom_call_target="tpu_custom_call" | custom-call | bytes 262144 | tf_op jit(solution)/shard_map/join/pallas_call | solution.py:17
  (3 shorter events, 0.0 us)
Async XLA Ops:
  0.0 6.6 %collective-permute-start = (bf16[2,2,64,256]{3,2,1,0:T(8,128)(2,1)}, bf16[2,2,64,256]{3,2,1,0:T(8,128)(2,1)S(1)}, u32[]{:S(2)}, u32[]{:S(2)}) collective-permute-start(bf16[2,2,64,256]{3,2,1,0:T(8,128)(2,1)} %volume.1), channel_id=1, source_target_pairs={{0,8},{1,9},{2,10},{3,11},{4,12},{5,13},{6,14},{7,15},{8,0},{9,1},... | collective-permute-start | bytes 393224 | tf_op jit(solution)/shard_map/ppermute | solution.py:194
  3.9 6.0 %collective-permute-start.2 = (bf16[32,2304]{1,0:T(8,128)(2,1)S(1)}, bf16[32,2304]{1,0:T(8,128)(2,1)S(1)}, u32[]{:S(2)}, u32[]{:S(2)}) collective-permute-start(bf16[32,2304]{1,0:T(8,128)(2,1)S(1)} %fetch.1.first), channel_id=1, source_target_pairs={{0,16},{1,17},{2,18},{3,19},{4,20},{5,21},{6,22},{7,23},{8,24},{9,... | collective-permute-start | bytes 442376 | tf_op jit(solution)/shard_map/ppermute | solution.py:194
  6.7 5.1 %collective-permute-start.1 = (bf16[1,2,64,256]{3,2,1,0:T(8,128)(2,1)S(1)}, bf16[1,2,64,256]{3,2,1,0:T(8,128)(2,1)S(1)}, u32[]{:S(2)}, u32[]{:S(2)}) collective-permute-start(bf16[1,2,64,256]{3,2,1,0:T(8,128)(2,1)S(1)} %border.1), channel_id=1, source_target_pairs={{0,16},{1,17},{2,18},{3,19},{4,20},{5,21},{6,22},{7,23},{8,24},{9,... | collective-permute-start | bytes 196616 | tf_op jit(solution)/shard_map/ppermute | solution.py:194
  8.5 8.4 %collective-permute-start.5 = (bf16[32,4608]{1,0:T(8,128)(2,1)S(1)}, bf16[32,4608]{1,0:T(8,128)(2,1)S(1)}, u32[]{:S(2)}, u32[]{:S(2)}) collective-permute-start(bf16[32,4608]{1,0:T(8,128)(2,1)S(1)} %get-tuple-element.27), channel_id=1, source_target_pairs={{0,16},{1,17},{2,18},{3,19},{4,20},{5,21},{6,22},{7,23},{8,24},{9,... | collective-permute-start | bytes 884744 | tf_op jit(solution)/shard_map/ppermute | solution.py:194
  8.8 8.1 %collective-permute-start.3 = (bf16[4,1,64,256]{3,2,1,0:T(8,128)(2,1)S(1)}, bf16[4,1,64,256]{3,2,1,0:T(8,128)(2,1)S(1)}, u32[]{:S(2)}, u32[]{:S(2)}) collective-permute-start(bf16[4,1,64,256]{3,2,1,0:T(8,128)(2,1)S(1)} %get-tuple-element.25), channel_id=1, source_target_pairs={{0,1},{1,0},{2,3},{3,2},{4,5},{5,4},{6,7},{7,6},{8,9},{9,8},{10,11... | collective-permute-start | bytes 393224 | tf_op jit(solution)/shard_map/ppermute | solution.py:194
  8.8 8.1 %collective-permute-start.4 = (bf16[4,1,64,256]{3,2,1,0:T(8,128)(2,1)S(1)}, bf16[4,1,64,256]{3,2,1,0:T(8,128)(2,1)S(1)}, u32[]{:S(2)}, u32[]{:S(2)}) collective-permute-start(bf16[4,1,64,256]{3,2,1,0:T(8,128)(2,1)S(1)} %get-tuple-element.26), channel_id=1, source_target_pairs={{1,2},{2,1},{3,4},{4,3},{5,6},{6,5},{9,10},{10,9},{11,12},{12,11},... | collective-permute-start | bytes 393224 | tf_op jit(solution)/shard_map/ppermute | solution.py:194
  11.8 1.9 %collective-permute-start.6 = (bf16[1,1,64,256]{3,2,1,0:T(8,128)(2,1)S(1)}, bf16[1,1,64,256]{3,2,1,0:T(8,128)(2,1)S(1)}, u32[]{:S(2)}, u32[]{:S(2)}) collective-permute-start(bf16[1,1,64,256]{3,2,1,0:T(8,128)(2,1)S(1)} %get-tuple-element.29), channel_id=1, source_target_pairs={{0,1},{1,0},{2,3},{3,2},{4,5},{5,4},{6,7},{7,6},{8,9},{9,8},{10,11... | collective-permute-start | bytes 98312 | tf_op jit(solution)/shard_map/ppermute | solution.py:194
  12.8 4.8 %copy-start = (bf16[6912,64]{0,1:T(8,128)(2,1)S(1)}, bf16[6912,64]{0,1:T(8,128)(2,1)}, u32[]{:S(2)}) copy-start(bf16[6912,64]{0,1:T(8,128)(2,1)} %param.3) | copy-start | bytes 2654212
  12.8 4.2 %collective-permute-start.7 = (bf16[1,1,64,256]{3,2,1,0:T(8,128)(2,1)S(1)}, bf16[1,1,64,256]{3,2,1,0:T(8,128)(2,1)S(1)}, u32[]{:S(2)}, u32[]{:S(2)}) collective-permute-start(bf16[1,1,64,256]{3,2,1,0:T(8,128)(2,1)S(1)} %get-tuple-element.32), channel_id=1, source_target_pairs={{1,2},{2,1},{3,4},{4,3},{5,6},{6,5},{9,10},{10,9},{11,12},{12,11},... | collective-permute-start | bytes 98312 | tf_op jit(solution)/shard_map/ppermute | solution.py:194
  13.7 4.0 %collective-permute-start.8 = (bf16[32,2304]{1,0:T(8,128)(2,1)S(1)}, bf16[32,2304]{1,0:T(8,128)(2,1)S(1)}, u32[]{:S(2)}, u32[]{:S(2)}) collective-permute-start(bf16[32,2304]{1,0:T(8,128)(2,1)S(1)} %collective-permute-done.2.here_first.here), channel_id=1, source_target_pairs={{0,1},{1,0},{2,3},{3,2},{4,5},{5,4},{6,7},{7,6},{8,9},{9,8},{10,11... | collective-permute-start | bytes 442376 | tf_op jit(solution)/shard_map/ppermute | solution.py:194
  17.0 1.6 %collective-permute-start.9 = (bf16[32,4608]{1,0:T(8,128)(2,1)S(1)}, bf16[32,4608]{1,0:T(8,128)(2,1)S(1)}, u32[]{:S(2)}, u32[]{:S(2)}) collective-permute-start(bf16[32,4608]{1,0:T(8,128)(2,1)S(1)} %collective-permute-done.5.here_second.here), channel_id=1, source_target_pairs={{0,1},{1,0},{2,3},{3,2},{4,5},{5,4},{6,7},{7,6},{8,9},{9,8},{10,11... | collective-permute-start | bytes 884744 | tf_op jit(solution)/shard_map/ppermute | solution.py:194
  19.1 4.5 %collective-permute-start.10 = (bf16[256,128]{1,0:T(8,128)(2,1)S(1)}, bf16[256,128]{1,0:T(8,128)(2,1)S(1)}, u32[]{:S(2)}, u32[]{:S(2)}) collective-permute-start(bf16[256,128]{1,0:T(8,128)(2,1)S(1)} %back.1), channel_id=1, source_target_pairs={{0,8},{1,9},{2,10},{3,11},{4,12},{5,13},{6,14},{7,15},{8,0},{9,1},... | collective-permute-start | bytes 196616 | tf_op jit(solution)/shard_map/ppermute | solution.py:194
